TPU v7x, 128 devices: a whole 4x4x4 slice. The times are simulated.
128 devices in a mesh: row: 8 (over y, core), col: 16 (over z, x).
Axes of the slice: x: 4, y: 4, z: 4, core: 2. Of those that a mesh axis runs over, the one named last changes fastest.
Arguments:
- patches: float32 [64, 128, 2, 128, 128], P('row', 'col'), may hold values from -6 to 6
- right_offset: int32 [64, 128], P('row', 'col'), may hold values from 57 to 112, as said below
- right_width: int32 [64, 128], P('row', 'col'), may hold values from 16 to 64
- down_offset: int32 [64, 128], P('row', 'col'), may hold values from 57 to 112, as said below
- down_width: int32 [64, 128], P('row', 'col'), may hold values from 16 to 64
Outputs:
- blended: float32 [64, 128, 2, 128, 128], P('row', 'col')
- phases: float32 [2, 64, 128], P(None, 'row', 'col')
Inputs may be any that keep to these rules, and one draw needn't show every extreme that they name: right_offset + right_width lies above 120 and at most 128. down_offset + down_width lies above 120 and at most 128.
All inputs are finite; a program needn't handle non-finite values.
Results may differ from a plain program's by a relative error of at most 0.0003.
Values sent between devices are 32-bit elements; how exact they have to be, the bound alone decides.
No kernel may reach another device: no remote copies, remote signals or barrier semaphores. Data moves between devices by JAX's collectives and lax.ppermute only.
A program may use at most 128 MiB of HBM per device.

v0:
```python
import jax
import jax.numpy as jnp
from jax import lax
from jax.sharding import PartitionSpec as P

ITERS = 2


eps_norm = 1.0
highest = lax.Precision.HIGHEST


def extended(array, sides, width):
    for axis, dim in sides:
        size, length = (lax.axis_size(axis), array.shape[dim])
        up = [(i, (i + 1) % size) for i in range(size - 1)]
        down = [(j, i) for i, j in up]
        last = lax.slice_in_dim(array, length - width, length, axis=dim)
        first = lax.slice_in_dim(array, 0, width, axis=dim)
        before = lax.ppermute(last, axis, up)
        after = lax.ppermute(first, axis, down)
        array = jnp.concatenate([before, array, after], axis=dim)
    return array


def shifted_2(array, axis, by):
    size = lax.axis_size(axis)
    pairs = [(i, i + by) for i in range(size) if 0 <= i + by < size]
    return lax.ppermute(array, axis, pairs)


def correlate(shifted, partner, width_table):
    real_part = jnp.sum(
        shifted[..., 0, :, :] * partner[..., 0, :, :]
        + shifted[..., 1, :, :] * partner[..., 1, :, :],
        axis=(-2, -1),
    )
    imag_part = jnp.sum(
        shifted[..., 0, :, :] * partner[..., 1, :, :]
        - shifted[..., 1, :, :] * partner[..., 0, :, :],
        axis=(-2, -1),
    )
    scale = 1.0 / jnp.sqrt(partner.shape[-1] * width_table.astype(jnp.float32))
    return jnp.stack([real_part * scale, imag_part * scale])


def complex_times(factor, field):
    return jnp.stack(
        [factor[0] * field[0] - factor[1] * field[1], factor[0] * field[1] + factor[1] * field[0]]
    )


def conj_times(factor, field):
    return jnp.stack(
        [factor[0] * field[0] + factor[1] * field[1], factor[0] * field[1] - factor[1] * field[0]]
    )


def rotate(factor, field):
    real_part = (
        factor[..., 0:1, :, :] * field[..., 0:1, :, :]
        - factor[..., 1:2, :, :] * field[..., 1:2, :, :]
    )
    imag_part = (
        factor[..., 0:1, :, :] * field[..., 1:2, :, :]
        + factor[..., 1:2, :, :] * field[..., 0:1, :, :]
    )
    return jnp.concatenate([real_part, imag_part], axis=-3)


def neighbours(phase_now):
    padded = extended(phase_now, (("row", 1), ("col", 2)), 1)
    return (padded[:, 1:-1, 2:], padded[:, 2:, 1:-1], padded[:, 1:-1, :-2], padded[:, :-2, 1:-1])


def apply_sync(phase_now, corr_east, corr_south, corr_west, corr_north):
    east_phase, south_phase, west_phase, north_phase = neighbours(phase_now)
    image = complex_times(corr_east, east_phase) + complex_times(corr_south, south_phase)
    return image + conj_times(corr_west, west_phase) + conj_times(corr_north, north_phase)


def scale_each(interior, count):
    total = lax.psum(jnp.sum(interior * interior), ("row", "col"))
    return 1.0 / jnp.sqrt(total / count + eps_norm)


def local(patches, right_offset, right_width, down_offset, down_width):
    rows_here = patches.shape[0]
    cols_here = patches.shape[1]
    patch_side = patches.shape[3]
    lane_index = jnp.arange(patch_side, dtype=jnp.int32)
    east_edge = shifted_2(patches[:, 0:1], "col", -1)
    south_edge = shifted_2(patches[0:1], "row", -1)
    east_patch = jnp.concatenate([patches[:, 1:], east_edge], axis=1)
    south_patch = jnp.concatenate([patches[1:], south_edge], axis=0)
    east_select = (
        (lane_index[:, None] == lane_index[None, :] + right_offset[:, :, None, None])
        & (lane_index[None, :] < right_width[:, :, None, None])
    ).astype(jnp.float32)
    south_select = (
        (lane_index[:, None] == lane_index[None, :] + down_offset[:, :, None, None])
        & (lane_index[None, :] < down_width[:, :, None, None])
    ).astype(jnp.float32)
    east_shifted = jnp.einsum("pqkrc,pqcd->pqkrd", patches, east_select, precision=highest)
    south_shifted = jnp.einsum("pqab,pqkac->pqkbc", south_select, patches, precision=highest)
    corr_east = correlate(east_shifted, east_patch, right_width)
    corr_south = correlate(south_shifted, south_patch, down_width)
    count = rows_here * cols_here * lax.axis_size("row") * lax.axis_size("col")
    west_rim = shifted_2(corr_east[:, :, cols_here - 1 : cols_here], "col", 1)
    north_rim = shifted_2(corr_south[:, rows_here - 1 : rows_here, :], "row", 1)
    corr_west = jnp.concatenate([west_rim, corr_east[:, :, :-1]], axis=2)
    corr_north = jnp.concatenate([north_rim, corr_south[:, :-1, :]], axis=1)
    phase_now = jnp.stack(
        [
            jnp.ones((rows_here, cols_here), jnp.float32),
            jnp.zeros((rows_here, cols_here), jnp.float32),
        ]
    )
    for step in range(ITERS):
        phase_now = apply_sync(phase_now, corr_east, corr_south, corr_west, corr_north)
        phase_now = phase_now * scale_each(phase_now, count)
    beside_all = neighbours(phase_now)
    east_phase = beside_all[0]
    south_phase = beside_all[1]
    east_place = jnp.einsum("pqkrd,pqcd->pqkrc", east_patch, east_select, precision=highest)
    south_place = jnp.einsum("pqab,pqkbc->pqkac", south_select, south_patch, precision=highest)
    own_factor = jnp.transpose(phase_now, (1, 2, 0))[:, :, :, None, None]
    east_factor = jnp.transpose(east_phase, (1, 2, 0))[:, :, :, None, None]
    south_factor = jnp.transpose(south_phase, (1, 2, 0))[:, :, :, None, None]
    numer = (
        rotate(own_factor, patches)
        + rotate(east_factor, east_place)
        + rotate(south_factor, south_place)
    )
    col_index = lax.axis_index("col") * cols_here + jnp.arange(cols_here, dtype=jnp.int32)
    row_index = lax.axis_index("row") * rows_here + jnp.arange(rows_here, dtype=jnp.int32)
    east_live = (col_index < cols_here * lax.axis_size("col") - 1)[None, :, None]
    south_live = (row_index < rows_here * lax.axis_size("row") - 1)[:, None, None]
    east_mask = (
        (lane_index >= right_offset[:, :, None])
        & (lane_index < right_offset[:, :, None] + right_width[:, :, None])
        & east_live
    ).astype(jnp.float32)
    south_mask = (
        (lane_index >= down_offset[:, :, None])
        & (lane_index < down_offset[:, :, None] + down_width[:, :, None])
        & south_live
    ).astype(jnp.float32)
    weight = 1.0 + east_mask[:, :, None, None, :] + south_mask[:, :, None, :, None]
    return (numer / weight, phase_now)


def solution(mesh):
    return jax.shard_map(
        local,
        mesh=mesh,
        in_specs=(
            P("row", "col", None, None, None),
            P("row", "col"),
            P("row", "col"),
            P("row", "col"),
            P("row", "col"),
        ),
        out_specs=(P("row", "col", None, None, None), P(None, "row", "col")),
        check_vma=False,
    )
```

profile of v0, /device:TPU:1, one launch (start us, length us, event | category | flops | bytes accessed | tf_op | source)
XLA Modules:
  0.0 289.2 jit_solution(13561521103684578000)
XLA Ops:
  0.7 3.5 %collective-permute-start.2 = (f32[2,1,8]{2,1,0:T(1,128)}, f32[2,1,8]{2,1,0:T(1,128)}, u32[]{:S(2)}, u32[]{:S(2)}) collective-permute-start(f32[2,1,8]{2,1,0:T(1,128)} %constant.5.clone.1), channel_id=1, source_target_pairs={{16,0},{32,16},{48,32},{64,48},{80,64},{96,80},{112,96},{17,1},{33... | collective-permute-start | bytes 200 | tf_op jit(solution)/shard_map/ppermute | solution.py:21
  4.1 3.2 %collective-permute-start.1 = (f32[2,1,8]{2,1,0:T(1,128)}, f32[2,1,8]{2,1,0:T(1,128)}, u32[]{:S(2)}, u32[]{:S(2)}) collective-permute-start(f32[2,1,8]{2,1,0:T(1,128)} %constant.5.clone.1), channel_id=1, source_target_pairs={{0,16},{16,32},{32,48},{48,64},{64,80},{80,96},{96,112},{1,17},{17... | collective-permute-start | bytes 200 | tf_op jit(solution)/shard_map/ppermute | solution.py:20
  7.3 2.3 slice.270
  9.6 1.9 collective-permute-start.4
  11.9 1.3 collective-permute-start
  15.1 12.5 %fusion.17 = f32[8,8,2,128,128]{4,3,2,1,0:T(8,128)} fusion(f32[8,8,2,128,128]{4,3,2,1,0:T(8,128)} %param.5, s32[8,8,128]{2,1,0:T(8,128)S(1)} %iota_add_fusion, pred[8,8,128]{2,1,0:T(8,128)(4,1)S(1)} %iota_compare_fusion.6), kind=kOutput, calls=%fused_computation.37 | convolution fusion | flops 3223322624 | bytes 16818176 | tf_op jit(solution)/shard_map/pqab,pqkac->pqkbc/dot_general | solution.py:105
  27.7 2.6 broadcast_add_fusion
  30.4 3.9 %slice.269 = f32[7,8,2,128,128]{4,3,2,1,0:T(8,128)} slice(f32[8,8,2,128,128]{4,3,2,1,0:T(8,128)S(1)} %bitcast.125), slice={[1:8], [0:8], [0:2], [0:128], [0:128]} | slice | bytes 14680064 | tf_op jit(solution)/shard_map/slice | solution.py:95
  34.3 4.0 %slice.260 = f32[8,7,2,128,128]{4,3,2,1,0:T(8,128)} slice(f32[8,8,2,128,128]{4,3,2,1,0:T(8,128)S(1)} %bitcast.125), slice={[0:8], [1:8], [0:2], [0:128], [0:128]} | slice | bytes 14680064 | tf_op jit(solution)/shard_map/slice | solution.py:94
  38.3 7.2 %convolution_bitcast_fusion = f32[8,8,2,128,128]{3,4,2,1,0:T(8,128)} fusion(f32[8,8,2,128,128]{4,3,2,1,0:T(8,128)S(1)} %bitcast.125, s32[8,8,128]{2,1,0:T(8,128)S(1)} %iota_add_fusion.1, pred[8,8,128]{2,1,0:T(8,128)(4,1)S(1)} %iota_compare_fusion.7), kind=kOutput, calls=%fused_computation.39 | convolution fusion | flops 3224371200 | bytes 16818176 | tf_op jit(solution)/shard_map/pqkrc,pqcd->pqkrd/dot_general | solution.py:104
  45.5 8.5 %copy.25 = f32[8,7,2,128,128]{3,4,2,1,0:T(8,128)} copy(f32[8,7,2,128,128]{4,3,2,1,0:T(8,128)} %slice.260) | data formatting | bytes 14680064
  56.6 5.2 %collective-permute-start.6 = (f32[2,10,1]{2,1,0:T(8,128)}, f32[2,10,1]{2,1,0:T(8,128)}, u32[]{:S(2)}, u32[]{:S(2)}) collective-permute-start(f32[2,10,1]{2,1,0:T(8,128)} %get-tuple-element.41), channel_id=1, source_target_pairs={{0,1},{1,2},{2,3},{3,4},{4,5},{5,6},{6,7},{7,8},{8,9},{9,10},{10,1... | collective-permute-start | bytes 248 | tf_op jit(solution)/shard_map/ppermute | solution.py:20
  61.9 8.5 %subtract_reduce_fusion = (f32[8,8]{1,0:T(8,128)S(1)}, f32[8,8]{1,0:T(8,128)S(1)}) fusion(f32[8,8,2,128,128]{4,3,2,1,0:T(8,128)} %fusion.17, f32[1,8,2,128,128]{4,3,2,1,0:T(8,128)S(1)} %collective-permute-done.4, f32[7,8,2,128,128]{4,3,2,1,0:T(8,128)} %slice.269), kind=kLoop, calls=%fused_computation.25 | loop fusion | flops 12582784 | bytes 16777728 | tf_op jit(solution)/shard_map/reduce_sum | solution.py:38
  71.6 5.2 %add_reduce_fusion.1 = (f32[8,8]{1,0:T(8,128)S(1)}, f32[8,8]{1,0:T(8,128)S(1)}) fusion(f32[8,8,2,128,128]{3,4,2,1,0:T(8,128)} %convolution_bitcast_fusion, f32[8,1,2,128,128]{3,4,2,1,0:T(8,128)S(1)} %collective-permute-done, f32[8,7,2,128,128]{3,4,2,1,0:T(8,128)S(1)} %copy-done), kind=kLoop, calls=%fused_computation.29 | loop fusion | flops 12582784 | bytes 16777728 | tf_op jit(solution)/shard_map/reduce_sum | solution.py:33
  78.3 3.0 %collective-permute-start.5 = (f32[2,8,1]{2,1,0:T(8,128)S(1)}, f32[2,8,1]{2,1,0:T(8,128)S(1)}, u32[]{:S(2)}, u32[]{:S(2)}) collective-permute-start(f32[2,8,1]{2,1,0:T(8,128)S(1)} %slice_maximum_fusion), channel_id=1, source_target_pairs={{0,1},{1,2},{2,3},{3,4},{4,5},{5,6},{6,7},{7,8},{8,9},{9,10},{10,1... | collective-permute-start | bytes 200 | tf_op jit(solution)/shard_map/ppermute | solution.py:29
  81.3 4.8 %collective-permute-start.7 = (f32[2,1,8]{2,1,0:T(1,128)S(1)}, f32[2,1,8]{2,1,0:T(1,128)S(1)}, u32[]{:S(2)}, u32[]{:S(2)}) collective-permute-start(f32[2,1,8]{2,1,0:T(1,128)S(1)} %pad_maximum_fusion.36), channel_id=1, source_target_pairs={{0,16},{16,32},{32,48},{48,64},{64,80},{80,96},{96,112},{1,17},{17... | collective-permute-start | bytes 200 | tf_op jit(solution)/shard_map/ppermute | solution.py:29
  86.1 7.8 %fusion.20 = f32[8,8,2,128,128]{4,3,2,1,0:T(8,128)} fusion(f32[1,8,2,128,128]{4,3,2,1,0:T(8,128)S(1)} %collective-permute-done.4, f32[7,8,2,128,128]{4,3,2,1,0:T(8,128)S(1)} %bitcast.127, s32[8,8,128]{2,1,0:T(8,128)S(1)} %copy-done.5, pred[8,8,128]{2,1,0:T(8,128)(4,1)S(1)} %copy-done.11), kind=kOutput, calls=%fused_computation.38 | convolution fusion | flops 3225419776 | bytes 16818176 | tf_op jit(solution)/shard_map/pqab,pqkbc->pqkac/dot_general | solution.py:126
  94.0 9.5 %fusion.1 = f32[8,8,2,128,128]{4,3,2,1,0:T(8,128)} fusion(f32[8,1,2,128,128]{3,4,2,1,0:T(8,128)S(1)} %collective-permute-done, f32[8,7,2,128,128]{3,4,2,1,0:T(8,128)S(1)} %copy-done, s32[8,8,128]{2,1,0:T(8,128)S(1)} %copy-done.3, pred[8,8,128]{2,1,0:T(8,128)(4,1)S(1)} %copy-done.8), kind=kOutput, calls=%fused_computation.11 | convolution fusion | flops 3225419776 | bytes 16818176 | tf_op jit(solution)/shard_map/pqkrd,pqcd->pqkrc/dot_general | solution.py:125
  105.6 67.8 %psum.14 = f32[]{:T(128)} all-reduce(f32[]{:T(128)} %get-tuple-element.14), channel_id=1, replica_groups=mesh['row'=8,'col'=16] {'row','col'}, use_global_device_ids=true, to_apply=%region_5.0 | all-reduce | flops 1 | bytes 8 | tf_op jit(solution)/shard_map/psum | solution.py:83
  174.1 3.2 %collective-permute-start.8 = (f32[2,1,8]{2,1,0:T(1,128)S(1)}, f32[2,1,8]{2,1,0:T(1,128)S(1)}, u32[]{:S(2)}, u32[]{:S(2)}) collective-permute-start(f32[2,1,8]{2,1,0:T(1,128)S(1)} %get-tuple-element.55), channel_id=1, source_target_pairs={{0,16},{16,32},{32,48},{48,64},{64,80},{80,96},{96,112},{1,17},{17... | collective-permute-start | bytes 200 | tf_op jit(solution)/shard_map/ppermute | solution.py:20
  177.3 1.9 collective-permute-start.9
  179.3 2.9 %collective-permute-done.9 = f32[2,1,8]{2,1,0:T(1,128)S(1)} collective-permute-done((f32[2,1,8]{2,1,0:T(1,128)S(1)}, f32[2,1,8]{2,1,0:T(1,128)S(1)}, u32[]{:S(2)}, u32[]{:S(2)}) %collective-permute-start.9) | collective-permute-done | bytes 96 | tf_op jit(solution)/shard_map/ppermute | solution.py:21
  183.6 4.0 %collective-permute-start.11 = (f32[2,10,1]{2,1,0:T(8,128)S(1)}, f32[2,10,1]{2,1,0:T(8,128)S(1)}, u32[]{:S(2)}, u32[]{:S(2)}) collective-permute-start(f32[2,10,1]{2,1,0:T(8,128)S(1)} %get-tuple-element.40), channel_id=1, source_target_pairs={{0,1},{1,2},{2,3},{3,4},{4,5},{5,6},{6,7},{7,8},{8,9},{9,10},{10,1... | collective-permute-start | bytes 248 | tf_op jit(solution)/shard_map/ppermute | solution.py:20
  189.1 67.1 %psum.15 = f32[]{:T(128)} all-reduce(f32[]{:T(128)} %get-tuple-element.6), channel_id=1, replica_groups=mesh['row'=8,'col'=16] {'row','col'}, use_global_device_ids=true, to_apply=%region_7.0 | all-reduce | flops 1 | bytes 8 | tf_op jit(solution)/shard_map/psum | solution.py:83
  257.0 1.9 collective-permute-start.12
  258.9 2.4 collective-permute-start.13
  261.4 2.5 collective-permute-done.13
  263.8 1.5 collective-permute-start.14
  265.4 4.4 %multiply_subtract_fusion.2 = (f32[8,8,1,128,128]{4,3,2,1,0:T(8,128)S(1)}, f32[8,8,1,128,128]{4,3,2,1,0:T(8,128)S(1)}) fusion(f32[8,8,2,128,128]{4,3,2,1,0:T(8,128)} %param.5, f32[8,8]{1,0:T(8,128)S(1)} %get-tuple-element.53, f32[8,8]{1,0:T(8,128)S(1)} %get-tuple-element.52), kind=kLoop, calls=%fused_computation.24 | loop fusion | flops 6291456 | bytes 16777728 | tf_op jit(solution)/shard_map/sub | solution.py:61
  271.3 4.2 %multiply_subtract_fusion = (f32[8,8,1,128,128]{4,3,2,1,0:T(8,128)}, f32[8,8,1,128,128]{4,3,2,1,0:T(8,128)}) fusion(f32[8,8,2,128,128]{4,3,2,1,0:T(8,128)S(1)} %bitcast.131, f32[8,8]{1,0:T(8,128)S(1)} %get-tuple-element.47, f32[8,8]{1,0:T(8,128)S(1)} %get-tuple-element.46), kind=kLoop, calls=%fused_computation.20 | loop fusion | flops 6291456 | bytes 16777728 | tf_op jit(solution)/shard_map/sub | solution.py:61
  275.6 4.0 %multiply_subtract_fusion.1 = (f32[8,8,1,128,128]{4,3,2,1,0:T(8,128)}, f32[8,8,1,128,128]{4,3,2,1,0:T(8,128)}) fusion(f32[8,8,2,128,128]{4,3,2,1,0:T(8,128)S(1)} %bitcast.129, f32[8,8]{1,0:T(8,128)S(1)} %get-tuple-element.56, f32[8,8]{1,0:T(8,128)S(1)} %get-tuple-element.57), kind=kLoop, calls=%fused_computation.22 | loop fusion | flops 6291456 | bytes 16777728 | tf_op jit(solution)/shard_map/sub | solution.py:61
  279.6 9.6 %fusion.3 = f32[8,8,2,128,128]{4,3,2,1,0:T(8,128)} fusion(f32[8,8,1,128,128]{4,3,2,1,0:T(8,128)S(1)} %get-tuple-element.32, f32[8,8,1,128,128]{4,3,2,1,0:T(8,128)S(1)} %get-tuple-element.31, f32[8,8,1,128,128]{4,3,2,1,0:T(8,128)} %get-tuple-element.30, f32[8,8,1,128,128]{4,3,2,1,0:T(8,128)} %get-tuple-element.29, ...), kind=kLoop, calls=%fused_computation.14 | loop fusion | flops 12582912 | bytes 37748736 | tf_op jit(solution)/shard_map/div | solution.py:150
  (113 shorter events, 14.5 us)
Async XLA Ops:
  0.6 10.9 %slice-start.2 = ((f32[8,8,2,128,128]{4,3,2,1,0:T(8,128)}), f32[8,1,2,128,128]{4,3,2,1,0:T(8,128)S(1)}, s32[]{:S(2)}) async-start(f32[8,8,2,128,128]{4,3,2,1,0:T(8,128)} %param.5), calls=%async_computation.2 | async-start | bytes 2097152 | tf_op jit(solution)/shard_map/slice | solution.py:92
  0.6 12.6 %copy-start.15 = (s32[8,8]{1,0:T(8,128)S(1)}, s32[8,8]{1,0:T(8,128)}, u32[]{:S(2)}) copy-start(s32[8,8]{1,0:T(8,128)} %param.8) | copy-start | bytes 772
  0.7 12.6 %copy-start.12 = (s32[8,8]{1,0:T(8,128)S(1)}, s32[8,8]{1,0:T(8,128)}, u32[]{:S(2)}) copy-start(s32[8,8]{1,0:T(8,128)} %param.9) | copy-start | bytes 772
  0.7 13.5 %copy-start.13 = (s32[8,8]{1,0:T(8,128)S(1)}, s32[8,8]{1,0:T(8,128)}, u32[]{:S(2)}) copy-start(s32[8,8]{1,0:T(8,128)} %param.7) | copy-start | bytes 772
  0.7 53.3 %collective-permute-start.2 = (f32[2,1,8]{2,1,0:T(1,128)}, f32[2,1,8]{2,1,0:T(1,128)}, u32[]{:S(2)}, u32[]{:S(2)}) collective-permute-start(f32[2,1,8]{2,1,0:T(1,128)} %constant.5.clone.1), channel_id=1, source_target_pairs={{16,0},{32,16},{48,32},{64,48},{80,64},{96,80},{112,96},{17,1},{33... | collective-permute-start | bytes 200 | tf_op jit(solution)/shard_map/ppermute | solution.py:21
  4.1 49.9 %collective-permute-start.1 = (f32[2,1,8]{2,1,0:T(1,128)}, f32[2,1,8]{2,1,0:T(1,128)}, u32[]{:S(2)}, u32[]{:S(2)}) collective-permute-start(f32[2,1,8]{2,1,0:T(1,128)} %constant.5.clone.1), channel_id=1, source_target_pairs={{0,16},{16,32},{32,48},{48,64},{64,80},{80,96},{96,112},{1,17},{17... | collective-permute-start | bytes 200 | tf_op jit(solution)/shard_map/ppermute | solution.py:20
  9.6 52.2 %collective-permute-start.4 = (f32[1,8,2,128,128]{4,3,2,1,0:T(8,128)}, f32[1,8,2,128,128]{4,3,2,1,0:T(8,128)S(1)}, u32[]{:S(2)}, u32[]{:S(2)}) collective-permute-start(f32[1,8,2,128,128]{4,3,2,1,0:T(8,128)} %slice.270), channel_id=1, source_target_pairs={{16,0},{32,16},{48,32},{64,48},{80,64},{96,80},{112,96},{17,1},{33... | collective-permute-start | bytes 3145736 | tf_op jit(solution)/shard_map/ppermute | solution.py:29
  11.9 58.5 %collective-permute-start = (f32[8,1,2,128,128]{3,4,2,1,0:T(8,128)S(1)}, f32[8,1,2,128,128]{3,4,2,1,0:T(8,128)S(1)}, u32[]{:S(2)}, u32[]{:S(2)}) collective-permute-start(f32[8,1,2,128,128]{3,4,2,1,0:T(8,128)S(1)} %copy.26), channel_id=1, source_target_pairs={{1,0},{2,1},{3,2},{4,3},{5,4},{6,5},{7,6},{8,7},{9,8},{10,9},{11,1... | collective-permute-start | bytes 3145736 | tf_op jit(solution)/shard_map/ppermute | solution.py:29
  13.3 14.3 %copy-start.4 = (s32[8,8,128]{2,1,0:T(8,128)}, s32[8,8,128]{2,1,0:T(8,128)S(1)}, u32[]{:S(2)}) copy-start(s32[8,8,128]{2,1,0:T(8,128)S(1)} %iota_add_fusion) | copy-start | bytes 98308
  14.2 24.1 %copy-start.2 = (s32[8,8,128]{2,1,0:T(8,128)}, s32[8,8,128]{2,1,0:T(8,128)S(1)}, u32[]{:S(2)}) copy-start(s32[8,8,128]{2,1,0:T(8,128)S(1)} %iota_add_fusion.1) | copy-start | bytes 98308
  14.2 16.2 %slice-start = ((s8[8388608]{0:T(1024)(128)(4,1)}), s8[4194304]{0:T(1024)(128)(4,1)S(1)}, s32[]{:S(2)}) async-start(s8[8388608]{0:T(1024)(128)(4,1)} %bitcast.124), calls=%async_computation | async-start | bytes 8388608
  15.1 12.6 %copy-start.16 = (s32[8,8]{1,0:T(8,128)S(1)}, s32[8,8]{1,0:T(8,128)}, u32[]{:S(2)}) copy-start(s32[8,8]{1,0:T(8,128)} %param.6) | copy-start | bytes 772
  15.1 15.3 %slice-start.1 = ((s8[8388608]{0:T(1024)(128)(4,1)}), s8[4194304]{0:T(1024)(128)(4,1)S(1)}, s32[]{:S(2)}) async-start(s8[8388608]{0:T(1024)(128)(4,1)} %bitcast.124), calls=%async_computation.1 | async-start | bytes 8388608
  55.4 22.1 %collective-permute-start.3 = (f32[2,10,1]{2,1,0:T(8,128)S(1)}, f32[2,10,1]{2,1,0:T(8,128)S(1)}, u32[]{:S(2)}, u32[]{:S(2)}) collective-permute-start(f32[2,10,1]{2,1,0:T(8,128)S(1)} %get-tuple-element.42), channel_id=1, source_target_pairs={{1,0},{2,1},{3,2},{4,3},{5,4},{6,5},{7,6},{8,7},{9,8},{10,9},{11,1... | collective-permute-start | bytes 248 | tf_op jit(solution)/shard_map/ppermute | solution.py:21
  56.6 46.9 %collective-permute-start.6 = (f32[2,10,1]{2,1,0:T(8,128)}, f32[2,10,1]{2,1,0:T(8,128)}, u32[]{:S(2)}, u32[]{:S(2)}) collective-permute-start(f32[2,10,1]{2,1,0:T(8,128)} %get-tuple-element.41), channel_id=1, source_target_pairs={{0,1},{1,2},{2,3},{3,4},{4,5},{5,6},{6,7},{7,8},{8,9},{9,10},{10,1... | collective-permute-start | bytes 248 | tf_op jit(solution)/shard_map/ppermute | solution.py:20
  61.9 9.7 %copy-start = (f32[8,7,2,128,128]{3,4,2,1,0:T(8,128)S(1)}, f32[8,7,2,128,128]{3,4,2,1,0:T(8,128)}, u32[]{:S(2)}) copy-start(f32[8,7,2,128,128]{3,4,2,1,0:T(8,128)} %copy.25) | copy-start | bytes 22020100
  61.9 24.2 %slice-start.3 = ((s8[7340032]{0:T(1024)(128)(4,1)}), s8[4194304]{0:T(1024)(128)(4,1)S(1)}, s32[]{:S(2)}) async-start(s8[7340032]{0:T(1024)(128)(4,1)} %bitcast.126), calls=%async_computation.3 | async-start | bytes 8388608
  70.4 15.7 %slice-start.4 = ((s8[7340032]{0:T(1024)(128)(4,1)}), s8[3145728]{0:T(1024)(128)(4,1)S(1)}, s32[]{:S(2)}) async-start(s8[7340032]{0:T(1024)(128)(4,1)} %bitcast.126), calls=%async_computation.4 | async-start | bytes 6291456
  71.6 14.5 %copy-start.5 = (s32[8,8,128]{2,1,0:T(8,128)S(1)}, s32[8,8,128]{2,1,0:T(8,128)}, u32[]{:S(2)}) copy-start(s32[8,8,128]{2,1,0:T(8,128)} %copy-done.4) | copy-start | bytes 98308
  71.6 14.5 %copy-start.11 = (pred[8,8,128]{2,1,0:T(8,128)(4,1)S(1)}, pred[8,8,128]{2,1,0:T(8,128)(4,1)}, u32[]{:S(2)}) copy-start(pred[8,8,128]{2,1,0:T(8,128)(4,1)} %copy-done.10) | copy-start | bytes 24580
  78.3 25.1 %collective-permute-start.5 = (f32[2,8,1]{2,1,0:T(8,128)S(1)}, f32[2,8,1]{2,1,0:T(8,128)S(1)}, u32[]{:S(2)}, u32[]{:S(2)}) collective-permute-start(f32[2,8,1]{2,1,0:T(8,128)S(1)} %slice_maximum_fusion), channel_id=1, source_target_pairs={{0,1},{1,2},{2,3},{3,4},{4,5},{5,6},{6,7},{7,8},{8,9},{9,10},{10,1... | collective-permute-start | bytes 200 | tf_op jit(solution)/shard_map/ppermute | solution.py:29
  81.3 12.6 %copy-start.3 = (s32[8,8,128]{2,1,0:T(8,128)S(1)}, s32[8,8,128]{2,1,0:T(8,128)}, u32[]{:S(2)}) copy-start(s32[8,8,128]{2,1,0:T(8,128)} %copy-done.2) | copy-start | bytes 98308
  81.3 12.6 %copy-start.8 = (pred[8,8,128]{2,1,0:T(8,128)(4,1)S(1)}, pred[8,8,128]{2,1,0:T(8,128)(4,1)}, u32[]{:S(2)}) copy-start(pred[8,8,128]{2,1,0:T(8,128)(4,1)} %copy-done.7) | copy-start | bytes 24580
  81.3 23.0 %collective-permute-start.7 = (f32[2,1,8]{2,1,0:T(1,128)S(1)}, f32[2,1,8]{2,1,0:T(1,128)S(1)}, u32[]{:S(2)}, u32[]{:S(2)}) collective-permute-start(f32[2,1,8]{2,1,0:T(1,128)S(1)} %pad_maximum_fusion.36), channel_id=1, source_target_pairs={{0,16},{16,32},{32,48},{48,64},{64,80},{80,96},{96,112},{1,17},{17... | collective-permute-start | bytes 200 | tf_op jit(solution)/shard_map/ppermute | solution.py:29
  174.1 5.1 %collective-permute-start.8 = (f32[2,1,8]{2,1,0:T(1,128)S(1)}, f32[2,1,8]{2,1,0:T(1,128)S(1)}, u32[]{:S(2)}, u32[]{:S(2)}) collective-permute-start(f32[2,1,8]{2,1,0:T(1,128)S(1)} %get-tuple-element.55), channel_id=1, source_target_pairs={{0,16},{16,32},{32,48},{48,64},{64,80},{80,96},{96,112},{1,17},{17... | collective-permute-start | bytes 200 | tf_op jit(solution)/shard_map/ppermute | solution.py:20
  177.3 4.9 %collective-permute-start.9 = (f32[2,1,8]{2,1,0:T(1,128)S(1)}, f32[2,1,8]{2,1,0:T(1,128)S(1)}, u32[]{:S(2)}, u32[]{:S(2)}) collective-permute-start(f32[2,1,8]{2,1,0:T(1,128)S(1)} %get-tuple-element.54), channel_id=1, source_target_pairs={{16,0},{32,16},{48,32},{64,48},{80,64},{96,80},{112,96},{17,1},{33... | collective-permute-start | bytes 200 | tf_op jit(solution)/shard_map/ppermute | solution.py:21
  182.3 5.3 %collective-permute-start.10 = (f32[2,10,1]{2,1,0:T(8,128)S(1)}, f32[2,10,1]{2,1,0:T(8,128)S(1)}, u32[]{:S(2)}, u32[]{:S(2)}) collective-permute-start(f32[2,10,1]{2,1,0:T(8,128)S(1)} %get-tuple-element.39), channel_id=1, source_target_pairs={{1,0},{2,1},{3,2},{4,3},{5,4},{6,5},{7,6},{8,7},{9,8},{10,9},{11,1... | collective-permute-start | bytes 248 | tf_op jit(solution)/shard_map/ppermute | solution.py:21
  183.6 4.8 %collective-permute-start.11 = (f32[2,10,1]{2,1,0:T(8,128)S(1)}, f32[2,10,1]{2,1,0:T(8,128)S(1)}, u32[]{:S(2)}, u32[]{:S(2)}) collective-permute-start(f32[2,10,1]{2,1,0:T(8,128)S(1)} %get-tuple-element.40), channel_id=1, source_target_pairs={{0,1},{1,2},{2,3},{3,4},{4,5},{5,6},{6,7},{7,8},{8,9},{9,10},{10,1... | collective-permute-start | bytes 248 | tf_op jit(solution)/shard_map/ppermute | solution.py:20
  257.0 12.8 %copy-start.9 = (f32[2,8,8]{2,1,0:T(8,128)}, f32[2,8,8]{2,1,0:T(8,128)S(1)}, u32[]{:S(2)}) copy-start(f32[2,8,8]{2,1,0:T(8,128)S(1)} %broadcast_multiply_fusion) | copy-start | bytes 1540
  257.0 4.4 %collective-permute-start.12 = (f32[2,1,8]{2,1,0:T(1,128)S(1)}, f32[2,1,8]{2,1,0:T(1,128)S(1)}, u32[]{:S(2)}, u32[]{:S(2)}) collective-permute-start(f32[2,1,8]{2,1,0:T(1,128)S(1)} %get-tuple-element.50), channel_id=1, source_target_pairs={{0,16},{16,32},{32,48},{48,64},{64,80},{80,96},{96,112},{1,17},{17... | collective-permute-start | bytes 200 | tf_op jit(solution)/shard_map/ppermute | solution.py:20
  258.9 4.9 %collective-permute-start.13 = (f32[2,1,8]{2,1,0:T(1,128)S(1)}, f32[2,1,8]{2,1,0:T(1,128)S(1)}, u32[]{:S(2)}, u32[]{:S(2)}) collective-permute-start(f32[2,1,8]{2,1,0:T(1,128)S(1)} %get-tuple-element.51), channel_id=1, source_target_pairs={{16,0},{32,16},{48,32},{64,48},{80,64},{96,80},{112,96},{17,1},{33... | collective-permute-start | bytes 200 | tf_op jit(solution)/shard_map/ppermute | solution.py:21
  263.8 5.9 %collective-permute-start.14 = (f32[2,10,1]{2,1,0:T(8,128)S(1)}, f32[2,10,1]{2,1,0:T(8,128)S(1)}, u32[]{:S(2)}, u32[]{:S(2)}) collective-permute-start(f32[2,10,1]{2,1,0:T(8,128)S(1)} %pad_maximum_fusion.6), channel_id=1, source_target_pairs={{1,0},{2,1},{3,2},{4,3},{5,4},{6,5},{7,6},{8,7},{9,8},{10,9},{11,1... | collective-permute-start | bytes 248 | tf_op jit(solution)/shard_map/ppermute | solution.py:21
  (9 other events, 49.7 us)
where the time goes:
time: 292 us; the launch traced here: 289 us
  blocking collectives  135 us (46%)
  other arithmetic  45.7 us (16%)
  starting transfers between devices  40.3 us (14%)
  matrix products  37 us (13%)
  local copies, waits for them, and re-layouts  22.6 us (8%)
  waiting for transfers between devices  6.16 us (2%)
    psum x2, blocking collectives, scale_each(): total = lax.psum(jnp.sum(interior * interior), ('row', 'col'))  135 us
    ppermute x5, starting transfers between devices, extended(): before = lax.ppermute(last, axis, up)  17.5 us
    sub x3, other arithmetic, rotate(): factor[..., 0:1, :, :] * field[..., 0:1, :, :]  12.6 us
    dot_general x1, matrix products, local(): jnp.einsum('pqab,pqkac->pqkbc', south_select, patches, precision=highest)  12.5 us
    ppermute x6, starting transfers between devices, extended(): after = lax.ppermute(first, axis, down)  11.9 us
    unnamed x52, local copies, waits for them, and re-layouts  11.7 us
    ppermute x4, starting transfers between devices, shifted_2(): return lax.ppermute(array, axis, pairs)  10.9 us
    div x1, other arithmetic, local(): return (numer / weight, phase_now)  9.56 us
  transfers between devices with their start and end apart: 15, of which 3 were waited for; matrix products, arithmetic and copies ran while one was open for 29% of the time, Pallas kernels for 0%

commit v1 on v0

v1 whole, which is shorter than its diff:
```python
import functools

import jax
import jax.numpy as jnp
from jax import lax
from jax.experimental import pallas as pl
from jax.experimental.pallas import tpu as pltpu
from jax.sharding import PartitionSpec as P

ITERS = 2
EPS_NORM = 1.0
SIDE = 128
HALF = 64
ROW0 = 56
PAD = 8
HIGHEST = lax.Precision.HIGHEST


def lanes(shape):
    return lax.broadcasted_iota(jnp.int32, shape, len(shape) - 1)


def fold8(x):
    total = x[0:8]
    for k in range(8, x.shape[0], 8):
        total = total + x[k : k + 8]
    return total


def products(ar, ai, br, bi):
    return fold8(ar * br + ai * bi), fold8(ar * bi - ai * br)


def placed_rows(pad_ref, j, part, first, offset):
    start = jnp.maximum(first - offset, -PAD) + PAD
    return pad_ref[j, part, pl.ds(start, 8), :]


def east_sums(a_real, a_imag, b_real, b_imag, offset, width):
    real, imag = None, None
    for k in range(0, SIDE, 32):
        pr, pi = products(a_real(k), a_imag(k), b_real(k), b_imag(k))
        real = pr if real is None else real + pr
        imag = pi if imag is None else imag + pi
    lane = lanes((8, SIDE))
    keep = (lane >= offset) & (lane < offset + width)
    return jnp.where(keep, real, 0.0), jnp.where(keep, imag, 0.0)


def south_sums(a_ref_at, pad_ref, j, offset, width):
    row = lax.broadcasted_iota(jnp.int32, (8, SIDE), 0)
    real = jnp.zeros((8, SIDE), jnp.float32)
    imag = real
    for first in range(ROW0, SIDE, 8):
        at = row + first
        keep = (at >= offset) & (at < offset + width)
        br = placed_rows(pad_ref, j, 0, first, offset)
        bi = placed_rows(pad_ref, j, 1, first, offset)
        ar, ai = a_ref_at(0, first), a_ref_at(1, first)
        real = real + jnp.where(keep, ar * br + ai * bi, 0.0)
        imag = imag + jnp.where(keep, ar * bi - ai * br, 0.0)
    return real, imag


def rows_of(parts):
    return jnp.concatenate([jnp.sum(x, axis=0, keepdims=True) for x in parts], axis=0)


def inner_kernel(ro, rw, do, dw, p_ref, x_ref, pad_ref):
    step = pl.program_id(0)
    rows, cols = x_ref.shape[1] // 8, p_ref.shape[1]
    i = rows - 1 - step
    zero = jnp.zeros((8, SIDE), jnp.float32)
    at = pl.ds(pl.multiple_of(i * 8, 8), 8)
    east = [[], []]
    for j in range(cols - 1):
        o, w = ro[i, j], rw[i, j]
        sums = east_sums(
            lambda k: p_ref[0, j, 0, k : k + 32, :],
            lambda k: p_ref[0, j, 1, k : k + 32, :],
            lambda k: pltpu.roll(p_ref[0, j + 1, 0, k : k + 32, :], o, 1),
            lambda k: pltpu.roll(p_ref[0, j + 1, 1, k : k + 32, :], o, 1),
            o,
            w,
        )
        for part in range(2):
            east[part].append(sums[part])
    for part in range(2):
        x_ref[part, at, :] = rows_of(east[part] + [zero])

    @pl.when(step > 0)
    def _():
        south = [[], []]
        for j in range(cols):
            sums = south_sums(
                lambda part, k: p_ref[0, j, part, k : k + 8, :], pad_ref, j, do[i, j], dw[i, j]
            )
            for part in range(2):
                south[part].append(sums[part])
        for part in range(2):
            x_ref[2 + part, at, :] = rows_of(south[part])

    @pl.when(step == 0)
    def _():
        for part in range(2):
            x_ref[2 + part, at, :] = zero

    pad_ref[:, :, PAD : PAD + HALF, :] = p_ref[0, :, :, 0:HALF, :]


def rim_kernel(ro, rw, do, dw, x_ref, col_ref, row_ref, east_ref, south_ref, wide_ref, out_ref, all_ref, pad_ref):
    rows, cols = col_ref.shape[0], row_ref.shape[1]
    pad_ref[:, :, PAD : PAD + HALF, :] = south_ref[...]
    all_ref[...] = x_ref[...]
    for i in range(rows):
        o, w = ro[i, cols - 1], rw[i, cols - 1]
        o2 = jnp.where(o >= HALF, o - HALF, o + HALF)
        sums = east_sums(
            lambda k: col_ref[i, 0, 0, k : k + 32, :],
            lambda k: col_ref[i, 0, 1, k : k + 32, :],
            lambda k: pltpu.roll(east_ref[i, k : k + 32, :], o, 1),
            lambda k: pltpu.roll(east_ref[i, k : k + 32, :], o2, 1),
            o,
            w,
        )
        at = i * cols + cols - 1
        for part in range(2):
            all_ref[part, at : at + 1, :] = jnp.sum(sums[part], axis=0, keepdims=True)
    south = [[], []]
    for j in range(cols):
        sums = south_sums(
            lambda part, k: row_ref[0, j, part, k : k + 8, :],
            pad_ref,
            j,
            do[rows - 1, j],
            dw[rows - 1, j],
        )
        for part in range(2):
            south[part].append(sums[part])
    for part in range(2):
        all_ref[2 + part, (rows - 1) * 8 : rows * 8, :] = rows_of(south[part])
    ones = jnp.ones((8, SIDE), jnp.float32)
    flat = all_ref[...].reshape(4 * rows * cols, SIDE)
    sums = lax.dot_general(
        ones, flat, (((1,), (1,)), ((), ())), precision=HIGHEST, preferred_element_type=jnp.float32
    )
    both = jnp.concatenate([sums[0:1, 0:SIDE], sums[0:1, SIDE : 2 * SIDE]], axis=0)
    out_ref[...] = both / jnp.sqrt(SIDE * wide_ref[...].astype(jnp.float32))


def sync_phases(east, south, n_cols, count):
    lane = lanes(east.shape)
    low = lane < HALF
    col, row = lane % 8, (lane // 8) % 8

    def lane_roll(x, by):
        return pltpu.roll(x, by % SIDE, 1)

    def dev_roll(x, by):
        return pltpu.roll(x, by % x.shape[0], 0)

    def to_east(x):
        return jnp.where(col < 7, lane_roll(x, -1), lane_roll(dev_roll(x, -1), 7))

    def to_west(x):
        return jnp.where(col > 0, lane_roll(x, 1), lane_roll(dev_roll(x, 1), -7))

    def to_south(x):
        return jnp.where(row < 7, lane_roll(x, -8), lane_roll(dev_roll(x, -n_cols), 56))

    def to_north(x):
        return jnp.where(row > 0, lane_roll(x, 8), lane_roll(dev_roll(x, n_cols), -56))

    def swap(x):
        return lane_roll(x, HALF)

    def split(x):
        other = swap(x)
        imag = jnp.where(low, other, x)
        return jnp.where(low, x, other), jnp.where(low, -imag, imag)

    east_r, east_i = split(east)
    south_r, south_i = split(south)
    phase = None
    for step in range(ITERS):
        if step == 0:
            image = east + south
            image = image + to_west(jnp.where(low, east, -east))
            image = image + to_north(jnp.where(low, south, -south))
        else:
            beside, below, other = to_east(phase), to_south(phase), swap(phase)
            image = east_r * beside + east_i * swap(beside)
            image = image + south_r * below + south_i * swap(below)
            image = image + to_west(east_r * phase - east_i * other)
            image = image + to_north(south_r * phase - south_i * other)
        total = jnp.sum(jnp.sum(image * image, axis=0, keepdims=True), axis=1, keepdims=True)
        phase = image / jnp.sqrt(total / count + EPS_NORM)
    return phase


def blend_kernel(
    n_cols, ro, rw, do, dw, me, g_ref, p_ref, east_ref, south_ref, out_ref, phase_ref, all_ref, near_ref, fac, sem, pad_ref
):
    step = pl.program_id(0)
    rows, cols = pl.num_programs(0), p_ref.shape[1]
    i = rows - 1 - step

    @pl.when(step == 0)
    def _():
        n_dev = all_ref.shape[0]
        all_ref[...] = sync_phases(
            g_ref[pl.ds(0, n_dev, 2), :], g_ref[pl.ds(1, n_dev, 2), :], n_cols, n_dev * HALF
        )
        d = me[0]
        lane = lanes((1, SIDE))
        own = all_ref[pl.ds(d, 1), :]
        right = all_ref[pl.ds(lax.rem(d + 1, n_dev), 1), :]
        lower = all_ref[pl.ds(lax.rem(d + n_cols, n_dev), 1), :]
        near_ref[0:1, :] = own
        near_ref[1:2, :] = jnp.where(lane % 8 < 7, pltpu.roll(own, SIDE - 1, 1), pltpu.roll(right, 7, 1))
        near_ref[2:3, :] = jnp.where(
            (lane // 8) % 8 < 7, pltpu.roll(own, SIDE - 8, 1), pltpu.roll(lower, 56, 1)
        )
        copy = pltpu.make_async_copy(near_ref, fac, sem)
        copy.start()
        for part in range(2):
            for k in range(8):
                at = part * HALF + k * 8
                phase_ref[part, k : k + 1, :] = own[:, at : at + 8]
        pad_ref[:, :, PAD : PAD + HALF, :] = south_ref[...]
        copy.wait()

    lane = lanes((8, SIDE))
    row = lax.broadcasted_iota(jnp.int32, (8, SIDE), 0)
    for j in range(cols):
        o, w = ro[i, j], rw[i, j]
        if j == cols - 1:
            w = jnp.where(me[1] > 0, w, 0)
        keep = (lane >= o) & (lane < o + w)
        down = do[i, j]
        deep = jnp.where((me[2] > 0) | (step > 0), dw[i, j], 0)
        at = i * 8 + j
        inv = jnp.where(keep, 0.5, 1.0)
        inv_south = jnp.where(keep, 1.0 / 3.0, 0.5)
        ratio = jnp.where(keep, 2.0 / 3.0, 0.5)
        gr, gi = fac[0, at] * inv, fac[0, HALF + at] * inv
        er = jnp.where(keep, fac[1, at] * 0.5, 0.0)
        ei = jnp.where(keep, fac[1, HALF + at] * 0.5, 0.0)
        sr, si = fac[2, at] * inv_south, fac[2, HALF + at] * inv_south
        o2 = jnp.where(o >= HALF, o - HALF, o + HALF)
        for first in range(0, SIDE, 8):
            rng = slice(first, first + 8)
            ar, ai = p_ref[0, j, 0, rng, :], p_ref[0, j, 1, rng, :]
            if j < cols - 1:
                br = pltpu.roll(p_ref[0, j + 1, 0, rng, :], o, 1)
                bi = pltpu.roll(p_ref[0, j + 1, 1, rng, :], o, 1)
            else:
                br = pltpu.roll(east_ref[0, rng, :], o, 1)
                bi = pltpu.roll(east_ref[0, rng, :], o2, 1)
            real = (gr * ar - gi * ai) + (er * br - ei * bi)
            imag = (gr * ai + gi * ar) + (er * bi + ei * br)
            if first >= ROW0:
                here = row + first
                inside = (here >= down) & (here < down + deep)
                cr = placed_rows(pad_ref, j, 0, first, down)
                ci = placed_rows(pad_ref, j, 1, first, down)
                real = jnp.where(inside, real * ratio + (sr * cr - si * ci), real)
                imag = jnp.where(inside, imag * ratio + (sr * ci + si * cr), imag)
            out_ref[0, j, 0, rng, :] = real
            out_ref[0, j, 1, rng, :] = imag
    pad_ref[:, :, PAD : PAD + HALF, :] = p_ref[0, :, :, 0:HALF, :]


def local(patches, right_offset, right_width, down_offset, down_width):
    rows, cols = patches.shape[:2]
    n_rows, n_cols = lax.axis_size("row"), lax.axis_size("col")
    n_dev = n_rows * n_cols
    r, c = lax.axis_index("row"), lax.axis_index("col")
    tables = (right_offset, right_width, down_offset, down_width)

    strip = jnp.concatenate([patches[:, 0, 0, :, :HALF], patches[:, 0, 1, :, :HALF]], axis=-1)
    east_edge = lax.ppermute(strip, "col", [(k + 1, k) for k in range(n_cols - 1)])
    south_edge = lax.ppermute(patches[0, :, :, :HALF, :], "row", [(k + 1, k) for k in range(n_rows - 1)])

    plane = (2, SIDE, SIDE)
    pad = pltpu.VMEM((cols, 2, PAD + HALF + 8, SIDE), jnp.float32)
    limit = pltpu.CompilerParams(vmem_limit_bytes=24 * 2**20, dimension_semantics=("arbitrary",))
    sums = pl.pallas_call(
        inner_kernel,
        out_shape=jax.ShapeDtypeStruct((4, rows * cols, SIDE), jnp.float32),
        grid_spec=pltpu.PrefetchScalarGridSpec(
            num_scalar_prefetch=4,
            grid=(rows,),
            in_specs=[pl.BlockSpec((1, cols, *plane), lambda s, *_: (rows - 1 - s, 0, 0, 0, 0))],
            out_specs=pl.BlockSpec((4, rows * cols, SIDE), lambda s, *_: (0, 0, 0)),
            scratch_shapes=[pad],
        ),
        compiler_params=limit,
        cost_estimate=pl.CostEstimate(flops=20_000_000, bytes_accessed=9_000_000, transcendentals=0),
        name="inner",
    )(*tables, patches)

    wide = jnp.stack([right_width.reshape(-1), down_width.reshape(-1)])
    wide = jnp.concatenate([wide, wide], axis=1)
    full = lambda shape: pl.BlockSpec(shape, lambda s, *_: (0,) * len(shape))
    corr = pl.pallas_call(
        rim_kernel,
        out_shape=jax.ShapeDtypeStruct((2, SIDE), jnp.float32),
        grid_spec=pltpu.PrefetchScalarGridSpec(
            num_scalar_prefetch=4,
            grid=(1,),
            in_specs=[
                full((4, rows * cols, SIDE)),
                pl.BlockSpec((rows, 1, *plane), lambda s, *_: (0, cols - 1, 0, 0, 0)),
                pl.BlockSpec((1, cols, *plane), lambda s, *_: (rows - 1, 0, 0, 0, 0)),
                full((rows, SIDE, SIDE)),
                full((cols, 2, HALF, SIDE)),
                full((2, SIDE)),
            ],
            out_specs=full((2, SIDE)),
            scratch_shapes=[pltpu.VMEM((4, rows * cols, SIDE), jnp.float32), pad],
        ),
        compiler_params=limit,
        cost_estimate=pl.CostEstimate(flops=5_000_000, bytes_accessed=3_000_000, transcendentals=0),
        name="rim",
    )(*tables, sums, patches, patches, east_edge, south_edge, wide)

    sent = jnp.broadcast_to(corr[None], (n_dev, 2, SIDE)).reshape(n_dev * 2, SIDE)
    grid = lax.all_to_all(sent, ("row", "col"), 0, 0, tiled=True)

    me = jnp.stack([r * n_cols + c, (c < n_cols - 1).astype(jnp.int32), (r < n_rows - 1).astype(jnp.int32)])
    blended, phases = pl.pallas_call(
        functools.partial(blend_kernel, n_cols),
        out_shape=(
            jax.ShapeDtypeStruct(patches.shape, jnp.float32),
            jax.ShapeDtypeStruct((2, rows, cols), jnp.float32),
        ),
        grid_spec=pltpu.PrefetchScalarGridSpec(
            num_scalar_prefetch=5,
            grid=(rows,),
            in_specs=[
                full((n_dev * 2, SIDE)),
                pl.BlockSpec((1, cols, *plane), lambda s, *_: (rows - 1 - s, 0, 0, 0, 0)),
                pl.BlockSpec((1, SIDE, SIDE), lambda s, *_: (rows - 1 - s, 0, 0)),
                full((cols, 2, HALF, SIDE)),
            ],
            out_specs=[
                pl.BlockSpec((1, cols, *plane), lambda s, *_: (rows - 1 - s, 0, 0, 0, 0)),
                full((2, rows, cols)),
            ],
            scratch_shapes=[
                pltpu.VMEM((n_dev, SIDE), jnp.float32),
                pltpu.VMEM((8, SIDE), jnp.float32),
                pltpu.SMEM((8, SIDE), jnp.float32),
                pltpu.SemaphoreType.DMA,
                pad,
            ],
        ),
        compiler_params=limit,
        cost_estimate=pl.CostEstimate(flops=30_000_000, bytes_accessed=18_000_000, transcendentals=0),
        name="blend",
    )(*tables, me, grid, patches, east_edge, south_edge)
    return blended, phases


def solution(mesh):
    return jax.shard_map(
        local,
        mesh=mesh,
        in_specs=(P("row", "col", None, None, None), *(P("row", "col"),) * 4),
        out_specs=(P("row", "col", None, None, None), P(None, "row", "col")),
        check_vma=False,
    )
```

time: 292 us -> 59.5 us (0.20)
  blocking collectives: 135 us -> 0 us
  other arithmetic: 45.7 us -> 0.36 us
  matrix products: 37 us -> 0 us
  starting transfers between devices: 40.3 us -> 17.1 us
  Pallas kernels: 0 us -> 15.5 us
  local copies, waits for them, and re-layouts: 22.6 us -> 14.2 us
  waiting for transfers between devices: 6.16 us -> 11.1 us
    psum x2 -> x0, blocking collectives: 135 us -> none  [scale_each(): total = lax.psum(jnp.sum(interior * interior), ('row', 'col'))]
    dot_general x4 -> x0, matrix products: 37 us -> none  [the longest x1 12.5 us: local(): jnp.einsum('pqab,pqkac->pqkbc', south_select, patches, precision=highest)]
    ppermute x15 -> x2, starting transfers between devices: 40.3 us -> 4.62 us  [the longest x1 3.33 us: local(): lax.ppermute(patches[0, :, :, :HALF, :], 'row', [(k + 1, k) for k in rang...]
    pallas_call x0 -> x3, Pallas kernels: none -> 15.5 us  [the longest x1 8.49 us: local(): pl.pallas_call(functools.partial(blend_kernel, n_cols), out_shape=(jax.Sh...]
    reduce_sum x4 -> x0, other arithmetic: 15 us -> none  [the longest x1 8.53 us: correlate(): jnp.sum(shifted[..., 0, :, :] * partner[..., 1, :, :] - shifted[..., 1, :...]
    sub x5 -> x0, other arithmetic: 12.6 us -> none  [the longest x3 12.6 us: rotate(): factor[..., 0:1, :, :] * field[..., 0:1, :, :]]
    all_to_all x0 -> x1, starting transfers between devices: none -> 12.5 us  [local(): grid = lax.all_to_all(sent, ('row', 'col'), 0, 0, tiled=True)]
    slice x9 -> x0, local copies, waits for them, and re-layouts: 10.9 us -> none  [the longest x1 3.98 us: local(): east_patch = jnp.concatenate([patches[:, 1:], east_edge], axis=1)]
  transfers between devices with their start and end apart: 15 -> 3, of which waited for: 3 -> 2; matrix products, arithmetic and copies ran while one was open for 29% -> 5% of each run, Pallas kernels for 0% -> 9%
where the time goes in v1:
time: 59.5 us; the launch traced here: 59 us
  starting transfers between devices  17.1 us (29%)
  Pallas kernels  15.5 us (26%)
  local copies, waits for them, and re-layouts  14.2 us (24%)
  waiting for transfers between devices  11.1 us (19%)
  between operations  0.74 us (1%)
    all_to_all x1, starting transfers between devices, local(): grid = lax.all_to_all(sent, ('row', 'col'), 0, 0, tiled=True)  12.5 us
    all_to_all x1, waiting for transfers between devices, local(): grid = lax.all_to_all(sent, ('row', 'col'), 0, 0, tiled=True)  10.1 us
    unnamed x20, local copies, waits for them, and re-layouts  9.52 us
    pallas_call x1, Pallas kernels, local(): pl.pallas_call(functools.partial(blend_kernel, n_cols), out_shape=(jax.Sh...  8.49 us
    pallas_call x1, Pallas kernels, local(): pl.pallas_call(inner_kernel, out_shape=jax.ShapeDtypeStruct((4, rows * co...  5.49 us
    ppermute x1, starting transfers between devices, local(): lax.ppermute(patches[0, :, :, :HALF, :], 'row', [(k + 1, k) for k in rang...  3.33 us
    pallas_call x1, Pallas kernels, local(): pl.pallas_call(rim_kernel, out_shape=jax.ShapeDtypeStruct((2, SIDE), jnp....  1.56 us
    another operation x2, local copies, waits for them, and re-layouts, local(): wide = jnp.stack([right_width.reshape(-1), down_width.reshape(-1)])  1.53 us
  transfers between devices with their start and end apart: 3, of which 2 were waited for; matrix products, arithmetic and copies ran while one was open for 5% of the time, Pallas kernels for 9%

profile of v1, /device:TPU:1, one launch (start us, length us, event | category | flops | bytes accessed | tf_op | source)
XLA Modules:
  0.0 59.0 jit_solution(6569252235581908910)
XLA Ops:
  0.6 1.1 %slice_bitcast_fusion = f32[8,2,64,128]{3,2,1,0:T(8,128)S(1)} fusion(f32[8,8,2,128,128]{4,3,2,1,0:T(8,128)} %p_ref.3), kind=kLoop, calls=%fused_computation.1 | loop fusion | bytes 1048576 | tf_op jit(solution)/shard_map/squeeze | solution.py:283
  1.7 3.3 %collective-permute-start.1 = (f32[8,2,64,128]{3,2,1,0:T(8,128)S(1)}, f32[8,2,64,128]{3,2,1,0:T(8,128)S(1)}, u32[]{:S(2)}, u32[]{:S(2)}) collective-permute-start(f32[8,2,64,128]{3,2,1,0:T(8,128)S(1)} %slice_bitcast_fusion), channel_id=1, source_target_pairs={{16,0},{32,16},{48,32},{64,48},{80,64},{96,80},{112,96},{17,1},{33... | collective-permute-start | bytes 1572872 | tf_op jit(solution)/shard_map/ppermute | solution.py:283
  5.1 1.3 %slice_bitcast_fusion.2 = (f32[8,128,64]{2,1,0:T(8,128)S(1)}, f32[8,128,64]{2,1,0:T(8,128)S(1)}) fusion(f32[8,8,2,128,128]{4,3,2,1,0:T(8,128)} %p_ref.3), kind=kLoop, calls=%fused_computation.3 | loop fusion | bytes 1048576 | tf_op jit(solution)/shard_map/squeeze | solution.py:281
  6.4 0.2 pad_maximum_fusion
  6.6 1.3 %collective-permute-start = (f32[8,128,128]{2,1,0:T(8,128)S(1)}, f32[8,128,128]{2,1,0:T(8,128)S(1)}, u32[]{:S(2)}, u32[]{:S(2)}) collective-permute-start(f32[8,128,128]{2,1,0:T(8,128)S(1)} %pad_maximum_fusion), channel_id=1, source_target_pairs={{1,0},{2,1},{3,2},{4,3},{5,4},{6,5},{7,6},{8,7},{9,8},{10,9},{11,1... | collective-permute-start | bytes 1572872 | tf_op jit(solution)/shard_map/ppermute | solution.py:282
  7.9 0.8 %stack_reshape.6 = s32[1,64]{1,0:T(1,128)S(1)} reshape(s32[8,8]{1,0:T(8,128)} %rw.5) | data formatting | bytes 512 | tf_op jit(solution)/shard_map/stack;reshape | solution.py:303
  8.6 0.8 %stack_reshape.7 = s32[1,64]{1,0:T(1,128)S(1)} reshape(s32[8,8]{1,0:T(8,128)} %dw.5) | data formatting | bytes 512 | tf_op jit(solution)/shard_map/stack;reshape | solution.py:303
  9.4 0.0 copy-start
  9.4 3.4 %copy-done = f32[8,8,2,128,128]{4,3,2,1,0:T(8,128)S(1)} copy-done((f32[8,8,2,128,128]{4,3,2,1,0:T(8,128)S(1)}, f32[8,8,2,128,128]{4,3,2,1,0:T(8,128)}, u32[]{:S(2)}) %copy-start) | copy-done | bytes 8388632
  12.8 0.0 copy-start.2
  12.8 0.7 %copy-done.2 = s32[8,8]{1,0:T(8,128)S(1)} copy-done((s32[8,8]{1,0:T(8,128)S(1)}, s32[8,8]{1,0:T(8,128)}, u32[]{:S(2)}) %copy-start.2) | copy-done | bytes 280
  13.5 0.0 copy-start.4
  13.5 0.7 %copy-done.4 = s32[8,8]{1,0:T(8,128)S(1)} copy-done((s32[8,8]{1,0:T(8,128)S(1)}, s32[8,8]{1,0:T(8,128)}, u32[]{:S(2)}) %copy-start.4) | copy-done | bytes 280
  14.2 0.0 copy-start.6
  14.2 0.7 %copy-done.6 = s32[8,8]{1,0:T(8,128)S(1)} copy-done((s32[8,8]{1,0:T(8,128)S(1)}, s32[8,8]{1,0:T(8,128)}, u32[]{:S(2)}) %copy-start.6) | copy-done | bytes 280
  14.9 0.7 %copy-done.8 = s32[8,8]{1,0:T(8,128)S(1)} copy-done((s32[8,8]{1,0:T(8,128)S(1)}, s32[8,8]{1,0:T(8,128)}, u32[]{:S(2)}) %copy-start.8) | copy-done | bytes 280
  15.6 5.5 %inner.1.x_ref = f32[4,64,128]{2,1,0:T(8,128)S(1)} custom-call(s32[8,8]{1,0:T(8,128)S(1)} %copy-done.6, s32[8,8]{1,0:T(8,128)S(1)} %copy-done.2, s32[8,8]{1,0:T(8,128)S(1)} %copy-done.8, s32[8,8]{1,0:T(8,128)S(1)} %copy-done.4, f32[8,8,2,128,128]{4,3,2,1,0:T(8,128)S(1)} %copy-done), custom_call_target="tpu_custom_call" | custom-call | flops 20000000 | bytes 9000000 | tf_op jit(solution)/shard_map/inner/pallas_call | solution.py:288
  21.0 0.1 add_add_fusion.wide_ref
  21.1 0.0 collective-permute-done.1.south_ref
  21.1 1.0 %collective-permute-done.east_ref = f32[8,128,128]{2,1,0:T(8,128)S(1)} collective-permute-done((f32[8,128,128]{2,1,0:T(8,128)S(1)}, f32[8,128,128]{2,1,0:T(8,128)S(1)}, u32[]{:S(2)}, u32[]{:S(2)}) %collective-permute-start) | collective-permute-done | bytes 524320 | tf_op jit(solution)/shard_map/ppermute | solution.py:282
  22.1 1.6 %rim.1 = f32[2,128]{1,0:T(2,128)S(1)} custom-call(s32[8,8]{1,0:T(8,128)S(1)} %copy-done.6, s32[8,8]{1,0:T(8,128)S(1)} %copy-done.2, s32[8,8]{1,0:T(8,128)S(1)} %copy-done.8, s32[8,8]{1,0:T(8,128)S(1)} %copy-done.4, f32[4,64,128]{2,1,0:T(8,128)S(1)} %inner.1.x_ref, f32[8,8,2,128,128]{4,3,2,1,0:T(8,128)S(1)} %copy-done, f32[8,8,2,128,128]{4,3,2,1,0:T(8,128)S(1)} %copy-done, ...), custom_call_target="tpu_custom_call" | custom-call | flops 5000000 | bytes 3000000 | tf_op jit(solution)/shard_map/rim/pallas_call | solution.py:306
  23.7 0.7 %broadcast_in_dim.2 = f32[128,2,128]{2,1,0:T(2,128)} broadcast(f32[2,128]{1,0:T(2,128)S(1)} %rim.1), dimensions={1,2} | broadcast | bytes 132096 | tf_op jit(solution)/shard_map/broadcast_in_dim | solution.py:328
  24.4 12.5 %all-to-all-start = ((f32[128,2,128]{2,1,0:T(2,128)}), f32[128,2,128]{2,1,0:T(2,128)S(1)}, u32[]{:S(2)}, u32[]{:S(2)}) async-start(f32[128,2,128]{2,1,0:T(2,128)} %broadcast_in_dim.2), calls=%async_computation | async-start | bytes 262144 | tf_op jit(solution)/shard_map/all_to_all | solution.py:329
  36.9 0.1 pad_add_fusion.me
  36.9 10.1 %all-to-all-done = f32[128,2,128]{2,1,0:T(2,128)S(1)} async-done(((f32[128,2,128]{2,1,0:T(2,128)}), f32[128,2,128]{2,1,0:T(2,128)S(1)}, u32[]{:S(2)}, u32[]{:S(2)}) %all-to-all-start) | async-done | bytes 131104 | tf_op jit(solution)/shard_map/all_to_all | solution.py:329
  47.1 0.0 copy-done.3
  47.1 0.0 copy-done.5
  47.1 0.0 copy-done.7
  47.1 0.0 copy-done.9
  47.1 0.0 copy-start.1
  47.1 3.4 %copy-done.1 = f32[8,8,2,128,128]{4,3,2,1,0:T(8,128)S(1)} copy-done((f32[8,8,2,128,128]{4,3,2,1,0:T(8,128)S(1)}, f32[8,8,2,128,128]{4,3,2,1,0:T(8,128)}, u32[]{:S(2)}) %copy-start.1) | copy-done | bytes 8388632
  50.5 8.5 %blend.1 = (f32[8,8,2,128,128]{4,3,2,1,0:T(8,128)}, f32[2,8,8]{2,1,0:T(8,128)}) custom-call(s32[8,8]{1,0:T(8,128)S(1)} %copy-done.7, s32[8,8]{1,0:T(8,128)S(1)} %copy-done.3, s32[8,8]{1,0:T(8,128)S(1)} %copy-done.9, s32[8,8]{1,0:T(8,128)S(1)} %copy-done.5, s32[3]{0:T(128)S(1)} %pad_add_fusion.me, f32[256,128]{1,0:T(8,128)S(1)} %bitcast.14, ...), custom_call_target="tpu_custom_call" | custom-call | flops 30000000 | bytes 18000000 | tf_op jit(solution)/shard_map/blend/pallas_call | solution.py:332
  (5 shorter events, 0.0 us)
Async XLA Ops:
  1.7 19.4 %collective-permute-start.1 = (f32[8,2,64,128]{3,2,1,0:T(8,128)S(1)}, f32[8,2,64,128]{3,2,1,0:T(8,128)S(1)}, u32[]{:S(2)}, u32[]{:S(2)}) collective-permute-start(f32[8,2,64,128]{3,2,1,0:T(8,128)S(1)} %slice_bitcast_fusion), channel_id=1, source_target_pairs={{16,0},{32,16},{48,32},{64,48},{80,64},{96,80},{112,96},{17,1},{33... | collective-permute-start | bytes 1572872 | tf_op jit(solution)/shard_map/ppermute | solution.py:283
  6.6 15.5 %collective-permute-start = (f32[8,128,128]{2,1,0:T(8,128)S(1)}, f32[8,128,128]{2,1,0:T(8,128)S(1)}, u32[]{:S(2)}, u32[]{:S(2)}) collective-permute-start(f32[8,128,128]{2,1,0:T(8,128)S(1)} %pad_maximum_fusion), channel_id=1, source_target_pairs={{1,0},{2,1},{3,2},{4,3},{5,4},{6,5},{7,6},{8,7},{9,8},{10,9},{11,1... | collective-permute-start | bytes 1572872 | tf_op jit(solution)/shard_map/ppermute | solution.py:282
  9.4 3.4 %copy-start = (f32[8,8,2,128,128]{4,3,2,1,0:T(8,128)S(1)}, f32[8,8,2,128,128]{4,3,2,1,0:T(8,128)}, u32[]{:S(2)}) copy-start(f32[8,8,2,128,128]{4,3,2,1,0:T(8,128)} %p_ref.3) | copy-start | bytes 25165828
  12.8 0.7 %copy-start.2 = (s32[8,8]{1,0:T(8,128)S(1)}, s32[8,8]{1,0:T(8,128)}, u32[]{:S(2)}) copy-start(s32[8,8]{1,0:T(8,128)} %rw.5) | copy-start | bytes 772
  13.5 0.7 %copy-start.4 = (s32[8,8]{1,0:T(8,128)S(1)}, s32[8,8]{1,0:T(8,128)}, u32[]{:S(2)}) copy-start(s32[8,8]{1,0:T(8,128)} %dw.5) | copy-start | bytes 772
  14.2 0.7 %copy-start.6 = (s32[8,8]{1,0:T(8,128)S(1)}, s32[8,8]{1,0:T(8,128)}, u32[]{:S(2)}) copy-start(s32[8,8]{1,0:T(8,128)} %ro.5) | copy-start | bytes 772
  14.9 0.7 %copy-start.8 = (s32[8,8]{1,0:T(8,128)S(1)}, s32[8,8]{1,0:T(8,128)}, u32[]{:S(2)}) copy-start(s32[8,8]{1,0:T(8,128)} %do.5) | copy-start | bytes 772
  21.1 25.9 %copy-start.3 = (s32[8,8]{1,0:T(8,128)S(1)}, s32[8,8]{1,0:T(8,128)}, u32[]{:S(2)}) copy-start(s32[8,8]{1,0:T(8,128)} %rw.5) | copy-start | bytes 772
  21.1 25.9 %copy-start.5 = (s32[8,8]{1,0:T(8,128)S(1)}, s32[8,8]{1,0:T(8,128)}, u32[]{:S(2)}) copy-start(s32[8,8]{1,0:T(8,128)} %dw.5) | copy-start | bytes 772
  21.1 25.9 %copy-start.7 = (s32[8,8]{1,0:T(8,128)S(1)}, s32[8,8]{1,0:T(8,128)}, u32[]{:S(2)}) copy-start(s32[8,8]{1,0:T(8,128)} %ro.5) | copy-start | bytes 772
  21.1 25.9 %copy-start.9 = (s32[8,8]{1,0:T(8,128)S(1)}, s32[8,8]{1,0:T(8,128)}, u32[]{:S(2)}) copy-start(s32[8,8]{1,0:T(8,128)} %do.5) | copy-start | bytes 772
  24.4 22.7 %all-to-all-start = ((f32[128,2,128]{2,1,0:T(2,128)}), f32[128,2,128]{2,1,0:T(2,128)S(1)}, u32[]{:S(2)}, u32[]{:S(2)}) async-start(f32[128,2,128]{2,1,0:T(2,128)} %broadcast_in_dim.2), calls=%async_computation | async-start | bytes 262144 | tf_op jit(solution)/shard_map/all_to_all | solution.py:329
  47.1 3.4 %copy-start.1 = (f32[8,8,2,128,128]{4,3,2,1,0:T(8,128)S(1)}, f32[8,8,2,128,128]{4,3,2,1,0:T(8,128)}, u32[]{:S(2)}) copy-start(f32[8,8,2,128,128]{4,3,2,1,0:T(8,128)} %p_ref.3) | copy-start | bytes 25165828

commit v2 on v0

v2 whole, which is shorter than its diff:
```python
import functools

import jax
import jax.numpy as jnp
from jax import lax
from jax.experimental import pallas as pl
from jax.experimental.pallas import tpu as pltpu
from jax.sharding import PartitionSpec as P

ITERS = 2
EPS_NORM = 1.0
SIDE = 128
HALF = 64
ROW0 = 56
PAD = 8
N = 8
SUMS = 4 * N * N
HIGHEST = lax.Precision.HIGHEST


def lanes(shape):
    return lax.broadcasted_iota(jnp.int32, shape, len(shape) - 1)


def plane(i, j, part):
    return pl.multiple_of(((i * N + j) * 2 + part) * SIDE, SIDE)


def fold8(x):
    total = x[0:8]
    for k in range(8, x.shape[0], 8):
        total = total + x[k : k + 8]
    return total


def other_half(o):
    return jnp.where(o >= HALF, o - HALF, o + HALF)


def east_sums(load_a, load_b, offset, width):
    real, imag = jnp.zeros((8, SIDE), jnp.float32), jnp.zeros((8, SIDE), jnp.float32)
    for k in range(0, SIDE, 32):
        ar, ai, br, bi = load_a(0, k), load_a(1, k), load_b(0, k), load_b(1, k)
        real = real + fold8(ar * br + ai * bi)
        imag = imag + fold8(ar * bi - ai * br)
    lane = lanes((8, SIDE))
    keep = (lane >= offset) & (lane < offset + width)
    return jnp.where(keep, real, 0.0), jnp.where(keep, imag, 0.0)


def south_sums(load_a, load_b, offset, width):
    row = lax.broadcasted_iota(jnp.int32, (8, SIDE), 0)
    real, imag = jnp.zeros((8, SIDE), jnp.float32), jnp.zeros((8, SIDE), jnp.float32)
    for first in range(ROW0, SIDE, 8):
        at = row + first
        keep = (at >= offset) & (at < offset + width)
        start = jnp.maximum(first - offset, -PAD)
        ar, ai, br, bi = load_a(0, first), load_a(1, first), load_b(0, start), load_b(1, start)
        real = real + jnp.where(keep, ar * br + ai * bi, 0.0)
        imag = imag + jnp.where(keep, ar * bi - ai * br, 0.0)
    return real, imag


def fetch_row(p_hbm, p_ref, sems, i):
    block = 2 * N * SIDE
    at = pl.multiple_of(i * block, block)
    return pltpu.make_async_copy(p_hbm.at[pl.ds(at, block), :], p_ref.at[pl.ds(at, block), :], sems.at[i])


def strip_kernel(p_hbm, east_ref, south_ref, col, sems):
    copies = [pltpu.make_async_copy(p_hbm.at[:, 0], col, sems.at[0])]
    copies[0].start()
    for j in range(N):
        for part in range(2):
            at = PAD + (j * 2 + part) * HALF
            copy = pltpu.make_async_copy(
                p_hbm.at[0, j, part, 0:HALF, :], south_ref.at[at : at + HALF, :], sems.at[1 + j * 2 + part]
            )
            copy.start()
            copies.append(copy)
    edge = jnp.zeros((PAD, SIDE), jnp.float32)
    south_ref[0:PAD, :] = edge
    south_ref[PAD + 2 * N * HALF :, :] = edge
    copies[0].wait()
    low = lanes((SIDE, SIDE)) < HALF
    for i in range(N):
        east_ref[i * SIDE : (i + 1) * SIDE, :] = jnp.where(low, col[i, 0], pltpu.roll(col[i, 1], HALF, 1))
    for copy in copies[1:]:
        copy.wait()


def inner_kernel(ro_hbm, rw_hbm, do_hbm, dw_hbm, p_hbm, x_ref, p_ref, ro, rw, do, dw, sems):
    pairs = ((ro_hbm, ro), (rw_hbm, rw), (do_hbm, do), (dw_hbm, dw))
    tables = [pltpu.make_async_copy(a, b, sems.at[N + k]) for k, (a, b) in enumerate(pairs)]
    for copy in tables:
        copy.start()
    for k in range(N):
        fetch_row(p_hbm, p_ref, sems, N - 1 - k).start()
    for copy in tables:
        copy.wait()

    def put(quantity, i, j, value):
        x_ref[pl.ds(quantity * N * N + i * N + j, 8, SUMS), :] = value

    def row_of_patches(step, carry):
        i = N - 1 - step
        fetch_row(p_hbm, p_ref, sems, i).wait()
        for j in range(N - 1):
            o, w = ro[i, j], rw[i, j]
            sums = east_sums(
                lambda part, k: p_ref[pl.ds(plane(i, j, part) + k, 32), :],
                lambda part, k: pltpu.roll(p_ref[pl.ds(plane(i, j + 1, part) + k, 32), :], o, 1),
                o,
                w,
            )
            put(0, i, j, sums[0])
            put(1, i, j, sums[1])

        @pl.when(step > 0)
        def _():
            for j in range(N):
                sums = south_sums(
                    lambda part, k: p_ref[pl.ds(plane(i, j, part) + k, 8), :],
                    lambda part, k: p_ref[pl.ds(plane(i + 1, j, part) + k, 8), :],
                    do[i, j],
                    dw[i, j],
                )
                put(2, i, j, sums[0])
                put(3, i, j, sums[1])

        return carry

    lax.fori_loop(0, N, row_of_patches, 0)


def rim_kernel(ro, rw, do, dw, x_ref, p_ref, east_ref, south_ref, rw_ref, dw_ref, out_ref, all_ref):
    total = x_ref[0:SUMS, :]
    for k in range(1, 8):
        total = total + x_ref[k * SUMS : (k + 1) * SUMS, :]
    all_ref[...] = total

    def put(quantity, i, j, value):
        at = quantity * N * N + i * N + j
        all_ref[at : at + 1, :] = jnp.sum(value, axis=0, keepdims=True)

    for i in range(N):
        o, w = ro[i, N - 1], rw[i, N - 1]
        turn = (o, other_half(o))
        sums = east_sums(
            lambda part, k: p_ref[pl.ds(plane(i, N - 1, part) + k, 32), :],
            lambda part, k: pltpu.roll(east_ref[i * SIDE + k : i * SIDE + k + 32, :], turn[part], 1),
            o,
            w,
        )
        put(0, i, N - 1, sums[0])
        put(1, i, N - 1, sums[1])
    for j in range(N):
        sums = south_sums(
            lambda part, k: p_ref[pl.ds(plane(N - 1, j, part) + k, 8), :],
            lambda part, k: south_ref[pl.ds(PAD + (j * 2 + part) * HALF + k, 8), :],
            do[N - 1, j],
            dw[N - 1, j],
        )
        put(2, N - 1, j, sums[0])
        put(3, N - 1, j, sums[1])
    ones = jnp.ones((8, SIDE), jnp.float32)
    sums = lax.dot_general(
        ones, all_ref[...], (((1,), (1,)), ((), ())), precision=HIGHEST, preferred_element_type=jnp.float32
    )

    def scaled(x, width_ref):
        width = width_ref[...].astype(jnp.float32)
        factor = 1.0 / jnp.sqrt(SIDE * width)
        return x * jnp.concatenate([factor[k : k + 1, :] for k in range(N)] * 2, axis=1)

    east = scaled(sums[0:1, 0:SIDE], rw_ref)
    south = scaled(sums[0:1, SIDE : 2 * SIDE], dw_ref)
    odd = lax.broadcasted_iota(jnp.int32, out_ref.shape, 0) % 2 == 1
    out_ref[...] = jnp.where(odd, south, east)


def sync_phases(east, south, n_cols, count):
    lane = lanes(east.shape)
    low = lane < HALF
    col, row = lane % 8, (lane // 8) % 8

    def lane_roll(x, by):
        return pltpu.roll(x, by % SIDE, 1)

    def dev_roll(x, by):
        return pltpu.roll(x, by % x.shape[0], 0)

    def to_east(x):
        return jnp.where(col < 7, lane_roll(x, -1), lane_roll(dev_roll(x, -1), 7))

    def to_west(x):
        return jnp.where(col > 0, lane_roll(x, 1), lane_roll(dev_roll(x, 1), -7))

    def to_south(x):
        return jnp.where(row < 7, lane_roll(x, -8), lane_roll(dev_roll(x, -n_cols), 56))

    def to_north(x):
        return jnp.where(row > 0, lane_roll(x, 8), lane_roll(dev_roll(x, n_cols), -56))

    def swap(x):
        return lane_roll(x, HALF)

    def split(x):
        other = swap(x)
        imag = jnp.where(low, other, x)
        return jnp.where(low, x, other), jnp.where(low, -imag, imag)

    east_r, east_i = split(east)
    south_r, south_i = split(south)
    phase = None
    for step in range(ITERS):
        if step == 0:
            image = east + south
            image = image + to_west(jnp.where(low, east, -east))
            image = image + to_north(jnp.where(low, south, -south))
        else:
            beside, below, other = to_east(phase), to_south(phase), swap(phase)
            image = east_r * beside + east_i * swap(beside)
            image = image + south_r * below + south_i * swap(below)
            image = image + to_west(east_r * phase - east_i * other)
            image = image + to_north(south_r * phase - south_i * other)
        total = jnp.sum(jnp.sum(image * image, axis=0, keepdims=True), axis=1, keepdims=True)
        phase = image / jnp.sqrt(total / count + EPS_NORM)
    return phase


def blend_kernel(
    n_cols, ro, rw, do, dw, me, g_ref, p_hbm, east_ref, south_ref, out_hbm, phase_ref,
    p_ref, stage, all_ref, near_ref, fac, sem, out_sem, sems,
):
    for i in range(N):
        fetch_row(p_hbm, p_ref, sems, i).start()
    n_dev = all_ref.shape[0]
    all_ref[...] = sync_phases(
        g_ref[pl.ds(0, n_dev, 2), :], g_ref[pl.ds(1, n_dev, 2), :], n_cols, n_dev * N * N
    )
    d = me[0]
    lane = lanes((1, SIDE))
    own = all_ref[pl.ds(d, 1), :]
    right = all_ref[pl.ds(lax.rem(d + 1, n_dev), 1), :]
    lower = all_ref[pl.ds(lax.rem(d + n_cols, n_dev), 1), :]
    near_ref[0:1, :] = own
    near_ref[1:2, :] = jnp.where(lane % 8 < 7, pltpu.roll(own, SIDE - 1, 1), pltpu.roll(right, 7, 1))
    near_ref[2:3, :] = jnp.where(
        (lane // 8) % 8 < 7, pltpu.roll(own, SIDE - 8, 1), pltpu.roll(lower, 56, 1)
    )
    copy = pltpu.make_async_copy(near_ref, fac, sem)
    copy.start()
    for part in range(2):
        for k in range(N):
            at = part * HALF + k * N
            phase_ref[part, k : k + 1, :] = own[:, at : at + N]
    copy.wait()

    lane = lanes((8, SIDE))
    row = lax.broadcasted_iota(jnp.int32, (8, SIDE), 0)

    def row_of_patches(i, last):
        for j in range(N):
            o, w = ro[i, j], rw[i, j]
            if j == N - 1:
                w = jnp.where(me[1] > 0, w, 0)
            keep = (lane >= o) & (lane < o + w)
            down = do[i, j]
            deep = jnp.where(me[2] > 0, dw[i, j], 0) if last else dw[i, j]
            at = i * N + j
            inv = jnp.where(keep, 0.5, 1.0)
            inv_south = jnp.where(keep, 1.0 / 3.0, 0.5)
            ratio = jnp.where(keep, 2.0 / 3.0, 0.5)
            gr, gi = fac[0, at] * inv, fac[0, HALF + at] * inv
            er = jnp.where(keep, fac[1, at] * 0.5, 0.0)
            ei = jnp.where(keep, fac[1, HALF + at] * 0.5, 0.0)
            sr, si = fac[2, at] * inv_south, fac[2, HALF + at] * inv_south
            turn = (o, other_half(o))
            for first in range(0, SIDE, 8):
                ar, ai = (p_ref[pl.ds(plane(i, j, part) + first, 8), :] for part in range(2))
                if j < N - 1:
                    br, bi = (
                        pltpu.roll(p_ref[pl.ds(plane(i, j + 1, part) + first, 8), :], o, 1) for part in range(2)
                    )
                else:
                    both = east_ref[pl.ds(pl.multiple_of(i * SIDE, SIDE) + first, 8), :]
                    br, bi = (pltpu.roll(both, turn[part], 1) for part in range(2))
                real = (gr * ar - gi * ai) + (er * br - ei * bi)
                imag = (gr * ai + gi * ar) + (er * bi + ei * br)
                if first >= ROW0:
                    here = row + first
                    inside = (here >= down) & (here < down + deep)
                    start = jnp.maximum(first - down, -PAD)
                    if last:
                        cr, ci = (south_ref[pl.ds(PAD + (j * 2 + part) * HALF + start, 8), :] for part in range(2))
                    else:
                        cr, ci = (p_ref[pl.ds(plane(i + 1, j, part) + start, 8), :] for part in range(2))
                    real = jnp.where(inside, real * ratio + (sr * cr - si * ci), real)
                    imag = jnp.where(inside, imag * ratio + (sr * ci + si * cr), imag)
                stage[pl.ds(plane(i, j, 0) + first, 8), :] = real
                stage[pl.ds(plane(i, j, 1) + first, 8), :] = imag
            begin = plane(i, j, 0)
            pltpu.make_async_copy(
                stage.at[pl.ds(begin, 2 * SIDE), :], out_hbm.at[pl.ds(begin, 2 * SIDE), :], out_sem
            ).start()

    fetch_row(p_hbm, p_ref, sems, 0).wait()

    def body(i, carry):
        fetch_row(p_hbm, p_ref, sems, i + 1).wait()
        row_of_patches(i, False)
        return carry

    lax.fori_loop(0, N - 1, body, 0)
    row_of_patches(N - 1, True)
    pltpu.make_async_copy(stage, out_hbm, out_sem).wait()


def local(patches, right_offset, right_width, down_offset, down_width):
    n_rows, n_cols = lax.axis_size("row"), lax.axis_size("col")
    n_dev = n_rows * n_cols
    r, c = lax.axis_index("row"), lax.axis_index("col")
    tables = (right_offset, right_width, down_offset, down_width)
    flat_shape = (N * N * 2 * SIDE, SIDE)
    flat = pltpu.with_memory_space_constraint(patches.reshape(flat_shape), pltpu.HBM)
    south_shape = (2 * PAD + N * 2 * HALF, SIDE)
    vmem, smem = pl.BlockSpec(memory_space=pltpu.VMEM), pl.BlockSpec(memory_space=pltpu.SMEM)
    hbm = pl.BlockSpec(memory_space=pltpu.HBM)
    f32 = lambda *shape: jax.ShapeDtypeStruct(shape, jnp.float32)

    def params(mib):
        return pltpu.CompilerParams(vmem_limit_bytes=mib * 2**20)

    def cost(flops, moved):
        return pl.CostEstimate(flops=flops, bytes_accessed=moved, transcendentals=0)

    strip, lower = pl.pallas_call(
        strip_kernel,
        out_shape=(f32(N * SIDE, SIDE), f32(*south_shape)),
        in_specs=[hbm],
        out_specs=(vmem, vmem),
        scratch_shapes=[pltpu.VMEM((N, 2, SIDE, SIDE), jnp.float32), pltpu.SemaphoreType.DMA((1 + 2 * N,))],
        compiler_params=params(8),
        cost_estimate=cost(400_000, 3_000_000),
        name="strips",
    )(pltpu.with_memory_space_constraint(patches, pltpu.HBM))
    east_edge = lax.ppermute(strip, "col", [(k + 1, k) for k in range(n_cols - 1)])
    south_edge = lax.ppermute(lower, "row", [(k + 1, k) for k in range(n_rows - 1)])

    sums, held = pl.pallas_call(
        inner_kernel,
        out_shape=(f32(8 * SUMS, SIDE), f32(*flat_shape)),
        in_specs=[hbm] * 5,
        out_specs=(vmem, vmem),
        scratch_shapes=[pltpu.SMEM((N, N), jnp.int32)] * 4 + [pltpu.SemaphoreType.DMA((N + 4,))],
        compiler_params=params(16),
        cost_estimate=cost(20_000_000, 9_000_000),
        name="inner",
    )(*tables, flat)

    sent = pl.pallas_call(
        rim_kernel,
        out_shape=f32(2 * n_dev, SIDE),
        in_specs=[smem] * 4 + [vmem] * 6,
        out_specs=vmem,
        scratch_shapes=[pltpu.VMEM((SUMS, SIDE), jnp.float32)],
        compiler_params=params(16),
        cost_estimate=cost(5_000_000, 3_000_000),
        name="rim",
    )(*tables, sums, held, east_edge, south_edge, right_width, down_width)
    grid = lax.all_to_all(sent, ("row", "col"), 0, 0, tiled=True)

    me = jnp.stack([r * n_cols + c, (c < n_cols - 1).astype(jnp.int32), (r < n_rows - 1).astype(jnp.int32)])
    blended, phases = pl.pallas_call(
        functools.partial(blend_kernel, n_cols),
        out_shape=(f32(*flat_shape), f32(2, N, N)),
        in_specs=[smem] * 5 + [vmem, hbm, vmem, vmem],
        out_specs=(hbm, vmem),
        scratch_shapes=[
            pltpu.VMEM(flat_shape, jnp.float32),
            pltpu.VMEM(flat_shape, jnp.float32),
            pltpu.VMEM((n_dev, SIDE), jnp.float32),
            pltpu.VMEM((8, SIDE), jnp.float32),
            pltpu.SMEM((8, SIDE), jnp.float32),
            pltpu.SemaphoreType.DMA,
            pltpu.SemaphoreType.DMA,
            pltpu.SemaphoreType.DMA((N,)),
        ],
        compiler_params=params(32),
        cost_estimate=cost(30_000_000, 10_000_000),
        name="blend",
    )(*tables, me, grid, flat, east_edge, south_edge)
    return blended.reshape(patches.shape), phases


def solution(mesh):
    return jax.shard_map(
        local,
        mesh=mesh,
        in_specs=(P("row", "col", None, None, None), *(P("row", "col"),) * 4),
        out_specs=(P("row", "col", None, None, None), P(None, "row", "col")),
        check_vma=False,
    )
```

time: 292 us -> 55.2 us (0.19)
  blocking collectives: 135 us -> 0 us
  other arithmetic: 45.7 us -> 0.08 us
  matrix products: 37 us -> 0 us
  starting transfers between devices: 40.3 us -> 17.1 us
  local copies, waits for them, and re-layouts: 22.6 us -> 0.02 us
  Pallas kernels: 0 us -> 17.9 us
  waiting for transfers between devices: 6.16 us -> 19.1 us
    psum x2 -> x0, blocking collectives: 135 us -> none  [scale_each(): total = lax.psum(jnp.sum(interior * interior), ('row', 'col'))]
    dot_general x4 -> x0, matrix products: 37 us -> none  [the longest x1 12.5 us: local(): jnp.einsum('pqab,pqkac->pqkbc', south_select, patches, precision=highest)]
    ppermute x15 -> x2, starting transfers between devices: 40.3 us -> 4.62 us  [the longest x1 3.33 us: local(): lax.ppermute(lower, 'row', [(k + 1, k) for k in range(n_rows - 1)])]
    pallas_call x0 -> x4, Pallas kernels: none -> 17.9 us  [the longest x1 8.85 us: local(): pl.pallas_call(functools.partial(blend_kernel, n_cols), out_shape=(f32(*f...]
    reduce_sum x4 -> x0, other arithmetic: 15 us -> none  [the longest x1 8.53 us: correlate(): jnp.sum(shifted[..., 0, :, :] * partner[..., 1, :, :] - shifted[..., 1, :...]
    sub x5 -> x0, other arithmetic: 12.6 us -> none  [the longest x3 12.6 us: rotate(): factor[..., 0:1, :, :] * field[..., 0:1, :, :]]
    all_to_all x0 -> x1, starting transfers between devices: none -> 12.5 us  [local(): grid = lax.all_to_all(sent, ('row', 'col'), 0, 0, tiled=True)]
    unnamed x52 -> x8, local copies, waits for them, and re-layouts: 11.7 us -> 0.02 us
  transfers between devices with their start and end apart: 15 -> 3, of which waited for: 3 -> 2; matrix products, arithmetic and copies ran while one was open for 29% -> 0% of each run, Pallas kernels for 0% -> 9%
where the time goes in v2:
time: 55.2 us; the launch traced here: 55 us
  waiting for transfers between devices  19.1 us (35%)
  Pallas kernels  17.9 us (32%)
  starting transfers between devices  17.1 us (31%)
  between operations  0.75 us (1%)
    all_to_all x1, starting transfers between devices, local(): grid = lax.all_to_all(sent, ('row', 'col'), 0, 0, tiled=True)  12.5 us
    all_to_all x1, waiting for transfers between devices, local(): grid = lax.all_to_all(sent, ('row', 'col'), 0, 0, tiled=True)  10.1 us
    ppermute x1, waiting for transfers between devices, local(): lax.ppermute(strip, 'col', [(k + 1, k) for k in range(n_cols - 1)])  9 us
    pallas_call x1, Pallas kernels, local(): pl.pallas_call(functools.partial(blend_kernel, n_cols), out_shape=(f32(*f...  8.85 us
    pallas_call x1, Pallas kernels, local(): pl.pallas_call(inner_kernel, out_shape=(f32(8 * SUMS, SIDE), f32(*flat_sh...  5.18 us
    ppermute x1, starting transfers between devices, local(): lax.ppermute(lower, 'row', [(k + 1, k) for k in range(n_rows - 1)])  3.33 us
    pallas_call x1, Pallas kernels, local(): pl.pallas_call(rim_kernel, out_shape=f32(2 * n_dev, SIDE), in_specs=[smem...  2.29 us
    pallas_call x1, Pallas kernels, local(): pl.pallas_call(strip_kernel, out_shape=(f32(N * SIDE, SIDE), f32(*south_s...  1.63 us
  transfers between devices with their start and end apart: 3, of which 2 were waited for; matrix products, arithmetic and copies ran while one was open for 0% of the time, Pallas kernels for 9%

profile of v2, /device:TPU:1, one launch (start us, length us, event | category | flops | bytes accessed | tf_op | source)
XLA Modules:
  0.0 55.0 jit_solution(10610592650852579751)
XLA Ops:
  0.6 0.0 copy-start.1
  0.6 0.0 copy-start.3
  0.7 0.0 copy-start
  0.7 0.0 copy-start.2
  0.7 1.6 %strips.1 = (f32[1024,128]{1,0:T(8,128)S(1)}, f32[1040,128]{1,0:T(8,128)S(1)}) custom-call(f32[8,8,2,128,128]{4,3,2,1,0:T(8,128)} %p_hbm.1), custom_call_target="tpu_custom_call" | custom-call | flops 400000 | bytes 3000000 | tf_op jit(solution)/shard_map/strips/pallas_call | solution.py:338
  2.3 3.3 %collective-permute-start.1 = (f32[1040,128]{1,0:T(8,128)S(1)}, f32[1040,128]{1,0:T(8,128)S(1)}, u32[]{:S(2)}, u32[]{:S(2)}) collective-permute-start(f32[1040,128]{1,0:T(8,128)S(1)} %get-tuple-element.11), channel_id=1, source_target_pairs={{16,0},{32,16},{48,32},{64,48},{80,64},{96,80},{112,96},{17,1},{33... | collective-permute-start | bytes 1597448 | tf_op jit(solution)/shard_map/ppermute | solution.py:349
  5.6 1.3 %collective-permute-start = (f32[1024,128]{1,0:T(8,128)S(1)}, f32[1024,128]{1,0:T(8,128)S(1)}, u32[]{:S(2)}, u32[]{:S(2)}) collective-permute-start(f32[1024,128]{1,0:T(8,128)S(1)} %get-tuple-element.10), channel_id=1, source_target_pairs={{1,0},{2,1},{3,2},{4,3},{5,4},{6,5},{7,6},{8,7},{9,8},{10,9},{11,1... | collective-permute-start | bytes 1572872 | tf_op jit(solution)/shard_map/ppermute | solution.py:348
  6.9 0.0 copy-done.1
  7.0 0.0 copy-done.3
  7.0 0.0 copy-done
  7.0 0.0 copy-done.2
  7.0 5.2 %inner.1 = (f32[2048,128]{1,0:T(8,128)S(1)}, f32[16384,128]{1,0:T(8,128)S(1)}) custom-call(s32[8,8]{1,0:T(8,128)S(1)} %copy-done.2, s32[8,8]{1,0:T(8,128)S(1)} %copy-done, s32[8,8]{1,0:T(8,128)S(1)} %copy-done.3, s32[8,8]{1,0:T(8,128)S(1)} %copy-done.1, f32[16384,128]{1,0:T(8,128)} %bitcast.8), custom_call_target="tpu_custom_call" | custom-call | flops 20000000 | bytes 9000000 | tf_op jit(solution)/shard_map/inner/pallas_call | solution.py:351
  12.2 9.0 %collective-permute-done.east_ref = f32[1024,128]{1,0:T(8,128)S(1)} collective-permute-done((f32[1024,128]{1,0:T(8,128)S(1)}, f32[1024,128]{1,0:T(8,128)S(1)}, u32[]{:S(2)}, u32[]{:S(2)}) %collective-permute-start) | collective-permute-done | bytes 524320 | tf_op jit(solution)/shard_map/ppermute | solution.py:348
  21.2 0.0 collective-permute-done.1.south_ref
  21.2 2.3 %rim.1 = f32[256,128]{1,0:T(8,128)} custom-call(s32[8,8]{1,0:T(8,128)S(1)} %copy-done.2, s32[8,8]{1,0:T(8,128)S(1)} %copy-done, s32[8,8]{1,0:T(8,128)S(1)} %copy-done.3, s32[8,8]{1,0:T(8,128)S(1)} %copy-done.1, f32[2048,128]{1,0:T(8,128)S(1)} %get-tuple-element.8.x_ref, f32[16384,128]{1,0:T(8,128)S(1)} %get-tuple-element.9.p_ref, ...), custom_call_target="tpu_custom_call" | custom-call | flops 5000000 | bytes 3000000 | tf_op jit(solution)/shard_map/rim/pallas_call | solution.py:362
  23.5 12.5 %all-to-all-start = ((f32[128,2,128]{2,1,0:T(2,128)}), f32[128,2,128]{2,1,0:T(2,128)S(1)}, u32[]{:S(2)}, u32[]{:S(2)}) async-start(f32[128,2,128]{2,1,0:T(2,128)} %bitcast.4), calls=%async_computation | async-start | bytes 262144 | tf_op jit(solution)/shard_map/all_to_all | solution.py:372
  35.9 0.1 pad_add_fusion.me
  36.0 10.1 %all-to-all-done = f32[128,2,128]{2,1,0:T(2,128)S(1)} async-done(((f32[128,2,128]{2,1,0:T(2,128)}), f32[128,2,128]{2,1,0:T(2,128)S(1)}, u32[]{:S(2)}, u32[]{:S(2)}) %all-to-all-start) | async-done | bytes 131104 | tf_op jit(solution)/shard_map/all_to_all | solution.py:372
  46.1 8.9 %blend.1 = (f32[16384,128]{1,0:T(8,128)}, f32[2,8,8]{2,1,0:T(8,128)}) custom-call(s32[8,8]{1,0:T(8,128)S(1)} %copy-done.2, s32[8,8]{1,0:T(8,128)S(1)} %copy-done, s32[8,8]{1,0:T(8,128)S(1)} %copy-done.3, s32[8,8]{1,0:T(8,128)S(1)} %copy-done.1, s32[3]{0:T(128)S(1)} %pad_add_fusion.me, f32[256,128]{1,0:T(8,128)S(1)} %bitcast.7, f32[16384,128]{1,0:T(8,128)} %bitcast.9, ...), custom_call_target="tpu_custom_call" | custom-call | flops 30000000 | bytes 10000000 | tf_op jit(solution)/shard_map/blend/pallas_call | solution.py:375
Async XLA Ops:
  0.6 6.3 %copy-start.1 = (s32[8,8]{1,0:T(8,128)S(1)}, s32[8,8]{1,0:T(8,128)}, u32[]{:S(2)}) copy-start(s32[8,8]{1,0:T(8,128)} %dw.3) | copy-start | bytes 772
  0.6 6.3 %copy-start.3 = (s32[8,8]{1,0:T(8,128)S(1)}, s32[8,8]{1,0:T(8,128)}, u32[]{:S(2)}) copy-start(s32[8,8]{1,0:T(8,128)} %do.3) | copy-start | bytes 772
  0.7 6.3 %copy-start = (s32[8,8]{1,0:T(8,128)S(1)}, s32[8,8]{1,0:T(8,128)}, u32[]{:S(2)}) copy-start(s32[8,8]{1,0:T(8,128)} %rw.3) | copy-start | bytes 772
  0.7 6.3 %copy-start.2 = (s32[8,8]{1,0:T(8,128)S(1)}, s32[8,8]{1,0:T(8,128)}, u32[]{:S(2)}) copy-start(s32[8,8]{1,0:T(8,128)} %ro.3) | copy-start | bytes 772
  2.3 18.9 %collective-permute-start.1 = (f32[1040,128]{1,0:T(8,128)S(1)}, f32[1040,128]{1,0:T(8,128)S(1)}, u32[]{:S(2)}, u32[]{:S(2)}) collective-permute-start(f32[1040,128]{1,0:T(8,128)S(1)} %get-tuple-element.11), channel_id=1, source_target_pairs={{16,0},{32,16},{48,32},{64,48},{80,64},{96,80},{112,96},{17,1},{33... | collective-permute-start | bytes 1597448 | tf_op jit(solution)/shard_map/ppermute | solution.py:349
  5.6 15.5 %collective-permute-start = (f32[1024,128]{1,0:T(8,128)S(1)}, f32[1024,128]{1,0:T(8,128)S(1)}, u32[]{:S(2)}, u32[]{:S(2)}) collective-permute-start(f32[1024,128]{1,0:T(8,128)S(1)} %get-tuple-element.10), channel_id=1, source_target_pairs={{1,0},{2,1},{3,2},{4,3},{5,4},{6,5},{7,6},{8,7},{9,8},{10,9},{11,1... | collective-permute-start | bytes 1572872 | tf_op jit(solution)/shard_map/ppermute | solution.py:348
  23.5 22.7 %all-to-all-start = ((f32[128,2,128]{2,1,0:T(2,128)}), f32[128,2,128]{2,1,0:T(2,128)S(1)}, u32[]{:S(2)}, u32[]{:S(2)}) async-start(f32[128,2,128]{2,1,0:T(2,128)} %bitcast.4), calls=%async_computation | async-start | bytes 262144 | tf_op jit(solution)/shard_map/all_to_all | solution.py:372

commit v3 on v2

--- a/solution.py
+++ b/solution.py
@@ -31,6 +31,10 @@
     for k in range(8, x.shape[0], 8):
         total = total + x[k : k + 8]
     return total
+
+
+def west_slots(lane):
+    return (lane % N == N - 1) & ((lane // N) % N >= N // 2)
 
 
 def other_half(o):
@@ -67,25 +71,52 @@
     return pltpu.make_async_copy(p_hbm.at[pl.ds(at, block), :], p_ref.at[pl.ds(at, block), :], sems.at[i])
 
 
-def strip_kernel(p_hbm, east_ref, south_ref, col, sems):
-    copies = [pltpu.make_async_copy(p_hbm.at[:, 0], col, sems.at[0])]
-    copies[0].start()
+def strip_kernel(ro_hbm, rw_hbm, p_hbm, left_ref, right_ref, late_ref, south_ref, first, last, ro, rw, sems):
+    half = N // 2
+    copies = [
+        pltpu.make_async_copy(ro_hbm, ro, sems.at[0]),
+        pltpu.make_async_copy(rw_hbm, rw, sems.at[1]),
+        pltpu.make_async_copy(p_hbm.at[0:half, 0], first.at[0:half], sems.at[2]),
+        pltpu.make_async_copy(p_hbm.at[half:N, N - 1], last, sems.at[3]),
+        pltpu.make_async_copy(p_hbm.at[half:N, 0], first.at[half:N], sems.at[4]),
+    ]
+    for copy in copies:
+        copy.start()
+    rows = []
     for j in range(N):
         for part in range(2):
             at = PAD + (j * 2 + part) * HALF
             copy = pltpu.make_async_copy(
-                p_hbm.at[0, j, part, 0:HALF, :], south_ref.at[at : at + HALF, :], sems.at[1 + j * 2 + part]
+                p_hbm.at[0, j, part, 0:HALF, :], south_ref.at[at : at + HALF, :], sems.at[5 + j * 2 + part]
             )
             copy.start()
-            copies.append(copy)
+            rows.append(copy)
     edge = jnp.zeros((PAD, SIDE), jnp.float32)
     south_ref[0:PAD, :] = edge
     south_ref[PAD + 2 * N * HALF :, :] = edge
+    lane = lanes((SIDE, SIDE))
+    low = lane < HALF
+
+    def pack(i):
+        return jnp.where(low, first[i, 0], pltpu.roll(first[i, 1], HALF, 1))
+
+    copies[2].wait()
+    for i in range(half):
+        left_ref[i * SIDE : (i + 1) * SIDE, :] = pack(i)
     copies[0].wait()
-    low = lanes((SIDE, SIDE)) < HALF
-    for i in range(N):
-        east_ref[i * SIDE : (i + 1) * SIDE, :] = jnp.where(low, col[i, 0], pltpu.roll(col[i, 1], HALF, 1))
-    for copy in copies[1:]:
+    copies[1].wait()
+    copies[3].wait()
+    for i in range(half):
+        o, w = ro[half + i, N - 1], rw[half + i, N - 1]
+        scale = 1.0 / jnp.sqrt(SIDE * jnp.full((1, SIDE), w).astype(jnp.float32))
+        real = pltpu.roll(last[i, 0], SIDE - o, 1)
+        imag = pltpu.roll(last[i, 1], other_half(SIDE - o), 1)
+        both = jnp.where(low, real, imag) * scale
+        right_ref[i * SIDE : (i + 1) * SIDE, :] = jnp.where(lane % HALF < w, both, 0.0)
+    copies[4].wait()
+    for i in range(half):
+        late_ref[i * SIDE : (i + 1) * SIDE, :] = pack(half + i)
+    for copy in rows:
         copy.wait()
 
 
@@ -133,7 +164,7 @@
     lax.fori_loop(0, N, row_of_patches, 0)
 
 
-def rim_kernel(ro, rw, do, dw, x_ref, p_ref, east_ref, south_ref, rw_ref, dw_ref, out_ref, all_ref):
+def rim_kernel(ro, rw, do, dw, x_ref, p_ref, east_ref, west_ref, late_ref, south_ref, rw_ref, dw_ref, out_ref, all_ref):
     total = x_ref[0:SUMS, :]
     for k in range(1, 8):
         total = total + x_ref[k * SUMS : (k + 1) * SUMS, :]
@@ -143,7 +174,9 @@
         at = quantity * N * N + i * N + j
         all_ref[at : at + 1, :] = jnp.sum(value, axis=0, keepdims=True)
 
-    for i in range(N):
+    half = N // 2
+    low = lanes((32, SIDE)) < HALF
+    for i in range(half):
         o, w = ro[i, N - 1], rw[i, N - 1]
         turn = (o, other_half(o))
         sums = east_sums(
@@ -154,6 +187,15 @@
         )
         put(0, i, N - 1, sums[0])
         put(1, i, N - 1, sums[1])
+    for i in range(half):
+        real, imag = jnp.zeros((8, SIDE), jnp.float32), jnp.zeros((8, SIDE), jnp.float32)
+        for k in range(i * SIDE, (i + 1) * SIDE, 32):
+            a, b = west_ref[k : k + 32, :], late_ref[k : k + 32, :]
+            cross = a * pltpu.roll(b, HALF, 1)
+            real = real + fold8(a * b)
+            imag = imag + fold8(jnp.where(low, cross, -cross))
+        put(0, half + i, N - 1, real)
+        put(1, half + i, N - 1, imag)
     for j in range(N):
         sums = south_sums(
             lambda part, k: p_ref[pl.ds(plane(N - 1, j, part) + k, 8), :],
@@ -168,13 +210,14 @@
         ones, all_ref[...], (((1,), (1,)), ((), ())), precision=HIGHEST, preferred_element_type=jnp.float32
     )
 
-    def scaled(x, width_ref):
+    def scale_of(width_ref):
         width = width_ref[...].astype(jnp.float32)
         factor = 1.0 / jnp.sqrt(SIDE * width)
-        return x * jnp.concatenate([factor[k : k + 1, :] for k in range(N)] * 2, axis=1)
-
-    east = scaled(sums[0:1, 0:SIDE], rw_ref)
-    south = scaled(sums[0:1, SIDE : 2 * SIDE], dw_ref)
+        return jnp.concatenate([factor[k : k + 1, :] for k in range(N)] * 2, axis=1)
+
+    foreign = west_slots(lanes((1, SIDE)))
+    east = sums[0:1, 0:SIDE] * jnp.where(foreign, 1.0, scale_of(rw_ref))
+    south = sums[0:1, SIDE : 2 * SIDE] * scale_of(dw_ref)
     odd = lax.broadcasted_iota(jnp.int32, out_ref.shape, 0) % 2 == 1
     out_ref[...] = jnp.where(odd, south, east)
 
@@ -210,6 +253,7 @@
         imag = jnp.where(low, other, x)
         return jnp.where(low, x, other), jnp.where(low, -imag, imag)
 
+    east = jnp.where(west_slots(lane), dev_roll(east, -1), east)
     east_r, east_i = split(east)
     south_r, south_i = split(south)
     phase = None
@@ -230,11 +274,18 @@
 
 
 def blend_kernel(
-    n_cols, ro, rw, do, dw, me, g_ref, p_hbm, east_ref, south_ref, out_hbm, phase_ref,
-    p_ref, stage, all_ref, near_ref, fac, sem, out_sem, sems,
+    n_cols, ro, rw, do, dw, me, g_ref, p_hbm, left_ref, late_ref, south_ref, out_hbm, phase_ref,
+    p_ref, east_ref, stage, all_ref, near_ref, fac, sem, out_sem, sems,
 ):
     for i in range(N):
         fetch_row(p_hbm, p_ref, sems, i).start()
+    size = left_ref.shape[0]
+    joins = [
+        pltpu.make_async_copy(ref, east_ref.at[k * size : (k + 1) * size, :], sems.at[N + k])
+        for k, ref in enumerate((left_ref, late_ref))
+    ]
+    for join in joins:
+        join.start()
     n_dev = all_ref.shape[0]
     all_ref[...] = sync_phases(
         g_ref[pl.ds(0, n_dev, 2), :], g_ref[pl.ds(1, n_dev, 2), :], n_cols, n_dev * N * N
@@ -306,6 +357,8 @@
             ).start()
 
     fetch_row(p_hbm, p_ref, sems, 0).wait()
+    for join in joins:
+        join.wait()
 
     def body(i, carry):
         fetch_row(p_hbm, p_ref, sems, i + 1).wait()
@@ -323,7 +376,8 @@
     r, c = lax.axis_index("row"), lax.axis_index("col")
     tables = (right_offset, right_width, down_offset, down_width)
     flat_shape = (N * N * 2 * SIDE, SIDE)
-    flat = pltpu.with_memory_space_constraint(patches.reshape(flat_shape), pltpu.HBM)
+    fixed = lambda x: pltpu.with_memory_space_constraint(x, pltpu.HBM)
+    flat = fixed(patches.reshape(flat_shape))
     south_shape = (2 * PAD + N * 2 * HALF, SIDE)
     vmem, smem = pl.BlockSpec(memory_space=pltpu.VMEM), pl.BlockSpec(memory_space=pltpu.SMEM)
     hbm = pl.BlockSpec(memory_space=pltpu.HBM)
@@ -335,17 +389,26 @@
     def cost(flops, moved):
         return pl.CostEstimate(flops=flops, bytes_accessed=moved, transcendentals=0)
 
-    strip, lower = pl.pallas_call(
+    half = N // 2 * SIDE
+    left, right, late, lower = pl.pallas_call(
         strip_kernel,
-        out_shape=(f32(N * SIDE, SIDE), f32(*south_shape)),
-        in_specs=[hbm],
-        out_specs=(vmem, vmem),
-        scratch_shapes=[pltpu.VMEM((N, 2, SIDE, SIDE), jnp.float32), pltpu.SemaphoreType.DMA((1 + 2 * N,))],
+        out_shape=(f32(half, SIDE), f32(half, SIDE), f32(half, SIDE), f32(*south_shape)),
+        in_specs=[hbm] * 3,
+        out_specs=(vmem,) * 4,
+        scratch_shapes=[
+            pltpu.VMEM((N, 2, SIDE, SIDE), jnp.float32),
+            pltpu.VMEM((N // 2, 2, SIDE, SIDE), jnp.float32),
+            pltpu.SMEM((N, N), jnp.int32),
+            pltpu.SMEM((N, N), jnp.int32),
+            pltpu.SemaphoreType.DMA((5 + 2 * N,)),
+        ],
         compiler_params=params(8),
         cost_estimate=cost(400_000, 3_000_000),
         name="strips",
-    )(pltpu.with_memory_space_constraint(patches, pltpu.HBM))
-    east_edge = lax.ppermute(strip, "col", [(k + 1, k) for k in range(n_cols - 1)])
+    )(fixed(right_offset), fixed(right_width), fixed(patches))
+    to_left = [(k + 1, k) for k in range(n_cols - 1)]
+    east_edge = lax.ppermute(left, "col", to_left)
+    west_edge = lax.ppermute(right, "col", [(k, k + 1) for k in range(n_cols - 1)])
     south_edge = lax.ppermute(lower, "row", [(k + 1, k) for k in range(n_rows - 1)])
 
     sums, held = pl.pallas_call(
@@ -357,40 +420,44 @@
         compiler_params=params(16),
         cost_estimate=cost(20_000_000, 9_000_000),
         name="inner",
-    )(*tables, flat)
+    )(*map(fixed, tables), flat)
+
+    late, sums = lax.optimization_barrier((late, sums))
+    late_edge = lax.ppermute(late, "col", to_left)
 
     sent = pl.pallas_call(
         rim_kernel,
         out_shape=f32(2 * n_dev, SIDE),
-        in_specs=[smem] * 4 + [vmem] * 6,
+        in_specs=[smem] * 4 + [vmem] * 8,
         out_specs=vmem,
         scratch_shapes=[pltpu.VMEM((SUMS, SIDE), jnp.float32)],
         compiler_params=params(16),
         cost_estimate=cost(5_000_000, 3_000_000),
         name="rim",
-    )(*tables, sums, held, east_edge, south_edge, right_width, down_width)
+    )(*tables, sums, held, east_edge, west_edge, late, south_edge, right_width, down_width)
     grid = lax.all_to_all(sent, ("row", "col"), 0, 0, tiled=True)
 
     me = jnp.stack([r * n_cols + c, (c < n_cols - 1).astype(jnp.int32), (r < n_rows - 1).astype(jnp.int32)])
     blended, phases = pl.pallas_call(
         functools.partial(blend_kernel, n_cols),
         out_shape=(f32(*flat_shape), f32(2, N, N)),
-        in_specs=[smem] * 5 + [vmem, hbm, vmem, vmem],
+        in_specs=[smem] * 5 + [vmem, hbm, vmem, vmem, vmem],
         out_specs=(hbm, vmem),
         scratch_shapes=[
             pltpu.VMEM(flat_shape, jnp.float32),
+            pltpu.VMEM((N * SIDE, SIDE), jnp.float32),
             pltpu.VMEM(flat_shape, jnp.float32),
             pltpu.VMEM((n_dev, SIDE), jnp.float32),
             pltpu.VMEM((8, SIDE), jnp.float32),
             pltpu.SMEM((8, SIDE), jnp.float32),
             pltpu.SemaphoreType.DMA,
             pltpu.SemaphoreType.DMA,
-            pltpu.SemaphoreType.DMA((N,)),
+            pltpu.SemaphoreType.DMA((N + 2,)),
         ],
         compiler_params=params(32),
         cost_estimate=cost(30_000_000, 10_000_000),
         name="blend",
-    )(*tables, me, grid, flat, east_edge, south_edge)
+    )(*tables, me, grid, flat, east_edge, late_edge, south_edge)
     return blended.reshape(patches.shape), phases
 
 

time: 55.2 us -> 52.2 us (0.946)
  waiting for transfers between devices: 19.1 us -> 10.1 us
  starting transfers between devices: 17.1 us -> 23.4 us
    ppermute x1 -> x3, waiting for transfers between devices: 9 us -> 0.01 us  [the longest x1 0.01 us: local(): east_edge = lax.ppermute(left, 'col', to_left)]
    ppermute x1 -> x3, starting transfers between devices: 1.29 us -> 6.59 us  [the longest x1 4 us: local(): lax.ppermute(right, 'col', [(k, k + 1) for k in range(n_cols - 1)])]
    all_to_all x1, starting transfers between devices: 12.5 us -> 13.5 us  [local(): grid = lax.all_to_all(sent, ('row', 'col'), 0, 0, tiled=True)]
  transfers between devices with their start and end apart: 3 -> 5, of which waited for: 2 -> 1; matrix products, arithmetic and copies ran while one was open for 0% -> 0% of each run, Pallas kernels for 9% -> 14%
where the time goes in v3:
time: 52.2 us; the launch traced here: 51.9 us
  starting transfers between devices  23.4 us (45%)
  Pallas kernels  17.5 us (34%)
  waiting for transfers between devices  10.1 us (19%)
  between operations  0.78 us (1%)
    all_to_all x1, starting transfers between devices, local(): grid = lax.all_to_all(sent, ('row', 'col'), 0, 0, tiled=True)  13.5 us
    all_to_all x1, waiting for transfers between devices, local(): grid = lax.all_to_all(sent, ('row', 'col'), 0, 0, tiled=True)  10.1 us
    pallas_call x1, Pallas kernels, local(): pl.pallas_call(functools.partial(blend_kernel, n_cols), out_shape=(f32(*f...  8.33 us
    pallas_call x1, Pallas kernels, local(): pl.pallas_call(inner_kernel, out_shape=(f32(8 * SUMS, SIDE), f32(*flat_sh...  5.18 us
    ppermute x1, starting transfers between devices, local(): lax.ppermute(right, 'col', [(k, k + 1) for k in range(n_cols - 1)])  4 us
    ppermute x1, starting transfers between devices, local(): lax.ppermute(lower, 'row', [(k + 1, k) for k in range(n_rows - 1)])  3.33 us
    pallas_call x1, Pallas kernels, local(): pl.pallas_call(rim_kernel, out_shape=f32(2 * n_dev, SIDE), in_specs=[smem...  2.23 us
    pallas_call x1, Pallas kernels, local(): pl.pallas_call(strip_kernel, out_shape=(f32(half, SIDE), f32(half, SIDE),...  1.77 us
  transfers between devices with their start and end apart: 5, of which 1 were waited for; matrix products, arithmetic and copies ran while one was open for 0% of the time, Pallas kernels for 14%

profile of v3, /device:TPU:1, one launch (start us, length us, event | category | flops | bytes accessed | tf_op | source)
XLA Modules:
  0.0 51.9 jit_solution(8955356751584143501)
XLA Ops:
  0.6 0.0 copy-start
  0.6 0.0 copy-start.1
  0.7 0.0 copy-start.2
  0.7 0.0 copy-start.3
  0.7 1.8 %strips.1 = (f32[512,128]{1,0:T(8,128)S(1)}, f32[512,128]{1,0:T(8,128)S(1)}, f32[512,128]{1,0:T(8,128)S(1)}, f32[1040,128]{1,0:T(8,128)S(1)}) custom-call(s32[8,8]{1,0:T(8,128)} %ro.3, s32[8,8]{1,0:T(8,128)} %rw.3, f32[8,8,2,128,128]{4,3,2,1,0:T(8,128)} %p_hbm.1), custom_call_target="tpu_custom_call" | custom-call | flops 400000 | bytes 3000000 | tf_op jit(solution)/shard_map/strips/pallas_call | solution.py:393
  2.5 3.3 %collective-permute-start.2 = (f32[1040,128]{1,0:T(8,128)S(1)}, f32[1040,128]{1,0:T(8,128)S(1)}, u32[]{:S(2)}, u32[]{:S(2)}) collective-permute-start(f32[1040,128]{1,0:T(8,128)S(1)} %get-tuple-element.19), channel_id=1, source_target_pairs={{16,0},{32,16},{48,32},{64,48},{80,64},{96,80},{112,96},{17,1},{33... | collective-permute-start | bytes 1597448 | tf_op jit(solution)/shard_map/ppermute | solution.py:412
  5.8 1.3 %collective-permute-start = (f32[512,128]{1,0:T(8,128)S(1)}, f32[512,128]{1,0:T(8,128)S(1)}, u32[]{:S(2)}, u32[]{:S(2)}) collective-permute-start(f32[512,128]{1,0:T(8,128)S(1)} %get-tuple-element.16), channel_id=1, source_target_pairs={{1,0},{2,1},{3,2},{4,3},{5,4},{6,5},{7,6},{8,7},{9,8},{10,9},{11,1... | collective-permute-start | bytes 786440 | tf_op jit(solution)/shard_map/ppermute | solution.py:410
  7.1 4.0 %collective-permute-start.1 = (f32[512,128]{1,0:T(8,128)S(1)}, f32[512,128]{1,0:T(8,128)S(1)}, u32[]{:S(2)}, u32[]{:S(2)}) collective-permute-start(f32[512,128]{1,0:T(8,128)S(1)} %get-tuple-element.17), channel_id=1, source_target_pairs={{0,1},{1,2},{2,3},{3,4},{4,5},{5,6},{6,7},{7,8},{8,9},{9,10},{10,1... | collective-permute-start | bytes 786440 | tf_op jit(solution)/shard_map/ppermute | solution.py:411
  11.1 5.2 %inner.1 = (f32[2048,128]{1,0:T(8,128)S(1)}, f32[16384,128]{1,0:T(8,128)S(1)}) custom-call(s32[8,8]{1,0:T(8,128)} %ro.3, s32[8,8]{1,0:T(8,128)} %rw.3, s32[8,8]{1,0:T(8,128)} %do.3, s32[8,8]{1,0:T(8,128)} %dw.3, f32[16384,128]{1,0:T(8,128)} %bitcast.8), custom_call_target="tpu_custom_call" | custom-call | flops 20000000 | bytes 9000000 | tf_op jit(solution)/shard_map/inner/pallas_call | solution.py:414
  16.3 1.3 %collective-permute-start.3 = (f32[512,128]{1,0:T(8,128)S(1)}, f32[512,128]{1,0:T(8,128)S(1)}, u32[]{:S(2)}, u32[]{:S(2)}) collective-permute-start(f32[512,128]{1,0:T(8,128)S(1)} %get-tuple-element.18.late_ref), channel_id=1, source_target_pairs={{1,0},{2,1},{3,2},{4,3},{5,4},{6,5},{7,6},{8,7},{9,8},{10,9},{11,1... | collective-permute-start | bytes 786440 | tf_op jit(solution)/shard_map/ppermute | solution.py:426
  17.6 0.0 collective-permute-done.east_ref.left_ref
  17.6 0.0 collective-permute-done.1.west_ref
  17.6 0.0 collective-permute-done.2.south_ref
  17.6 0.0 copy-done
  17.6 0.0 copy-done.1
  17.6 0.0 copy-done.2
  17.6 0.0 copy-done.3
  17.7 2.2 %rim.1 = f32[256,128]{1,0:T(8,128)} custom-call(s32[8,8]{1,0:T(8,128)S(1)} %copy-done.1, s32[8,8]{1,0:T(8,128)S(1)} %copy-done, s32[8,8]{1,0:T(8,128)S(1)} %copy-done.3, s32[8,8]{1,0:T(8,128)S(1)} %copy-done.2, f32[2048,128]{1,0:T(8,128)S(1)} %get-tuple-element.14.x_ref, f32[16384,128]{1,0:T(8,128)S(1)} %get-tuple-element.15.p_ref, ...), custom_call_target="tpu_custom_call" | custom-call | flops 5000000 | bytes 3000000 | tf_op jit(solution)/shard_map/rim/pallas_call | solution.py:428
  19.9 13.5 %all-to-all-start = ((f32[128,2,128]{2,1,0:T(2,128)}), f32[128,2,128]{2,1,0:T(2,128)S(1)}, u32[]{:S(2)}, u32[]{:S(2)}) async-start(f32[128,2,128]{2,1,0:T(2,128)} %bitcast.4), calls=%async_computation | async-start | bytes 262144 | tf_op jit(solution)/shard_map/all_to_all | solution.py:438
  33.4 0.1 pad_add_fusion.me
  33.5 0.0 collective-permute-done.3.late_ref
  33.5 10.1 %all-to-all-done = f32[128,2,128]{2,1,0:T(2,128)S(1)} async-done(((f32[128,2,128]{2,1,0:T(2,128)}), f32[128,2,128]{2,1,0:T(2,128)S(1)}, u32[]{:S(2)}, u32[]{:S(2)}) %all-to-all-start) | async-done | bytes 131104 | tf_op jit(solution)/shard_map/all_to_all | solution.py:438
  43.6 8.3 %blend.1 = (f32[16384,128]{1,0:T(8,128)}, f32[2,8,8]{2,1,0:T(8,128)}) custom-call(s32[8,8]{1,0:T(8,128)S(1)} %copy-done.1, s32[8,8]{1,0:T(8,128)S(1)} %copy-done, s32[8,8]{1,0:T(8,128)S(1)} %copy-done.3, s32[8,8]{1,0:T(8,128)S(1)} %copy-done.2, s32[3]{0:T(128)S(1)} %pad_add_fusion.me, f32[256,128]{1,0:T(8,128)S(1)} %bitcast.7, f32[16384,128]{1,0:T(8,128)} %bitcast.9, ...), custom_call_target="tpu_custom_call" | custom-call | flops 30000000 | bytes 10000000 | tf_op jit(solution)/shard_map/blend/pallas_call | solution.py:441
Async XLA Ops:
  0.6 17.0 %copy-start = (s32[8,8]{1,0:T(8,128)S(1)}, s32[8,8]{1,0:T(8,128)}, u32[]{:S(2)}) copy-start(s32[8,8]{1,0:T(8,128)} %rw.3) | copy-start | bytes 772
  0.6 17.0 %copy-start.1 = (s32[8,8]{1,0:T(8,128)S(1)}, s32[8,8]{1,0:T(8,128)}, u32[]{:S(2)}) copy-start(s32[8,8]{1,0:T(8,128)} %ro.3) | copy-start | bytes 772
  0.7 17.0 %copy-start.2 = (s32[8,8]{1,0:T(8,128)S(1)}, s32[8,8]{1,0:T(8,128)}, u32[]{:S(2)}) copy-start(s32[8,8]{1,0:T(8,128)} %dw.3) | copy-start | bytes 772
  0.7 17.0 %copy-start.3 = (s32[8,8]{1,0:T(8,128)S(1)}, s32[8,8]{1,0:T(8,128)}, u32[]{:S(2)}) copy-start(s32[8,8]{1,0:T(8,128)} %do.3) | copy-start | bytes 772
  2.5 15.2 %collective-permute-start.2 = (f32[1040,128]{1,0:T(8,128)S(1)}, f32[1040,128]{1,0:T(8,128)S(1)}, u32[]{:S(2)}, u32[]{:S(2)}) collective-permute-start(f32[1040,128]{1,0:T(8,128)S(1)} %get-tuple-element.19), channel_id=1, source_target_pairs={{16,0},{32,16},{48,32},{64,48},{80,64},{96,80},{112,96},{17,1},{33... | collective-permute-start | bytes 1597448 | tf_op jit(solution)/shard_map/ppermute | solution.py:412
  5.8 11.8 %collective-permute-start = (f32[512,128]{1,0:T(8,128)S(1)}, f32[512,128]{1,0:T(8,128)S(1)}, u32[]{:S(2)}, u32[]{:S(2)}) collective-permute-start(f32[512,128]{1,0:T(8,128)S(1)} %get-tuple-element.16), channel_id=1, source_target_pairs={{1,0},{2,1},{3,2},{4,3},{5,4},{6,5},{7,6},{8,7},{9,8},{10,9},{11,1... | collective-permute-start | bytes 786440 | tf_op jit(solution)/shard_map/ppermute | solution.py:410
  7.1 10.5 %collective-permute-start.1 = (f32[512,128]{1,0:T(8,128)S(1)}, f32[512,128]{1,0:T(8,128)S(1)}, u32[]{:S(2)}, u32[]{:S(2)}) collective-permute-start(f32[512,128]{1,0:T(8,128)S(1)} %get-tuple-element.17), channel_id=1, source_target_pairs={{0,1},{1,2},{2,3},{3,4},{4,5},{5,6},{6,7},{7,8},{8,9},{9,10},{10,1... | collective-permute-start | bytes 786440 | tf_op jit(solution)/shard_map/ppermute | solution.py:411
  16.3 17.2 %collective-permute-start.3 = (f32[512,128]{1,0:T(8,128)S(1)}, f32[512,128]{1,0:T(8,128)S(1)}, u32[]{:S(2)}, u32[]{:S(2)}) collective-permute-start(f32[512,128]{1,0:T(8,128)S(1)} %get-tuple-element.18.late_ref), channel_id=1, source_target_pairs={{1,0},{2,1},{3,2},{4,3},{5,4},{6,5},{7,6},{8,7},{9,8},{10,9},{11,1... | collective-permute-start | bytes 786440 | tf_op jit(solution)/shard_map/ppermute | solution.py:426
  19.9 23.7 %all-to-all-start = ((f32[128,2,128]{2,1,0:T(2,128)}), f32[128,2,128]{2,1,0:T(2,128)S(1)}, u32[]{:S(2)}, u32[]{:S(2)}) async-start(f32[128,2,128]{2,1,0:T(2,128)} %bitcast.4), calls=%async_computation | async-start | bytes 262144 | tf_op jit(solution)/shard_map/all_to_all | solution.py:438

commit v4 on v3

--- a/solution.py
+++ b/solution.py
@@ -13,6 +13,7 @@
 HALF = 64
 ROW0 = 56
 PAD = 8
+KEEP = 2
 N = 8
 SUMS = 4 * N * N
 HIGHEST = lax.Precision.HIGHEST
@@ -120,22 +121,24 @@
         copy.wait()
 
 
-def inner_kernel(ro_hbm, rw_hbm, do_hbm, dw_hbm, p_hbm, x_ref, p_ref, ro, rw, do, dw, sems):
-    pairs = ((ro_hbm, ro), (rw_hbm, rw), (do_hbm, do), (dw_hbm, dw))
-    tables = [pltpu.make_async_copy(a, b, sems.at[N + k]) for k, (a, b) in enumerate(pairs)]
-    for copy in tables:
+def fetch_tables(refs, scratch, sems):
+    copies = [pltpu.make_async_copy(a, b, sems.at[k]) for k, (a, b) in enumerate(zip(refs, scratch))]
+    for copy in copies:
         copy.start()
-    for k in range(N):
-        fetch_row(p_hbm, p_ref, sems, N - 1 - k).start()
+    return copies
+
+
+def inner_kernel(ro_hbm, rw_hbm, do_hbm, dw_hbm, p_ref, x_ref, keep_ref, ro, rw, do, dw, sems):
+    tables = fetch_tables((ro_hbm, rw_hbm, do_hbm, dw_hbm), (ro, rw, do, dw), sems)
+    keep = pltpu.make_async_copy(p_ref.at[0 : keep_ref.shape[0], :], keep_ref, sems.at[4])
+    keep.start()
     for copy in tables:
         copy.wait()
 
     def put(quantity, i, j, value):
         x_ref[pl.ds(quantity * N * N + i * N + j, 8, SUMS), :] = value
 
-    def row_of_patches(step, carry):
-        i = N - 1 - step
-        fetch_row(p_hbm, p_ref, sems, i).wait()
+    def row_of_patches(i, carry):
         for j in range(N - 1):
             o, w = ro[i, j], rw[i, j]
             sums = east_sums(
@@ -147,7 +150,7 @@
             put(0, i, j, sums[0])
             put(1, i, j, sums[1])
 
-        @pl.when(step > 0)
+        @pl.when(i < N - 1)
         def _():
             for j in range(N):
                 sums = south_sums(
@@ -162,9 +165,14 @@
         return carry
 
     lax.fori_loop(0, N, row_of_patches, 0)
-
-
-def rim_kernel(ro, rw, do, dw, x_ref, p_ref, east_ref, west_ref, late_ref, south_ref, rw_ref, dw_ref, out_ref, all_ref):
+    keep.wait()
+
+
+def rim_kernel(
+    ro_hbm, rw_hbm, do_hbm, dw_hbm, x_ref, p_ref, east_ref, west_ref, late_ref, south_ref, rw_ref, dw_ref, out_ref,
+    all_ref, ro, rw, do, dw, sems,
+):
+    tables = fetch_tables((ro_hbm, rw_hbm, do_hbm, dw_hbm), (ro, rw, do, dw), sems)
     total = x_ref[0:SUMS, :]
     for k in range(1, 8):
         total = total + x_ref[k * SUMS : (k + 1) * SUMS, :]
@@ -176,6 +184,17 @@
 
     half = N // 2
     low = lanes((32, SIDE)) < HALF
+    for i in range(half):
+        real, imag = jnp.zeros((8, SIDE), jnp.float32), jnp.zeros((8, SIDE), jnp.float32)
+        for k in range(i * SIDE, (i + 1) * SIDE, 32):
+            a, b = west_ref[k : k + 32, :], late_ref[k : k + 32, :]
+            cross = a * pltpu.roll(b, HALF, 1)
+            real = real + fold8(a * b)
+            imag = imag + fold8(jnp.where(low, cross, -cross))
+        put(0, half + i, N - 1, real)
+        put(1, half + i, N - 1, imag)
+    for copy in tables:
+        copy.wait()
     for i in range(half):
         o, w = ro[i, N - 1], rw[i, N - 1]
         turn = (o, other_half(o))
@@ -187,15 +206,6 @@
         )
         put(0, i, N - 1, sums[0])
         put(1, i, N - 1, sums[1])
-    for i in range(half):
-        real, imag = jnp.zeros((8, SIDE), jnp.float32), jnp.zeros((8, SIDE), jnp.float32)
-        for k in range(i * SIDE, (i + 1) * SIDE, 32):
-            a, b = west_ref[k : k + 32, :], late_ref[k : k + 32, :]
-            cross = a * pltpu.roll(b, HALF, 1)
-            real = real + fold8(a * b)
-            imag = imag + fold8(jnp.where(low, cross, -cross))
-        put(0, half + i, N - 1, real)
-        put(1, half + i, N - 1, imag)
     for j in range(N):
         sums = south_sums(
             lambda part, k: p_ref[pl.ds(plane(N - 1, j, part) + k, 8), :],
@@ -274,11 +284,15 @@
 
 
 def blend_kernel(
-    n_cols, ro, rw, do, dw, me, g_ref, p_hbm, left_ref, late_ref, south_ref, out_hbm, phase_ref,
-    p_ref, east_ref, stage, all_ref, near_ref, fac, sem, out_sem, sems,
+    n_rows, n_cols, ro_hbm, rw_hbm, do_hbm, dw_hbm, g_ref, keep_ref, p_hbm, left_ref, late_ref, south_ref, out_hbm, phase_ref,
+    p_ref, east_ref, stage, all_ref, near_ref, fac, ro, rw, do, dw, sem, out_sem, sems,
 ):
-    for i in range(N):
+    r, c = lax.axis_index("row"), lax.axis_index("col")
+    for i in range(KEEP, N):
         fetch_row(p_hbm, p_ref, sems, i).start()
+    tables = fetch_tables((ro_hbm, rw_hbm, do_hbm, dw_hbm), (ro, rw, do, dw), sems.at[pl.ds(N + 2, 4)])
+    for i in range(KEEP):
+        fetch_row(keep_ref, p_ref, sems, i).start()
     size = left_ref.shape[0]
     joins = [
         pltpu.make_async_copy(ref, east_ref.at[k * size : (k + 1) * size, :], sems.at[N + k])
@@ -290,7 +304,7 @@
     all_ref[...] = sync_phases(
         g_ref[pl.ds(0, n_dev, 2), :], g_ref[pl.ds(1, n_dev, 2), :], n_cols, n_dev * N * N
     )
-    d = me[0]
+    d = r * n_cols + c
     lane = lanes((1, SIDE))
     own = all_ref[pl.ds(d, 1), :]
     right = all_ref[pl.ds(lax.rem(d + 1, n_dev), 1), :]
@@ -315,10 +329,10 @@
         for j in range(N):
             o, w = ro[i, j], rw[i, j]
             if j == N - 1:
-                w = jnp.where(me[1] > 0, w, 0)
+                w = jnp.where(c < n_cols - 1, w, 0)
             keep = (lane >= o) & (lane < o + w)
             down = do[i, j]
-            deep = jnp.where(me[2] > 0, dw[i, j], 0) if last else dw[i, j]
+            deep = jnp.where(r < n_rows - 1, dw[i, j], 0) if last else dw[i, j]
             at = i * N + j
             inv = jnp.where(keep, 0.5, 1.0)
             inv_south = jnp.where(keep, 1.0 / 3.0, 0.5)
@@ -357,7 +371,7 @@
             ).start()
 
     fetch_row(p_hbm, p_ref, sems, 0).wait()
-    for join in joins:
+    for join in joins + tables:
         join.wait()
 
     def body(i, carry):
@@ -373,13 +387,14 @@
 def local(patches, right_offset, right_width, down_offset, down_width):
     n_rows, n_cols = lax.axis_size("row"), lax.axis_size("col")
     n_dev = n_rows * n_cols
-    r, c = lax.axis_index("row"), lax.axis_index("col")
     tables = (right_offset, right_width, down_offset, down_width)
     flat_shape = (N * N * 2 * SIDE, SIDE)
     fixed = lambda x: pltpu.with_memory_space_constraint(x, pltpu.HBM)
-    flat = fixed(patches.reshape(flat_shape))
+    flat = patches.reshape(flat_shape)
+    pinned = [fixed(x) for x in tables]
+    table_scratch = [pltpu.SMEM((N, N), jnp.int32)] * 4
     south_shape = (2 * PAD + N * 2 * HALF, SIDE)
-    vmem, smem = pl.BlockSpec(memory_space=pltpu.VMEM), pl.BlockSpec(memory_space=pltpu.SMEM)
+    vmem = pl.BlockSpec(memory_space=pltpu.VMEM)
     hbm = pl.BlockSpec(memory_space=pltpu.HBM)
     f32 = lambda *shape: jax.ShapeDtypeStruct(shape, jnp.float32)
 
@@ -409,39 +424,36 @@
     to_left = [(k + 1, k) for k in range(n_cols - 1)]
     east_edge = lax.ppermute(left, "col", to_left)
     west_edge = lax.ppermute(right, "col", [(k, k + 1) for k in range(n_cols - 1)])
+    late_edge = lax.ppermute(late, "col", to_left)
     south_edge = lax.ppermute(lower, "row", [(k + 1, k) for k in range(n_rows - 1)])
 
-    sums, held = pl.pallas_call(
+    sums, keep = pl.pallas_call(
         inner_kernel,
-        out_shape=(f32(8 * SUMS, SIDE), f32(*flat_shape)),
-        in_specs=[hbm] * 5,
+        out_shape=(f32(8 * SUMS, SIDE), f32(KEEP * N * 2 * SIDE, SIDE)),
+        in_specs=[hbm] * 4 + [vmem],
         out_specs=(vmem, vmem),
-        scratch_shapes=[pltpu.SMEM((N, N), jnp.int32)] * 4 + [pltpu.SemaphoreType.DMA((N + 4,))],
+        scratch_shapes=table_scratch + [pltpu.SemaphoreType.DMA((5,))],
         compiler_params=params(16),
         cost_estimate=cost(20_000_000, 9_000_000),
         name="inner",
-    )(*map(fixed, tables), flat)
-
-    late, sums = lax.optimization_barrier((late, sums))
-    late_edge = lax.ppermute(late, "col", to_left)
+    )(*pinned, flat)
 
     sent = pl.pallas_call(
         rim_kernel,
         out_shape=f32(2 * n_dev, SIDE),
-        in_specs=[smem] * 4 + [vmem] * 8,
+        in_specs=[hbm] * 4 + [vmem] * 8,
         out_specs=vmem,
-        scratch_shapes=[pltpu.VMEM((SUMS, SIDE), jnp.float32)],
+        scratch_shapes=[pltpu.VMEM((SUMS, SIDE), jnp.float32)] + table_scratch + [pltpu.SemaphoreType.DMA((4,))],
         compiler_params=params(16),
         cost_estimate=cost(5_000_000, 3_000_000),
         name="rim",
-    )(*tables, sums, held, east_edge, west_edge, late, south_edge, right_width, down_width)
+    )(*pinned, sums, flat, east_edge, west_edge, late, south_edge, right_width, down_width)
     grid = lax.all_to_all(sent, ("row", "col"), 0, 0, tiled=True)
 
-    me = jnp.stack([r * n_cols + c, (c < n_cols - 1).astype(jnp.int32), (r < n_rows - 1).astype(jnp.int32)])
     blended, phases = pl.pallas_call(
-        functools.partial(blend_kernel, n_cols),
+        functools.partial(blend_kernel, n_rows, n_cols),
         out_shape=(f32(*flat_shape), f32(2, N, N)),
-        in_specs=[smem] * 5 + [vmem, hbm, vmem, vmem, vmem],
+        in_specs=[hbm] * 4 + [vmem, vmem, hbm, vmem, vmem, vmem],
         out_specs=(hbm, vmem),
         scratch_shapes=[
             pltpu.VMEM(flat_shape, jnp.float32),
@@ -450,14 +462,15 @@
             pltpu.VMEM((n_dev, SIDE), jnp.float32),
             pltpu.VMEM((8, SIDE), jnp.float32),
             pltpu.SMEM((8, SIDE), jnp.float32),
+            *table_scratch,
             pltpu.SemaphoreType.DMA,
             pltpu.SemaphoreType.DMA,
-            pltpu.SemaphoreType.DMA((N + 2,)),
+            pltpu.SemaphoreType.DMA((N + 6,)),
         ],
         compiler_params=params(32),
         cost_estimate=cost(30_000_000, 10_000_000),
         name="blend",
-    )(*tables, me, grid, flat, east_edge, late_edge, south_edge)
+    )(*pinned, grid, keep, fixed(flat), east_edge, late_edge, south_edge)
     return blended.reshape(patches.shape), phases
 
 

time: 52.2 us -> 51.5 us (0.987)
  Pallas kernels: 17.5 us -> 16.4 us
    pallas_call x3, Pallas kernels: 15.7 us -> 14.5 us  [the longest x1 6.71 us: local(): pl.pallas_call(functools.partial(blend_kernel, n_rows, n_cols), out_shape...]
  transfers between devices with their start and end apart: 5 -> 5, of which waited for: 1 -> 1; matrix products, arithmetic and copies ran while one was open for 0% -> 0% of each run, Pallas kernels for 14% -> 15%
where the time goes in v4:
time: 51.5 us; the launch traced here: 51.1 us
  starting transfers between devices  23.7 us (46%)
  Pallas kernels  16.4 us (32%)
  waiting for transfers between devices  10.2 us (20%)
  between operations  0.74 us (1%)
    all_to_all x1, starting transfers between devices, local(): grid = lax.all_to_all(sent, ('row', 'col'), 0, 0, tiled=True)  13.5 us
    all_to_all x1, waiting for transfers between devices, local(): grid = lax.all_to_all(sent, ('row', 'col'), 0, 0, tiled=True)  10.2 us
    pallas_call x1, Pallas kernels, local(): pl.pallas_call(functools.partial(blend_kernel, n_rows, n_cols), out_shape...  6.71 us
    pallas_call x1, Pallas kernels, local(): pl.pallas_call(inner_kernel, out_shape=(f32(8 * SUMS, SIDE), f32(KEEP * N...  4.8 us
    ppermute x1, starting transfers between devices, local(): lax.ppermute(right, 'col', [(k, k + 1) for k in range(n_cols - 1)])  4 us
    ppermute x1, starting transfers between devices, local(): lax.ppermute(lower, 'row', [(k + 1, k) for k in range(n_rows - 1)])  3.59 us
    pallas_call x1, Pallas kernels, local(): pl.pallas_call(rim_kernel, out_shape=f32(2 * n_dev, SIDE), in_specs=[hbm]...  3.01 us
    pallas_call x1, Pallas kernels, local(): pl.pallas_call(strip_kernel, out_shape=(f32(half, SIDE), f32(half, SIDE),...  1.91 us
  transfers between devices with their start and end apart: 5, of which 1 were waited for; matrix products, arithmetic and copies ran while one was open for 0% of the time, Pallas kernels for 15%

profile of v4, /device:TPU:1, one launch (start us, length us, event | category | flops | bytes accessed | tf_op | source)
XLA Modules:
  0.0 51.1 jit_solution(9864420698657321746)
XLA Ops:
  0.6 0.0 copy-start
  0.6 1.9 %strips.1 = (f32[512,128]{1,0:T(8,128)S(1)}, f32[512,128]{1,0:T(8,128)S(1)}, f32[512,128]{1,0:T(8,128)S(1)}, f32[1040,128]{1,0:T(8,128)S(1)}) custom-call(s32[8,8]{1,0:T(8,128)} %ro_hbm.7, s32[8,8]{1,0:T(8,128)} %rw_hbm.7, f32[8,8,2,128,128]{4,3,2,1,0:T(8,128)} %p_hbm.1), custom_call_target="tpu_custom_call" | custom-call | flops 400000 | bytes 3000000 | tf_op jit(solution)/shard_map/strips/pallas_call | solution.py:408
  2.6 3.6 %collective-permute-start.2 = (f32[1040,128]{1,0:T(8,128)S(1)}, f32[1040,128]{1,0:T(8,128)S(1)}, u32[]{:S(2)}, u32[]{:S(2)}) collective-permute-start(f32[1040,128]{1,0:T(8,128)S(1)} %get-tuple-element.14), channel_id=1, source_target_pairs={{16,0},{32,16},{48,32},{64,48},{80,64},{96,80},{112,96},{17,1},{33... | collective-permute-start | bytes 1597448 | tf_op jit(solution)/shard_map/ppermute | solution.py:428
  6.2 1.3 %collective-permute-start = (f32[512,128]{1,0:T(8,128)S(1)}, f32[512,128]{1,0:T(8,128)S(1)}, u32[]{:S(2)}, u32[]{:S(2)}) collective-permute-start(f32[512,128]{1,0:T(8,128)S(1)} %get-tuple-element.11), channel_id=1, source_target_pairs={{1,0},{2,1},{3,2},{4,3},{5,4},{6,5},{7,6},{8,7},{9,8},{10,9},{11,1... | collective-permute-start | bytes 786440 | tf_op jit(solution)/shard_map/ppermute | solution.py:425
  7.5 4.0 %collective-permute-start.1 = (f32[512,128]{1,0:T(8,128)S(1)}, f32[512,128]{1,0:T(8,128)S(1)}, u32[]{:S(2)}, u32[]{:S(2)}) collective-permute-start(f32[512,128]{1,0:T(8,128)S(1)} %get-tuple-element.12), channel_id=1, source_target_pairs={{0,1},{1,2},{2,3},{3,4},{4,5},{5,6},{6,7},{7,8},{8,9},{9,10},{10,1... | collective-permute-start | bytes 786440 | tf_op jit(solution)/shard_map/ppermute | solution.py:426
  11.5 1.3 %collective-permute-start.3 = (f32[512,128]{1,0:T(8,128)S(1)}, f32[512,128]{1,0:T(8,128)S(1)}, u32[]{:S(2)}, u32[]{:S(2)}) collective-permute-start(f32[512,128]{1,0:T(8,128)S(1)} %get-tuple-element.13.late_ref), channel_id=1, source_target_pairs={{1,0},{2,1},{3,2},{4,3},{5,4},{6,5},{7,6},{8,7},{9,8},{10,9},{11,1... | collective-permute-start | bytes 786440 | tf_op jit(solution)/shard_map/ppermute | solution.py:427
  12.8 0.0 copy-done
  12.8 4.8 %inner.1 = (f32[2048,128]{1,0:T(8,128)S(1)}, f32[4096,128]{1,0:T(8,128)S(1)}) custom-call(s32[8,8]{1,0:T(8,128)} %ro_hbm.7, s32[8,8]{1,0:T(8,128)} %rw_hbm.7, s32[8,8]{1,0:T(8,128)} %do_hbm.5, s32[8,8]{1,0:T(8,128)} %dw_hbm.5, f32[16384,128]{1,0:T(8,128)S(1)} %bitcast.5), custom_call_target="tpu_custom_call" | custom-call | flops 20000000 | bytes 9000000 | tf_op jit(solution)/shard_map/inner/pallas_call | solution.py:430
  17.6 0.0 collective-permute-done.east_ref.left_ref
  17.6 0.0 collective-permute-done.1.west_ref
  17.6 0.0 collective-permute-done.2.south_ref
  17.6 3.0 %rim.1 = f32[256,128]{1,0:T(8,128)} custom-call(s32[8,8]{1,0:T(8,128)} %ro_hbm.7, s32[8,8]{1,0:T(8,128)} %rw_hbm.7, s32[8,8]{1,0:T(8,128)} %do_hbm.5, s32[8,8]{1,0:T(8,128)} %dw_hbm.5, f32[2048,128]{1,0:T(8,128)S(1)} %get-tuple-element.10.x_ref, f32[16384,128]{1,0:T(8,128)S(1)} %bitcast.6, f32[512,128]{1,0:T(8,128)S(1)} %collective-permute-done.east_ref.left_ref, ...), custom_call_target="tpu_custom_call" | custom-call | flops 5000000 | bytes 3000000 | tf_op jit(solution)/shard_map/rim/pallas_call | solution.py:441
  20.6 13.5 %all-to-all-start = ((f32[128,2,128]{2,1,0:T(2,128)}), f32[128,2,128]{2,1,0:T(2,128)S(1)}, u32[]{:S(2)}, u32[]{:S(2)}) async-start(f32[128,2,128]{2,1,0:T(2,128)} %bitcast.1), calls=%async_computation | async-start | bytes 262144 | tf_op jit(solution)/shard_map/all_to_all | solution.py:451
  34.1 0.0 collective-permute-done.3.late_ref
  34.2 10.2 %all-to-all-done = f32[128,2,128]{2,1,0:T(2,128)S(1)} async-done(((f32[128,2,128]{2,1,0:T(2,128)}), f32[128,2,128]{2,1,0:T(2,128)S(1)}, u32[]{:S(2)}, u32[]{:S(2)}) %all-to-all-start) | async-done | bytes 131104 | tf_op jit(solution)/shard_map/all_to_all | solution.py:451
  44.3 6.7 %blend.1 = (f32[16384,128]{1,0:T(8,128)}, f32[2,8,8]{2,1,0:T(8,128)}) custom-call(s32[8,8]{1,0:T(8,128)} %ro_hbm.7, s32[8,8]{1,0:T(8,128)} %rw_hbm.7, s32[8,8]{1,0:T(8,128)} %do_hbm.5, s32[8,8]{1,0:T(8,128)} %dw_hbm.5, f32[256,128]{1,0:T(8,128)S(1)} %bitcast.7, f32[4096,128]{1,0:T(8,128)S(1)} %get-tuple-element.15.keep_ref, f32[16384,128]{1,0:T(8,128)} %bitcast.4, ...), custom_call_target="tpu_custom_call" | custom-call | flops 30000000 | bytes 10000000 | tf_op jit(solution)/shard_map/blend/pallas_call | solution.py:453
Async XLA Ops:
  0.6 12.1 %copy-start = (f32[8,8,2,128,128]{4,3,2,1,0:T(8,128)S(1)}, f32[8,8,2,128,128]{4,3,2,1,0:T(8,128)}, u32[]{:S(2)}) copy-start(f32[8,8,2,128,128]{4,3,2,1,0:T(8,128)} %p_hbm.1) | copy-start | bytes 25165828
  2.6 15.1 %collective-permute-start.2 = (f32[1040,128]{1,0:T(8,128)S(1)}, f32[1040,128]{1,0:T(8,128)S(1)}, u32[]{:S(2)}, u32[]{:S(2)}) collective-permute-start(f32[1040,128]{1,0:T(8,128)S(1)} %get-tuple-element.14), channel_id=1, source_target_pairs={{16,0},{32,16},{48,32},{64,48},{80,64},{96,80},{112,96},{17,1},{33... | collective-permute-start | bytes 1597448 | tf_op jit(solution)/shard_map/ppermute | solution.py:428
  6.2 11.4 %collective-permute-start = (f32[512,128]{1,0:T(8,128)S(1)}, f32[512,128]{1,0:T(8,128)S(1)}, u32[]{:S(2)}, u32[]{:S(2)}) collective-permute-start(f32[512,128]{1,0:T(8,128)S(1)} %get-tuple-element.11), channel_id=1, source_target_pairs={{1,0},{2,1},{3,2},{4,3},{5,4},{6,5},{7,6},{8,7},{9,8},{10,9},{11,1... | collective-permute-start | bytes 786440 | tf_op jit(solution)/shard_map/ppermute | solution.py:425
  7.5 10.1 %collective-permute-start.1 = (f32[512,128]{1,0:T(8,128)S(1)}, f32[512,128]{1,0:T(8,128)S(1)}, u32[]{:S(2)}, u32[]{:S(2)}) collective-permute-start(f32[512,128]{1,0:T(8,128)S(1)} %get-tuple-element.12), channel_id=1, source_target_pairs={{0,1},{1,2},{2,3},{3,4},{4,5},{5,6},{6,7},{7,8},{8,9},{9,10},{10,1... | collective-permute-start | bytes 786440 | tf_op jit(solution)/shard_map/ppermute | solution.py:426
  11.5 22.7 %collective-permute-start.3 = (f32[512,128]{1,0:T(8,128)S(1)}, f32[512,128]{1,0:T(8,128)S(1)}, u32[]{:S(2)}, u32[]{:S(2)}) collective-permute-start(f32[512,128]{1,0:T(8,128)S(1)} %get-tuple-element.13.late_ref), channel_id=1, source_target_pairs={{1,0},{2,1},{3,2},{4,3},{5,4},{6,5},{7,6},{8,7},{9,8},{10,9},{11,1... | collective-permute-start | bytes 786440 | tf_op jit(solution)/shard_map/ppermute | solution.py:427
  20.6 23.7 %all-to-all-start = ((f32[128,2,128]{2,1,0:T(2,128)}), f32[128,2,128]{2,1,0:T(2,128)S(1)}, u32[]{:S(2)}, u32[]{:S(2)}) async-start(f32[128,2,128]{2,1,0:T(2,128)} %bitcast.1), calls=%async_computation | async-start | bytes 262144 | tf_op jit(solution)/shard_map/all_to_all | solution.py:451

commit v5 on v4

--- a/solution.py
+++ b/solution.py
@@ -72,7 +72,9 @@
     return pltpu.make_async_copy(p_hbm.at[pl.ds(at, block), :], p_ref.at[pl.ds(at, block), :], sems.at[i])
 
 
-def strip_kernel(ro_hbm, rw_hbm, p_hbm, left_ref, right_ref, late_ref, south_ref, first, last, ro, rw, sems):
+def strip_kernel(
+    ro_hbm, rw_hbm, do_hbm, dw_hbm, p_hbm, left_ref, right_ref, late_ref, south_ref, table_ref, first, last, ro, rw, sems
+):
     half = N // 2
     copies = [
         pltpu.make_async_copy(ro_hbm, ro, sems.at[0]),
@@ -83,7 +85,12 @@
     ]
     for copy in copies:
         copy.start()
-    rows = []
+    rows = [
+        pltpu.make_async_copy(ref, table_ref.at[k], sems.at[5 + 2 * N + k])
+        for k, ref in enumerate((ro_hbm, rw_hbm, do_hbm, dw_hbm))
+    ]
+    for copy in rows:
+        copy.start()
     for j in range(N):
         for part in range(2):
             at = PAD + (j * 2 + part) * HALF
@@ -121,19 +128,13 @@
         copy.wait()
 
 
-def fetch_tables(refs, scratch, sems):
-    copies = [pltpu.make_async_copy(a, b, sems.at[k]) for k, (a, b) in enumerate(zip(refs, scratch))]
-    for copy in copies:
-        copy.start()
-    return copies
-
-
-def inner_kernel(ro_hbm, rw_hbm, do_hbm, dw_hbm, p_ref, x_ref, keep_ref, ro, rw, do, dw, sems):
-    tables = fetch_tables((ro_hbm, rw_hbm, do_hbm, dw_hbm), (ro, rw, do, dw), sems)
-    keep = pltpu.make_async_copy(p_ref.at[0 : keep_ref.shape[0], :], keep_ref, sems.at[4])
+def inner_kernel(table_ref, p_ref, x_ref, keep_ref, table, sems):
+    tables = pltpu.make_async_copy(table_ref, table, sems.at[0])
+    tables.start()
+    keep = pltpu.make_async_copy(p_ref.at[0 : keep_ref.shape[0], :], keep_ref, sems.at[1])
     keep.start()
-    for copy in tables:
-        copy.wait()
+    tables.wait()
+    ro, rw, do, dw = (table.at[k] for k in range(4))
 
     def put(quantity, i, j, value):
         x_ref[pl.ds(quantity * N * N + i * N + j, 8, SUMS), :] = value
@@ -169,10 +170,12 @@
 
 
 def rim_kernel(
-    ro_hbm, rw_hbm, do_hbm, dw_hbm, x_ref, p_ref, east_ref, west_ref, late_ref, south_ref, rw_ref, dw_ref, out_ref,
-    all_ref, ro, rw, do, dw, sems,
+    n_rows, n_cols, table_ref, x_ref, p_ref, east_ref, west_ref, late_ref, south_ref, out_ref, all_ref, table, sem
 ):
-    tables = fetch_tables((ro_hbm, rw_hbm, do_hbm, dw_hbm), (ro, rw, do, dw), sems)
+    tables = pltpu.make_async_copy(table_ref, table, sem)
+    tables.start()
+    ro, rw, do, dw = (table.at[k] for k in range(4))
+    r, c = lax.axis_index("row"), lax.axis_index("col")
     total = x_ref[0:SUMS, :]
     for k in range(1, 8):
         total = total + x_ref[k * SUMS : (k + 1) * SUMS, :]
@@ -191,12 +194,11 @@
             cross = a * pltpu.roll(b, HALF, 1)
             real = real + fold8(a * b)
             imag = imag + fold8(jnp.where(low, cross, -cross))
-        put(0, half + i, N - 1, real)
-        put(1, half + i, N - 1, imag)
-    for copy in tables:
-        copy.wait()
+        put(0, half + i, N - 1, jnp.where(c > 0, real, 0.0))
+        put(1, half + i, N - 1, jnp.where(c > 0, imag, 0.0))
+    tables.wait()
     for i in range(half):
-        o, w = ro[i, N - 1], rw[i, N - 1]
+        o, w = ro[i, N - 1], jnp.where(c < n_cols - 1, rw[i, N - 1], 0)
         turn = (o, other_half(o))
         sums = east_sums(
             lambda part, k: p_ref[pl.ds(plane(i, N - 1, part) + k, 32), :],
@@ -211,7 +213,7 @@
             lambda part, k: p_ref[pl.ds(plane(N - 1, j, part) + k, 8), :],
             lambda part, k: south_ref[pl.ds(PAD + (j * 2 + part) * HALF + k, 8), :],
             do[N - 1, j],
-            dw[N - 1, j],
+            jnp.where(r < n_rows - 1, dw[N - 1, j], 0),
         )
         put(2, N - 1, j, sums[0])
         put(3, N - 1, j, sums[1])
@@ -220,14 +222,14 @@
         ones, all_ref[...], (((1,), (1,)), ((), ())), precision=HIGHEST, preferred_element_type=jnp.float32
     )
 
-    def scale_of(width_ref):
-        width = width_ref[...].astype(jnp.float32)
+    def scale_of(k):
+        width = table_ref[k].astype(jnp.float32)
         factor = 1.0 / jnp.sqrt(SIDE * width)
         return jnp.concatenate([factor[k : k + 1, :] for k in range(N)] * 2, axis=1)
 
     foreign = west_slots(lanes((1, SIDE)))
-    east = sums[0:1, 0:SIDE] * jnp.where(foreign, 1.0, scale_of(rw_ref))
-    south = sums[0:1, SIDE : 2 * SIDE] * scale_of(dw_ref)
+    east = sums[0:1, 0:SIDE] * jnp.where(foreign, 1.0, scale_of(1))
+    south = sums[0:1, SIDE : 2 * SIDE] * scale_of(3)
     odd = lax.broadcasted_iota(jnp.int32, out_ref.shape, 0) % 2 == 1
     out_ref[...] = jnp.where(odd, south, east)
 
@@ -284,13 +286,15 @@
 
 
 def blend_kernel(
-    n_rows, n_cols, ro_hbm, rw_hbm, do_hbm, dw_hbm, g_ref, keep_ref, p_hbm, left_ref, late_ref, south_ref, out_hbm, phase_ref,
-    p_ref, east_ref, stage, all_ref, near_ref, fac, ro, rw, do, dw, sem, out_sem, sems,
+    n_rows, n_cols, table_ref, g_ref, keep_ref, p_hbm, left_ref, late_ref, south_ref, out_hbm, phase_ref,
+    p_ref, east_ref, stage, all_ref, near_ref, fac, table, sem, out_sem, sems,
 ):
     r, c = lax.axis_index("row"), lax.axis_index("col")
     for i in range(KEEP, N):
         fetch_row(p_hbm, p_ref, sems, i).start()
-    tables = fetch_tables((ro_hbm, rw_hbm, do_hbm, dw_hbm), (ro, rw, do, dw), sems.at[pl.ds(N + 2, 4)])
+    tables = pltpu.make_async_copy(table_ref, table, sems.at[N + 2])
+    tables.start()
+    ro, rw, do, dw = (table.at[k] for k in range(4))
     for i in range(KEEP):
         fetch_row(keep_ref, p_ref, sems, i).start()
     size = left_ref.shape[0]
@@ -371,7 +375,7 @@
             ).start()
 
     fetch_row(p_hbm, p_ref, sems, 0).wait()
-    for join in joins + tables:
+    for join in joins + [tables]:
         join.wait()
 
     def body(i, carry):
@@ -391,8 +395,7 @@
     flat_shape = (N * N * 2 * SIDE, SIDE)
     fixed = lambda x: pltpu.with_memory_space_constraint(x, pltpu.HBM)
     flat = patches.reshape(flat_shape)
-    pinned = [fixed(x) for x in tables]
-    table_scratch = [pltpu.SMEM((N, N), jnp.int32)] * 4
+    table_scratch = pltpu.SMEM((4, N, N), jnp.int32)
     south_shape = (2 * PAD + N * 2 * HALF, SIDE)
     vmem = pl.BlockSpec(memory_space=pltpu.VMEM)
     hbm = pl.BlockSpec(memory_space=pltpu.HBM)
@@ -405,55 +408,59 @@
         return pl.CostEstimate(flops=flops, bytes_accessed=moved, transcendentals=0)
 
     half = N // 2 * SIDE
-    left, right, late, lower = pl.pallas_call(
+    left, right, late, lower, table = pl.pallas_call(
         strip_kernel,
-        out_shape=(f32(half, SIDE), f32(half, SIDE), f32(half, SIDE), f32(*south_shape)),
-        in_specs=[hbm] * 3,
-        out_specs=(vmem,) * 4,
+        out_shape=(
+            *(f32(half, SIDE),) * 3,
+            f32(*south_shape),
+            jax.ShapeDtypeStruct((4, N, N), jnp.int32),
+        ),
+        in_specs=[hbm] * 5,
+        out_specs=(vmem,) * 5,
         scratch_shapes=[
             pltpu.VMEM((N, 2, SIDE, SIDE), jnp.float32),
             pltpu.VMEM((N // 2, 2, SIDE, SIDE), jnp.float32),
             pltpu.SMEM((N, N), jnp.int32),
             pltpu.SMEM((N, N), jnp.int32),
-            pltpu.SemaphoreType.DMA((5 + 2 * N,)),
+            pltpu.SemaphoreType.DMA((9 + 2 * N,)),
         ],
         compiler_params=params(8),
         cost_estimate=cost(400_000, 3_000_000),
         name="strips",
-    )(fixed(right_offset), fixed(right_width), fixed(patches))
-    to_left = [(k + 1, k) for k in range(n_cols - 1)]
+    )(*map(fixed, tables), fixed(patches))
+    to_left = [(k, (k - 1) % n_cols) for k in range(n_cols)]
     east_edge = lax.ppermute(left, "col", to_left)
-    west_edge = lax.ppermute(right, "col", [(k, k + 1) for k in range(n_cols - 1)])
+    west_edge = lax.ppermute(right, "col", [(k, (k + 1) % n_cols) for k in range(n_cols)])
     late_edge = lax.ppermute(late, "col", to_left)
-    south_edge = lax.ppermute(lower, "row", [(k + 1, k) for k in range(n_rows - 1)])
+    south_edge = lax.ppermute(lower, "row", [(k, (k - 1) % n_rows) for k in range(n_rows)])
 
     sums, keep = pl.pallas_call(
         inner_kernel,
         out_shape=(f32(8 * SUMS, SIDE), f32(KEEP * N * 2 * SIDE, SIDE)),
-        in_specs=[hbm] * 4 + [vmem],
+        in_specs=[vmem] * 2,
         out_specs=(vmem, vmem),
-        scratch_shapes=table_scratch + [pltpu.SemaphoreType.DMA((5,))],
+        scratch_shapes=[table_scratch, pltpu.SemaphoreType.DMA((2,))],
         compiler_params=params(16),
         cost_estimate=cost(20_000_000, 9_000_000),
         name="inner",
-    )(*pinned, flat)
+    )(table, flat)
 
     sent = pl.pallas_call(
-        rim_kernel,
+        functools.partial(rim_kernel, n_rows, n_cols),
         out_shape=f32(2 * n_dev, SIDE),
-        in_specs=[hbm] * 4 + [vmem] * 8,
+        in_specs=[vmem] * 7,
         out_specs=vmem,
-        scratch_shapes=[pltpu.VMEM((SUMS, SIDE), jnp.float32)] + table_scratch + [pltpu.SemaphoreType.DMA((4,))],
+        scratch_shapes=[pltpu.VMEM((SUMS, SIDE), jnp.float32), table_scratch, pltpu.SemaphoreType.DMA],
         compiler_params=params(16),
         cost_estimate=cost(5_000_000, 3_000_000),
         name="rim",
-    )(*pinned, sums, flat, east_edge, west_edge, late, south_edge, right_width, down_width)
+    )(table, sums, flat, east_edge, west_edge, late, south_edge)
     grid = lax.all_to_all(sent, ("row", "col"), 0, 0, tiled=True)
 
     blended, phases = pl.pallas_call(
         functools.partial(blend_kernel, n_rows, n_cols),
         out_shape=(f32(*flat_shape), f32(2, N, N)),
-        in_specs=[hbm] * 4 + [vmem, vmem, hbm, vmem, vmem, vmem],
+        in_specs=[hbm, vmem, vmem, hbm, vmem, vmem, vmem],
         out_specs=(hbm, vmem),
         scratch_shapes=[
             pltpu.VMEM(flat_shape, jnp.float32),
@@ -462,15 +469,15 @@
             pltpu.VMEM((n_dev, SIDE), jnp.float32),
             pltpu.VMEM((8, SIDE), jnp.float32),
             pltpu.SMEM((8, SIDE), jnp.float32),
-            *table_scratch,
+            table_scratch,
             pltpu.SemaphoreType.DMA,
             pltpu.SemaphoreType.DMA,
-            pltpu.SemaphoreType.DMA((N + 6,)),
+            pltpu.SemaphoreType.DMA((N + 3,)),
         ],
         compiler_params=params(32),
         cost_estimate=cost(30_000_000, 10_000_000),
         name="blend",
-    )(*pinned, grid, keep, fixed(flat), east_edge, late_edge, south_edge)
+    )(fixed(table), grid, keep, fixed(flat), east_edge, late_edge, south_edge)
     return blended.reshape(patches.shape), phases
 
 

time: 51.5 us -> 45.6 us (0.89)
  starting transfers between devices: 23.7 us -> 19.1 us
  Pallas kernels: 16.4 us -> 15.4 us
    all_to_all x1, starting transfers between devices: 13.5 us -> 6.82 us  [local(): grid = lax.all_to_all(sent, ('row', 'col'), 0, 0, tiled=True)]
    ppermute x2, starting transfers between devices: 7.6 us -> 1.44 us  [the longest x1 1.43 us: local(): lax.ppermute(lower, 'row', [(k, (k - 1) % n_rows) for k in range(n_rows)])]
    ppermute x1, starting transfers between devices: 1.29 us -> 6.04 us  [local(): east_edge = lax.ppermute(left, 'col', to_left)]
    ppermute x1, starting transfers between devices: 1.29 us -> 4.78 us  [local(): late_edge = lax.ppermute(late, 'col', to_left)]
    pallas_call x2, Pallas kernels: 4.92 us -> 4.12 us  [the longest x1 2.17 us: local(): pl.pallas_call(functools.partial(rim_kernel, n_rows, n_cols), out_shape=f...]
where the time goes in v5:
time: 45.6 us; the launch traced here: 45.5 us
  starting transfers between devices  19.1 us (42%)
  Pallas kernels  15.4 us (34%)
  waiting for transfers between devices  10.2 us (22%)
  between operations  0.72 us (2%)
    all_to_all x1, waiting for transfers between devices, local(): grid = lax.all_to_all(sent, ('row', 'col'), 0, 0, tiled=True)  10.2 us
    all_to_all x1, starting transfers between devices, local(): grid = lax.all_to_all(sent, ('row', 'col'), 0, 0, tiled=True)  6.82 us
    pallas_call x1, Pallas kernels, local(): pl.pallas_call(functools.partial(blend_kernel, n_rows, n_cols), out_shape...  6.66 us
    ppermute x1, starting transfers between devices, local(): east_edge = lax.ppermute(left, 'col', to_left)  6.04 us
    ppermute x1, starting transfers between devices, local(): late_edge = lax.ppermute(late, 'col', to_left)  4.78 us
    pallas_call x1, Pallas kernels, local(): pl.pallas_call(inner_kernel, out_shape=(f32(8 * SUMS, SIDE), f32(KEEP * N...  4.64 us
    pallas_call x1, Pallas kernels, local(): pl.pallas_call(functools.partial(rim_kernel, n_rows, n_cols), out_shape=f...  2.17 us
    pallas_call x1, Pallas kernels, local(): pl.pallas_call(strip_kernel, out_shape=(*(f32(half, SIDE),) * 3, f32(*sou...  1.95 us
  transfers between devices with their start and end apart: 5, of which 1 were waited for; matrix products, arithmetic and copies ran while one was open for 0% of the time, Pallas kernels for 15%

profile of v5, /device:TPU:1, one launch (start us, length us, event | category | flops | bytes accessed | tf_op | source)
XLA Modules:
  0.0 45.5 jit_solution(4899092993821194052)
XLA Ops:
  0.6 0.0 copy-start
  0.6 1.9 %strips.1 = (f32[512,128]{1,0:T(8,128)S(1)}, f32[512,128]{1,0:T(8,128)S(1)}, f32[512,128]{1,0:T(8,128)S(1)}, f32[1040,128]{1,0:T(8,128)S(1)}, s32[4,8,8]{2,1,0:T(8,128)S(1)}) custom-call(s32[8,8]{1,0:T(8,128)} %ro_hbm.1, s32[8,8]{1,0:T(8,128)} %rw_hbm.1, s32[8,8]{1,0:T(8,128)} %do_hbm.1, s32[8,8]{1,0:T(8,128)} %dw_hbm.1, f32[8,8,2,128,128]{4,3,2,1,0:T(8,128)} %p_hbm.1), custom_call_target="tpu_custom_call" | custom-call | flops 400000 | bytes 3000000 | tf_op jit(solution)/shard_map/strips/pallas_call | solution.py:411
  2.6 0.0 copy-start.1
  2.6 1.4 %collective-permute-start.2 = (f32[1040,128]{1,0:T(8,128)S(1)}, f32[1040,128]{1,0:T(8,128)S(1)}, u32[]{:S(2)}, u32[]{:S(2)}) collective-permute-start(f32[1040,128]{1,0:T(8,128)S(1)} %get-tuple-element.16), channel_id=1, source_target_pairs={{0,112},{16,0},{32,16},{48,32},{64,48},{80,64},{96,80},{112,96},{1... | collective-permute-start | bytes 1597448 | tf_op jit(solution)/shard_map/ppermute | solution.py:435
  4.0 6.0 %collective-permute-start = (f32[512,128]{1,0:T(8,128)S(1)}, f32[512,128]{1,0:T(8,128)S(1)}, u32[]{:S(2)}, u32[]{:S(2)}) collective-permute-start(f32[512,128]{1,0:T(8,128)S(1)} %get-tuple-element.13), channel_id=1, source_target_pairs={{0,15},{1,0},{2,1},{3,2},{4,3},{5,4},{6,5},{7,6},{8,7},{9,8},{10,9... | collective-permute-start | bytes 786440 | tf_op jit(solution)/shard_map/ppermute | solution.py:432
  10.1 0.0 collective-permute-start.1
  10.1 4.8 %collective-permute-start.3 = (f32[512,128]{1,0:T(8,128)S(1)}, f32[512,128]{1,0:T(8,128)S(1)}, u32[]{:S(2)}, u32[]{:S(2)}) collective-permute-start(f32[512,128]{1,0:T(8,128)S(1)} %get-tuple-element.15.late_ref), channel_id=1, source_target_pairs={{0,15},{1,0},{2,1},{3,2},{4,3},{5,4},{6,5},{7,6},{8,7},{9,8},{10,9... | collective-permute-start | bytes 786440 | tf_op jit(solution)/shard_map/ppermute | solution.py:434
  14.9 0.0 copy-done
  14.9 4.6 %inner.1 = (f32[2048,128]{1,0:T(8,128)S(1)}, f32[4096,128]{1,0:T(8,128)S(1)}) custom-call(s32[4,8,8]{2,1,0:T(8,128)S(1)} %get-tuple-element.11.table_ref, f32[16384,128]{1,0:T(8,128)S(1)} %bitcast.5), custom_call_target="tpu_custom_call" | custom-call | flops 20000000 | bytes 9000000 | tf_op jit(solution)/shard_map/inner/pallas_call | solution.py:437
  19.5 0.0 collective-permute-done.east_ref.left_ref
  19.5 0.0 collective-permute-done.1.west_ref
  19.5 0.0 collective-permute-done.2.south_ref
  19.6 2.2 %rim.1 = f32[256,128]{1,0:T(8,128)} custom-call(s32[4,8,8]{2,1,0:T(8,128)S(1)} %get-tuple-element.11.table_ref, f32[2048,128]{1,0:T(8,128)S(1)} %get-tuple-element.12.x_ref, f32[16384,128]{1,0:T(8,128)S(1)} %bitcast.6, f32[512,128]{1,0:T(8,128)S(1)} %collective-permute-done.east_ref.left_ref, f32[512,128]{1,0:T(8,128)S(1)} %collective-permute-done.1.west_ref, ...), custom_call_target="tpu_custom_call" | custom-call | flops 5000000 | bytes 3000000 | tf_op jit(solution)/shard_map/rim/pallas_call | solution.py:448
  21.7 0.0 copy-done.1
  21.7 6.8 %all-to-all-start = ((f32[128,2,128]{2,1,0:T(2,128)}), f32[128,2,128]{2,1,0:T(2,128)S(1)}, u32[]{:S(2)}, u32[]{:S(2)}) async-start(f32[128,2,128]{2,1,0:T(2,128)} %bitcast.1), calls=%async_computation | async-start | bytes 262144 | tf_op jit(solution)/shard_map/all_to_all | solution.py:458
  28.6 0.0 collective-permute-done.3.late_ref
  28.6 10.2 %all-to-all-done = f32[128,2,128]{2,1,0:T(2,128)S(1)} async-done(((f32[128,2,128]{2,1,0:T(2,128)}), f32[128,2,128]{2,1,0:T(2,128)S(1)}, u32[]{:S(2)}, u32[]{:S(2)}) %all-to-all-start) | async-done | bytes 131104 | tf_op jit(solution)/shard_map/all_to_all | solution.py:458
  38.8 6.7 %blend.1 = (f32[16384,128]{1,0:T(8,128)}, f32[2,8,8]{2,1,0:T(8,128)}) custom-call(s32[4,8,8]{2,1,0:T(8,128)} %copy-done.1, f32[256,128]{1,0:T(8,128)S(1)} %bitcast.7, f32[4096,128]{1,0:T(8,128)S(1)} %get-tuple-element.17.keep_ref, f32[16384,128]{1,0:T(8,128)} %bitcast.4, f32[512,128]{1,0:T(8,128)S(1)} %collective-permute-done.east_ref.left_ref, ...), custom_call_target="tpu_custom_call" | custom-call | flops 30000000 | bytes 10000000 | tf_op jit(solution)/shard_map/blend/pallas_call | solution.py:460
Async XLA Ops:
  0.6 14.2 %copy-start = (f32[8,8,2,128,128]{4,3,2,1,0:T(8,128)S(1)}, f32[8,8,2,128,128]{4,3,2,1,0:T(8,128)}, u32[]{:S(2)}) copy-start(f32[8,8,2,128,128]{4,3,2,1,0:T(8,128)} %p_hbm.1) | copy-start | bytes 25165828
  2.6 19.1 %copy-start.1 = (s32[4,8,8]{2,1,0:T(8,128)}, s32[4,8,8]{2,1,0:T(8,128)S(1)}, u32[]{:S(2)}) copy-start(s32[4,8,8]{2,1,0:T(8,128)S(1)} %get-tuple-element.11.table_ref) | copy-start | bytes 3076
  2.6 16.9 %collective-permute-start.2 = (f32[1040,128]{1,0:T(8,128)S(1)}, f32[1040,128]{1,0:T(8,128)S(1)}, u32[]{:S(2)}, u32[]{:S(2)}) collective-permute-start(f32[1040,128]{1,0:T(8,128)S(1)} %get-tuple-element.16), channel_id=1, source_target_pairs={{0,112},{16,0},{32,16},{48,32},{64,48},{80,64},{96,80},{112,96},{1... | collective-permute-start | bytes 1597448 | tf_op jit(solution)/shard_map/ppermute | solution.py:435
  4.0 15.5 %collective-permute-start = (f32[512,128]{1,0:T(8,128)S(1)}, f32[512,128]{1,0:T(8,128)S(1)}, u32[]{:S(2)}, u32[]{:S(2)}) collective-permute-start(f32[512,128]{1,0:T(8,128)S(1)} %get-tuple-element.13), channel_id=1, source_target_pairs={{0,15},{1,0},{2,1},{3,2},{4,3},{5,4},{6,5},{7,6},{8,7},{9,8},{10,9... | collective-permute-start | bytes 786440 | tf_op jit(solution)/shard_map/ppermute | solution.py:432
  10.1 9.5 %collective-permute-start.1 = (f32[512,128]{1,0:T(8,128)S(1)}, f32[512,128]{1,0:T(8,128)S(1)}, u32[]{:S(2)}, u32[]{:S(2)}) collective-permute-start(f32[512,128]{1,0:T(8,128)S(1)} %get-tuple-element.14), channel_id=1, source_target_pairs={{0,1},{1,2},{2,3},{3,4},{4,5},{5,6},{6,7},{7,8},{8,9},{9,10},{10,1... | collective-permute-start | bytes 786440 | tf_op jit(solution)/shard_map/ppermute | solution.py:433
  10.1 18.5 %collective-permute-start.3 = (f32[512,128]{1,0:T(8,128)S(1)}, f32[512,128]{1,0:T(8,128)S(1)}, u32[]{:S(2)}, u32[]{:S(2)}) collective-permute-start(f32[512,128]{1,0:T(8,128)S(1)} %get-tuple-element.15.late_ref), channel_id=1, source_target_pairs={{0,15},{1,0},{2,1},{3,2},{4,3},{5,4},{6,5},{7,6},{8,7},{9,8},{10,9... | collective-permute-start | bytes 786440 | tf_op jit(solution)/shard_map/ppermute | solution.py:434
  21.7 17.1 %all-to-all-start = ((f32[128,2,128]{2,1,0:T(2,128)}), f32[128,2,128]{2,1,0:T(2,128)S(1)}, u32[]{:S(2)}, u32[]{:S(2)}) async-start(f32[128,2,128]{2,1,0:T(2,128)} %bitcast.1), calls=%async_computation | async-start | bytes 262144 | tf_op jit(solution)/shard_map/all_to_all | solution.py:458

commit v6 on v5

--- a/solution.py
+++ b/solution.py
@@ -14,6 +14,7 @@
 ROW0 = 56
 PAD = 8
 KEEP = 2
+SPLIT = 3
 N = 8
 SUMS = 4 * N * N
 HIGHEST = lax.Precision.HIGHEST
@@ -35,7 +36,7 @@
 
 
 def west_slots(lane):
-    return (lane % N == N - 1) & ((lane // N) % N >= N // 2)
+    return (lane % N == N - 1) & ((lane // N) % N >= SPLIT)
 
 
 def other_half(o):
@@ -75,13 +76,12 @@
 def strip_kernel(
     ro_hbm, rw_hbm, do_hbm, dw_hbm, p_hbm, left_ref, right_ref, late_ref, south_ref, table_ref, first, last, ro, rw, sems
 ):
-    half = N // 2
     copies = [
         pltpu.make_async_copy(ro_hbm, ro, sems.at[0]),
         pltpu.make_async_copy(rw_hbm, rw, sems.at[1]),
-        pltpu.make_async_copy(p_hbm.at[0:half, 0], first.at[0:half], sems.at[2]),
-        pltpu.make_async_copy(p_hbm.at[half:N, N - 1], last, sems.at[3]),
-        pltpu.make_async_copy(p_hbm.at[half:N, 0], first.at[half:N], sems.at[4]),
+        pltpu.make_async_copy(p_hbm.at[0:SPLIT, 0], first.at[0:SPLIT], sems.at[2]),
+        pltpu.make_async_copy(p_hbm.at[SPLIT:N, N - 1], last, sems.at[3]),
+        pltpu.make_async_copy(p_hbm.at[SPLIT:N, 0], first.at[SPLIT:N], sems.at[4]),
     ]
     for copy in copies:
         copy.start()
@@ -109,21 +109,21 @@
         return jnp.where(low, first[i, 0], pltpu.roll(first[i, 1], HALF, 1))
 
     copies[2].wait()
-    for i in range(half):
+    for i in range(SPLIT):
         left_ref[i * SIDE : (i + 1) * SIDE, :] = pack(i)
     copies[0].wait()
     copies[1].wait()
     copies[3].wait()
-    for i in range(half):
-        o, w = ro[half + i, N - 1], rw[half + i, N - 1]
+    for i in range(N - SPLIT):
+        o, w = ro[SPLIT + i, N - 1], rw[SPLIT + i, N - 1]
         scale = 1.0 / jnp.sqrt(SIDE * jnp.full((1, SIDE), w).astype(jnp.float32))
         real = pltpu.roll(last[i, 0], SIDE - o, 1)
         imag = pltpu.roll(last[i, 1], other_half(SIDE - o), 1)
         both = jnp.where(low, real, imag) * scale
         right_ref[i * SIDE : (i + 1) * SIDE, :] = jnp.where(lane % HALF < w, both, 0.0)
     copies[4].wait()
-    for i in range(half):
-        late_ref[i * SIDE : (i + 1) * SIDE, :] = pack(half + i)
+    for i in range(N - SPLIT):
+        late_ref[i * SIDE : (i + 1) * SIDE, :] = pack(SPLIT + i)
     for copy in rows:
         copy.wait()
 
@@ -185,19 +185,18 @@
         at = quantity * N * N + i * N + j
         all_ref[at : at + 1, :] = jnp.sum(value, axis=0, keepdims=True)
 
-    half = N // 2
     low = lanes((32, SIDE)) < HALF
-    for i in range(half):
+    for i in range(N - SPLIT):
         real, imag = jnp.zeros((8, SIDE), jnp.float32), jnp.zeros((8, SIDE), jnp.float32)
         for k in range(i * SIDE, (i + 1) * SIDE, 32):
             a, b = west_ref[k : k + 32, :], late_ref[k : k + 32, :]
             cross = a * pltpu.roll(b, HALF, 1)
             real = real + fold8(a * b)
             imag = imag + fold8(jnp.where(low, cross, -cross))
-        put(0, half + i, N - 1, jnp.where(c > 0, real, 0.0))
-        put(1, half + i, N - 1, jnp.where(c > 0, imag, 0.0))
+        put(0, SPLIT + i, N - 1, jnp.where(c > 0, real, 0.0))
+        put(1, SPLIT + i, N - 1, jnp.where(c > 0, imag, 0.0))
     tables.wait()
-    for i in range(half):
+    for i in range(SPLIT):
         o, w = ro[i, N - 1], jnp.where(c < n_cols - 1, rw[i, N - 1], 0)
         turn = (o, other_half(o))
         sums = east_sums(
@@ -299,8 +298,8 @@
         fetch_row(keep_ref, p_ref, sems, i).start()
     size = left_ref.shape[0]
     joins = [
-        pltpu.make_async_copy(ref, east_ref.at[k * size : (k + 1) * size, :], sems.at[N + k])
-        for k, ref in enumerate((left_ref, late_ref))
+        pltpu.make_async_copy(left_ref, east_ref.at[0:size, :], sems.at[N]),
+        pltpu.make_async_copy(late_ref, east_ref.at[size : N * SIDE, :], sems.at[N + 1]),
     ]
     for join in joins:
         join.start()
@@ -407,11 +406,13 @@
     def cost(flops, moved):
         return pl.CostEstimate(flops=flops, bytes_accessed=moved, transcendentals=0)
 
-    half = N // 2 * SIDE
+    near, far = SPLIT * SIDE, (N - SPLIT) * SIDE
     left, right, late, lower, table = pl.pallas_call(
         strip_kernel,
         out_shape=(
-            *(f32(half, SIDE),) * 3,
+            f32(near, SIDE),
+            f32(far, SIDE),
+            f32(far, SIDE),
             f32(*south_shape),
             jax.ShapeDtypeStruct((4, N, N), jnp.int32),
         ),
@@ -419,7 +420,7 @@
         out_specs=(vmem,) * 5,
         scratch_shapes=[
             pltpu.VMEM((N, 2, SIDE, SIDE), jnp.float32),
-            pltpu.VMEM((N // 2, 2, SIDE, SIDE), jnp.float32),
+            pltpu.VMEM((N - SPLIT, 2, SIDE, SIDE), jnp.float32),
             pltpu.SMEM((N, N), jnp.int32),
             pltpu.SMEM((N, N), jnp.int32),
             pltpu.SemaphoreType.DMA((9 + 2 * N,)),
@@ -431,7 +432,6 @@
     to_left = [(k, (k - 1) % n_cols) for k in range(n_cols)]
     east_edge = lax.ppermute(left, "col", to_left)
     west_edge = lax.ppermute(right, "col", [(k, (k + 1) % n_cols) for k in range(n_cols)])
-    late_edge = lax.ppermute(late, "col", to_left)
     south_edge = lax.ppermute(lower, "row", [(k, (k - 1) % n_rows) for k in range(n_rows)])
 
     sums, keep = pl.pallas_call(
@@ -455,6 +455,8 @@
         cost_estimate=cost(5_000_000, 3_000_000),
         name="rim",
     )(table, sums, flat, east_edge, west_edge, late, south_edge)
+    late_out, sent = lax.optimization_barrier((late, sent))
+    late_edge = lax.ppermute(late_out, "col", to_left)
     grid = lax.all_to_all(sent, ("row", "col"), 0, 0, tiled=True)
 
     blended, phases = pl.pallas_call(

time: 45.6 us -> 44.3 us (0.971)
  blocking collectives: 0 us -> 17.1 us
  waiting for transfers between devices: 10.2 us -> 0.9 us
  starting transfers between devices: 19.1 us -> 10.4 us
    all_to_all x0 -> x1, blocking collectives: none -> 17.1 us  [local(): grid = lax.all_to_all(sent, ('row', 'col'), 0, 0, tiled=True)]
    all_to_all x1 -> x0, waiting for transfers between devices: 10.2 us -> none  [local(): grid = lax.all_to_all(sent, ('row', 'col'), 0, 0, tiled=True)]
    all_to_all x1 -> x0, starting transfers between devices: 6.82 us -> none  [local(): grid = lax.all_to_all(sent, ('row', 'col'), 0, 0, tiled=True)]
    ppermute x1, starting transfers between devices: 4.78 us -> 2.93 us  [local(): late_edge = lax.ppermute(late_out, 'col', to_left)]
    ppermute x1, starting transfers between devices: 6.04 us -> 4.74 us  [local(): east_edge = lax.ppermute(left, 'col', to_left)]
    ppermute x1, starting transfers between devices: 0.01 us -> 1.29 us  [local(): lax.ppermute(right, 'col', [(k, (k + 1) % n_cols) for k in range(n_cols)])]
    ppermute x1, waiting for transfers between devices: 0.01 us -> 0.9 us  [local(): lax.ppermute(right, 'col', [(k, (k + 1) % n_cols) for k in range(n_cols)])]
    pallas_call x1, Pallas kernels: 2.17 us -> 1.47 us  [local(): pl.pallas_call(functools.partial(rim_kernel, n_rows, n_cols), out_shape=f...]
  transfers between devices with their start and end apart: 5 -> 4, of which waited for: 1 -> 1; matrix products, arithmetic and copies ran while one was open for 0% -> 0% of each run, Pallas kernels for 15% -> 11%
where the time goes in v6:
time: 44.3 us; the launch traced here: 44.2 us
  blocking collectives  17.1 us (39%)
  Pallas kernels  15.1 us (34%)
  starting transfers between devices  10.4 us (23%)
  waiting for transfers between devices  0.9 us (2%)
  between operations  0.69 us (2%)
    all_to_all x1, blocking collectives, local(): grid = lax.all_to_all(sent, ('row', 'col'), 0, 0, tiled=True)  17.1 us
    pallas_call x1, Pallas kernels, local(): pl.pallas_call(functools.partial(blend_kernel, n_rows, n_cols), out_shape...  6.98 us
    ppermute x1, starting transfers between devices, local(): east_edge = lax.ppermute(left, 'col', to_left)  4.74 us
    pallas_call x1, Pallas kernels, local(): pl.pallas_call(inner_kernel, out_shape=(f32(8 * SUMS, SIDE), f32(KEEP * N...  4.64 us
    ppermute x1, starting transfers between devices, local(): late_edge = lax.ppermute(late_out, 'col', to_left)  2.93 us
    pallas_call x1, Pallas kernels, local(): pl.pallas_call(strip_kernel, out_shape=(f32(near, SIDE), f32(far, SIDE),...  2.01 us
    pallas_call x1, Pallas kernels, local(): pl.pallas_call(functools.partial(rim_kernel, n_rows, n_cols), out_shape=f...  1.47 us
    ppermute x1, starting transfers between devices, local(): lax.ppermute(lower, 'row', [(k, (k - 1) % n_rows) for k in range(n_rows)])  1.43 us
  transfers between devices with their start and end apart: 4, of which 1 were waited for; matrix products, arithmetic and copies ran while one was open for 0% of the time, Pallas kernels for 11%

profile of v6, /device:TPU:1, one launch (start us, length us, event | category | flops | bytes accessed | tf_op | source)
XLA Modules:
  0.0 44.2 jit_solution(17183935784755550857)
XLA Ops:
  0.6 0.0 copy-start
  0.6 2.0 %strips.1 = (f32[384,128]{1,0:T(8,128)S(1)}, f32[640,128]{1,0:T(8,128)S(1)}, f32[640,128]{1,0:T(8,128)S(1)}, f32[1040,128]{1,0:T(8,128)S(1)}, s32[4,8,8]{2,1,0:T(8,128)S(1)}) custom-call(s32[8,8]{1,0:T(8,128)} %ro_hbm.1, s32[8,8]{1,0:T(8,128)} %rw_hbm.1, s32[8,8]{1,0:T(8,128)} %do_hbm.1, s32[8,8]{1,0:T(8,128)} %dw_hbm.1, f32[8,8,2,128,128]{4,3,2,1,0:T(8,128)} %p_hbm.1), custom_call_target="tpu_custom_call" | custom-call | flops 400000 | bytes 3000000 | tf_op jit(solution)/shard_map/strips/pallas_call | solution.py:410
  2.7 0.0 copy-start.1
  2.7 1.4 %collective-permute-start.2 = (f32[1040,128]{1,0:T(8,128)S(1)}, f32[1040,128]{1,0:T(8,128)S(1)}, u32[]{:S(2)}, u32[]{:S(2)}) collective-permute-start(f32[1040,128]{1,0:T(8,128)S(1)} %get-tuple-element.18), channel_id=1, source_target_pairs={{0,112},{16,0},{32,16},{48,32},{64,48},{80,64},{96,80},{112,96},{1... | collective-permute-start | bytes 1597448 | tf_op jit(solution)/shard_map/ppermute | solution.py:435
  4.1 1.3 %collective-permute-start.1 = (f32[640,128]{1,0:T(8,128)S(1)}, f32[640,128]{1,0:T(8,128)S(1)}, u32[]{:S(2)}, u32[]{:S(2)}) collective-permute-start(f32[640,128]{1,0:T(8,128)S(1)} %get-tuple-element.17), channel_id=1, source_target_pairs={{0,1},{1,2},{2,3},{3,4},{4,5},{5,6},{6,7},{7,8},{8,9},{9,10},{10,1... | collective-permute-start | bytes 983048 | tf_op jit(solution)/shard_map/ppermute | solution.py:434
  5.4 4.7 %collective-permute-start = (f32[384,128]{1,0:T(8,128)S(1)}, f32[384,128]{1,0:T(8,128)S(1)}, u32[]{:S(2)}, u32[]{:S(2)}) collective-permute-start(f32[384,128]{1,0:T(8,128)S(1)} %get-tuple-element.16), channel_id=1, source_target_pairs={{0,15},{1,0},{2,1},{3,2},{4,3},{5,4},{6,5},{7,6},{8,7},{9,8},{10,9... | collective-permute-start | bytes 589832 | tf_op jit(solution)/shard_map/ppermute | solution.py:433
  10.1 0.0 copy-done
  10.1 4.6 %inner.1 = (f32[2048,128]{1,0:T(8,128)S(1)}, f32[4096,128]{1,0:T(8,128)S(1)}) custom-call(s32[4,8,8]{2,1,0:T(8,128)S(1)} %get-tuple-element.13.table_ref, f32[16384,128]{1,0:T(8,128)S(1)} %bitcast.5), custom_call_target="tpu_custom_call" | custom-call | flops 20000000 | bytes 9000000 | tf_op jit(solution)/shard_map/inner/pallas_call | solution.py:437
  14.8 0.0 collective-permute-done.east_ref.left_ref
  14.8 0.9 %collective-permute-done.1.west_ref = f32[640,128]{1,0:T(8,128)S(1)} collective-permute-done((f32[640,128]{1,0:T(8,128)S(1)}, f32[640,128]{1,0:T(8,128)S(1)}, u32[]{:S(2)}, u32[]{:S(2)}) %collective-permute-start.1) | collective-permute-done | bytes 327712 | tf_op jit(solution)/shard_map/ppermute | solution.py:434
  15.7 0.0 collective-permute-done.2.south_ref
  15.7 1.5 %rim.1 = f32[256,128]{1,0:T(8,128)S(1)} custom-call(s32[4,8,8]{2,1,0:T(8,128)S(1)} %get-tuple-element.13.table_ref, f32[2048,128]{1,0:T(8,128)S(1)} %get-tuple-element.15.x_ref, f32[16384,128]{1,0:T(8,128)S(1)} %bitcast.6, f32[384,128]{1,0:T(8,128)S(1)} %collective-permute-done.east_ref.left_ref, f32[640,128]{1,0:T(8,128)S(1)} %collective-permute-done.1.west_ref, ...), custom_call_target="tpu_custom_call" | custom-call | flops 5000000 | bytes 3000000 | tf_op jit(solution)/shard_map/rim/pallas_call | solution.py:448
  17.2 0.0 copy-done.1
  17.2 2.9 %collective-permute-start.3 = (f32[640,128]{1,0:T(8,128)S(1)}, f32[640,128]{1,0:T(8,128)S(1)}, u32[]{:S(2)}, u32[]{:S(2)}) collective-permute-start(f32[640,128]{1,0:T(8,128)S(1)} %get-tuple-element.21.late_ref), channel_id=1, source_target_pairs={{0,15},{1,0},{2,1},{3,2},{4,3},{5,4},{6,5},{7,6},{8,7},{9,8},{10,9... | collective-permute-start | bytes 983048 | tf_op jit(solution)/shard_map/ppermute | solution.py:459
  20.1 17.1 %all_to_all.11 = f32[128,2,128]{2,1,0:T(2,128)S(1)} all-to-all(f32[128,2,128]{2,1,0:T(2,128)S(1)} %bitcast.8), channel_id=1, replica_groups=mesh['row'=8,'col'=16] {'row','col'}, dimensions={0} | all-to-all | bytes 262144 | tf_op jit(solution)/shard_map/all_to_all | solution.py:460
  37.2 0.0 collective-permute-done.3.late_ref
  37.2 7.0 %blend.1 = (f32[16384,128]{1,0:T(8,128)}, f32[2,8,8]{2,1,0:T(8,128)}) custom-call(s32[4,8,8]{2,1,0:T(8,128)} %copy-done.1, f32[256,128]{1,0:T(8,128)S(1)} %bitcast.7, f32[4096,128]{1,0:T(8,128)S(1)} %get-tuple-element.20.keep_ref, f32[16384,128]{1,0:T(8,128)} %bitcast.4, f32[384,128]{1,0:T(8,128)S(1)} %collective-permute-done.east_ref.left_ref, ...), custom_call_target="tpu_custom_call" | custom-call | flops 30000000 | bytes 10000000 | tf_op jit(solution)/shard_map/blend/pallas_call | solution.py:462
Async XLA Ops:
  0.6 9.5 %copy-start = (f32[8,8,2,128,128]{4,3,2,1,0:T(8,128)S(1)}, f32[8,8,2,128,128]{4,3,2,1,0:T(8,128)}, u32[]{:S(2)}) copy-start(f32[8,8,2,128,128]{4,3,2,1,0:T(8,128)} %p_hbm.1) | copy-start | bytes 25165828
  2.7 14.5 %copy-start.1 = (s32[4,8,8]{2,1,0:T(8,128)}, s32[4,8,8]{2,1,0:T(8,128)S(1)}, u32[]{:S(2)}) copy-start(s32[4,8,8]{2,1,0:T(8,128)S(1)} %get-tuple-element.13.table_ref) | copy-start | bytes 3076
  2.7 13.0 %collective-permute-start.2 = (f32[1040,128]{1,0:T(8,128)S(1)}, f32[1040,128]{1,0:T(8,128)S(1)}, u32[]{:S(2)}, u32[]{:S(2)}) collective-permute-start(f32[1040,128]{1,0:T(8,128)S(1)} %get-tuple-element.18), channel_id=1, source_target_pairs={{0,112},{16,0},{32,16},{48,32},{64,48},{80,64},{96,80},{112,96},{1... | collective-permute-start | bytes 1597448 | tf_op jit(solution)/shard_map/ppermute | solution.py:435
  4.1 11.6 %collective-permute-start.1 = (f32[640,128]{1,0:T(8,128)S(1)}, f32[640,128]{1,0:T(8,128)S(1)}, u32[]{:S(2)}, u32[]{:S(2)}) collective-permute-start(f32[640,128]{1,0:T(8,128)S(1)} %get-tuple-element.17), channel_id=1, source_target_pairs={{0,1},{1,2},{2,3},{3,4},{4,5},{5,6},{6,7},{7,8},{8,9},{9,10},{10,1... | collective-permute-start | bytes 983048 | tf_op jit(solution)/shard_map/ppermute | solution.py:434
  5.4 9.4 %collective-permute-start = (f32[384,128]{1,0:T(8,128)S(1)}, f32[384,128]{1,0:T(8,128)S(1)}, u32[]{:S(2)}, u32[]{:S(2)}) collective-permute-start(f32[384,128]{1,0:T(8,128)S(1)} %get-tuple-element.16), channel_id=1, source_target_pairs={{0,15},{1,0},{2,1},{3,2},{4,3},{5,4},{6,5},{7,6},{8,7},{9,8},{10,9... | collective-permute-start | bytes 589832 | tf_op jit(solution)/shard_map/ppermute | solution.py:433
  17.2 20.0 %collective-permute-start.3 = (f32[640,128]{1,0:T(8,128)S(1)}, f32[640,128]{1,0:T(8,128)S(1)}, u32[]{:S(2)}, u32[]{:S(2)}) collective-permute-start(f32[640,128]{1,0:T(8,128)S(1)} %get-tuple-element.21.late_ref), channel_id=1, source_target_pairs={{0,15},{1,0},{2,1},{3,2},{4,3},{5,4},{6,5},{7,6},{8,7},{9,8},{10,9... | collective-permute-start | bytes 983048 | tf_op jit(solution)/shard_map/ppermute | solution.py:459

commit v7 on v6

--- a/solution.py
+++ b/solution.py
@@ -74,19 +74,18 @@
 
 
 def strip_kernel(
-    ro_hbm, rw_hbm, do_hbm, dw_hbm, p_hbm, left_ref, right_ref, late_ref, south_ref, table_ref, first, last, ro, rw, sems
+    ro_hbm, rw_hbm, do_hbm, dw_hbm, p_hbm, left_ref, right_ref, south_ref, table_ref, first, last, ro, rw, sems
 ):
     copies = [
         pltpu.make_async_copy(ro_hbm, ro, sems.at[0]),
         pltpu.make_async_copy(rw_hbm, rw, sems.at[1]),
         pltpu.make_async_copy(p_hbm.at[0:SPLIT, 0], first.at[0:SPLIT], sems.at[2]),
         pltpu.make_async_copy(p_hbm.at[SPLIT:N, N - 1], last, sems.at[3]),
-        pltpu.make_async_copy(p_hbm.at[SPLIT:N, 0], first.at[SPLIT:N], sems.at[4]),
     ]
     for copy in copies:
         copy.start()
     rows = [
-        pltpu.make_async_copy(ref, table_ref.at[k], sems.at[5 + 2 * N + k])
+        pltpu.make_async_copy(ref, table_ref.at[k], sems.at[4 + 2 * N + k])
         for k, ref in enumerate((ro_hbm, rw_hbm, do_hbm, dw_hbm))
     ]
     for copy in rows:
@@ -95,7 +94,7 @@
         for part in range(2):
             at = PAD + (j * 2 + part) * HALF
             copy = pltpu.make_async_copy(
-                p_hbm.at[0, j, part, 0:HALF, :], south_ref.at[at : at + HALF, :], sems.at[5 + j * 2 + part]
+                p_hbm.at[0, j, part, 0:HALF, :], south_ref.at[at : at + HALF, :], sems.at[4 + j * 2 + part]
             )
             copy.start()
             rows.append(copy)
@@ -121,18 +120,20 @@
         imag = pltpu.roll(last[i, 1], other_half(SIDE - o), 1)
         both = jnp.where(low, real, imag) * scale
         right_ref[i * SIDE : (i + 1) * SIDE, :] = jnp.where(lane % HALF < w, both, 0.0)
-    copies[4].wait()
-    for i in range(N - SPLIT):
-        late_ref[i * SIDE : (i + 1) * SIDE, :] = pack(SPLIT + i)
     for copy in rows:
         copy.wait()
 
 
-def inner_kernel(table_ref, p_ref, x_ref, keep_ref, table, sems):
+def inner_kernel(table_ref, p_ref, sum_ref, keep_ref, late_ref, x_ref, table, sems):
     tables = pltpu.make_async_copy(table_ref, table, sems.at[0])
     tables.start()
     keep = pltpu.make_async_copy(p_ref.at[0 : keep_ref.shape[0], :], keep_ref, sems.at[1])
     keep.start()
+    low = lanes((SIDE, SIDE)) < HALF
+    for i in range(SPLIT, N):
+        real, imag = (p_ref[pl.ds(plane(i, 0, part), SIDE), :] for part in range(2))
+        at = (i - SPLIT) * SIDE
+        late_ref[at : at + SIDE, :] = jnp.where(low, real, pltpu.roll(imag, HALF, 1))
     tables.wait()
     ro, rw, do, dw = (table.at[k] for k in range(4))
 
@@ -166,6 +167,10 @@
         return carry
 
     lax.fori_loop(0, N, row_of_patches, 0)
+    total = x_ref[0:SUMS, :]
+    for k in range(1, 8):
+        total = total + x_ref[k * SUMS : (k + 1) * SUMS, :]
+    sum_ref[...] = total
     keep.wait()
 
 
@@ -176,10 +181,7 @@
     tables.start()
     ro, rw, do, dw = (table.at[k] for k in range(4))
     r, c = lax.axis_index("row"), lax.axis_index("col")
-    total = x_ref[0:SUMS, :]
-    for k in range(1, 8):
-        total = total + x_ref[k * SUMS : (k + 1) * SUMS, :]
-    all_ref[...] = total
+    all_ref[...] = x_ref[...]
 
     def put(quantity, i, j, value):
         at = quantity * N * N + i * N + j
@@ -407,23 +409,22 @@
         return pl.CostEstimate(flops=flops, bytes_accessed=moved, transcendentals=0)
 
     near, far = SPLIT * SIDE, (N - SPLIT) * SIDE
-    left, right, late, lower, table = pl.pallas_call(
+    left, right, lower, table = pl.pallas_call(
         strip_kernel,
         out_shape=(
             f32(near, SIDE),
-            f32(far, SIDE),
             f32(far, SIDE),
             f32(*south_shape),
             jax.ShapeDtypeStruct((4, N, N), jnp.int32),
         ),
         in_specs=[hbm] * 5,
-        out_specs=(vmem,) * 5,
+        out_specs=(vmem,) * 4,
         scratch_shapes=[
-            pltpu.VMEM((N, 2, SIDE, SIDE), jnp.float32),
+            pltpu.VMEM((SPLIT, 2, SIDE, SIDE), jnp.float32),
             pltpu.VMEM((N - SPLIT, 2, SIDE, SIDE), jnp.float32),
             pltpu.SMEM((N, N), jnp.int32),
             pltpu.SMEM((N, N), jnp.int32),
-            pltpu.SemaphoreType.DMA((9 + 2 * N,)),
+            pltpu.SemaphoreType.DMA((8 + 2 * N,)),
         ],
         compiler_params=params(8),
         cost_estimate=cost(400_000, 3_000_000),
@@ -434,12 +435,12 @@
     west_edge = lax.ppermute(right, "col", [(k, (k + 1) % n_cols) for k in range(n_cols)])
     south_edge = lax.ppermute(lower, "row", [(k, (k - 1) % n_rows) for k in range(n_rows)])
 
-    sums, keep = pl.pallas_call(
+    sums, keep, late = pl.pallas_call(
         inner_kernel,
-        out_shape=(f32(8 * SUMS, SIDE), f32(KEEP * N * 2 * SIDE, SIDE)),
+        out_shape=(f32(SUMS, SIDE), f32(KEEP * N * 2 * SIDE, SIDE), f32(far, SIDE)),
         in_specs=[vmem] * 2,
-        out_specs=(vmem, vmem),
-        scratch_shapes=[table_scratch, pltpu.SemaphoreType.DMA((2,))],
+        out_specs=(vmem,) * 3,
+        scratch_shapes=[pltpu.VMEM((8 * SUMS, SIDE), jnp.float32), table_scratch, pltpu.SemaphoreType.DMA((2,))],
         compiler_params=params(16),
         cost_estimate=cost(20_000_000, 9_000_000),
         name="inner",

time: 44.3 us -> 44.2 us (level)
  no operation moved by 1% of the time
where the time goes in v7:
time: 44.2 us; the launch traced here: 44.1 us
  blocking collectives  17.1 us (39%)
  Pallas kernels  15.1 us (34%)
  starting transfers between devices  10.4 us (24%)
  waiting for transfers between devices  0.85 us (2%)
  between operations  0.69 us (2%)
    all_to_all x1, blocking collectives, local(): grid = lax.all_to_all(sent, ('row', 'col'), 0, 0, tiled=True)  17.1 us
    pallas_call x1, Pallas kernels, local(): pl.pallas_call(functools.partial(blend_kernel, n_rows, n_cols), out_shape...  6.98 us
    ppermute x1, starting transfers between devices, local(): east_edge = lax.ppermute(left, 'col', to_left)  4.74 us
    pallas_call x1, Pallas kernels, local(): pl.pallas_call(inner_kernel, out_shape=(f32(SUMS, SIDE), f32(KEEP * N * 2...  4.7 us
    ppermute x1, starting transfers between devices, local(): late_edge = lax.ppermute(late_out, 'col', to_left)  2.93 us
    pallas_call x1, Pallas kernels, local(): pl.pallas_call(strip_kernel, out_shape=(f32(near, SIDE), f32(far, SIDE),...  1.84 us
    pallas_call x1, Pallas kernels, local(): pl.pallas_call(functools.partial(rim_kernel, n_rows, n_cols), out_shape=f...  1.55 us
    ppermute x1, starting transfers between devices, local(): lax.ppermute(lower, 'row', [(k, (k - 1) % n_rows) for k in range(n_rows)])  1.43 us
  transfers between devices with their start and end apart: 4, of which 1 were waited for; matrix products, arithmetic and copies ran while one was open for 0% of the time, Pallas kernels for 11%

profile of v7, /device:TPU:1, one launch (start us, length us, event | category | flops | bytes accessed | tf_op | source)
XLA Modules:
  0.0 44.1 jit_solution(17932159621141366306)
XLA Ops:
  0.6 0.0 copy-start
  0.6 1.8 %strips.1 = (f32[384,128]{1,0:T(8,128)S(1)}, f32[640,128]{1,0:T(8,128)S(1)}, f32[1040,128]{1,0:T(8,128)S(1)}, s32[4,8,8]{2,1,0:T(8,128)S(1)}) custom-call(s32[8,8]{1,0:T(8,128)} %ro_hbm.1, s32[8,8]{1,0:T(8,128)} %rw_hbm.1, s32[8,8]{1,0:T(8,128)} %do_hbm.1, s32[8,8]{1,0:T(8,128)} %dw_hbm.1, f32[8,8,2,128,128]{4,3,2,1,0:T(8,128)} %p_hbm.1), custom_call_target="tpu_custom_call" | custom-call | flops 400000 | bytes 3000000 | tf_op jit(solution)/shard_map/strips/pallas_call | solution.py:412
  2.5 0.0 copy-start.1
  2.5 1.4 %collective-permute-start.2 = (f32[1040,128]{1,0:T(8,128)S(1)}, f32[1040,128]{1,0:T(8,128)S(1)}, u32[]{:S(2)}, u32[]{:S(2)}) collective-permute-start(f32[1040,128]{1,0:T(8,128)S(1)} %get-tuple-element.18), channel_id=1, source_target_pairs={{0,112},{16,0},{32,16},{48,32},{64,48},{80,64},{96,80},{112,96},{1... | collective-permute-start | bytes 1597448 | tf_op jit(solution)/shard_map/ppermute | solution.py:436
  3.9 1.3 %collective-permute-start.1 = (f32[640,128]{1,0:T(8,128)S(1)}, f32[640,128]{1,0:T(8,128)S(1)}, u32[]{:S(2)}, u32[]{:S(2)}) collective-permute-start(f32[640,128]{1,0:T(8,128)S(1)} %get-tuple-element.17), channel_id=1, source_target_pairs={{0,1},{1,2},{2,3},{3,4},{4,5},{5,6},{6,7},{7,8},{8,9},{9,10},{10,1... | collective-permute-start | bytes 983048 | tf_op jit(solution)/shard_map/ppermute | solution.py:435
  5.2 4.7 %collective-permute-start = (f32[384,128]{1,0:T(8,128)S(1)}, f32[384,128]{1,0:T(8,128)S(1)}, u32[]{:S(2)}, u32[]{:S(2)}) collective-permute-start(f32[384,128]{1,0:T(8,128)S(1)} %get-tuple-element.16), channel_id=1, source_target_pairs={{0,15},{1,0},{2,1},{3,2},{4,3},{5,4},{6,5},{7,6},{8,7},{9,8},{10,9... | collective-permute-start | bytes 589832 | tf_op jit(solution)/shard_map/ppermute | solution.py:434
  10.0 0.0 copy-done
  10.0 4.7 %inner.1 = (f32[256,128]{1,0:T(8,128)S(1)}, f32[4096,128]{1,0:T(8,128)S(1)}, f32[640,128]{1,0:T(8,128)S(1)}) custom-call(s32[4,8,8]{2,1,0:T(8,128)S(1)} %get-tuple-element.13.table_ref, f32[16384,128]{1,0:T(8,128)S(1)} %bitcast.5), custom_call_target="tpu_custom_call" | custom-call | flops 20000000 | bytes 9000000 | tf_op jit(solution)/shard_map/inner/pallas_call | solution.py:438
  14.7 0.0 collective-permute-done.east_ref.left_ref
  14.7 0.8 %collective-permute-done.1.west_ref = f32[640,128]{1,0:T(8,128)S(1)} collective-permute-done((f32[640,128]{1,0:T(8,128)S(1)}, f32[640,128]{1,0:T(8,128)S(1)}, u32[]{:S(2)}, u32[]{:S(2)}) %collective-permute-start.1) | collective-permute-done | bytes 327712 | tf_op jit(solution)/shard_map/ppermute | solution.py:435
  15.5 0.0 collective-permute-done.2.south_ref
  15.5 1.5 %rim.1 = f32[256,128]{1,0:T(8,128)S(1)} custom-call(s32[4,8,8]{2,1,0:T(8,128)S(1)} %get-tuple-element.13.table_ref, f32[256,128]{1,0:T(8,128)S(1)} %get-tuple-element.15.x_ref, f32[16384,128]{1,0:T(8,128)S(1)} %bitcast.6, f32[384,128]{1,0:T(8,128)S(1)} %collective-permute-done.east_ref.left_ref, f32[640,128]{1,0:T(8,128)S(1)} %collective-permute-done.1.west_ref, ...), custom_call_target="tpu_custom_call" | custom-call | flops 5000000 | bytes 3000000 | tf_op jit(solution)/shard_map/rim/pallas_call | solution.py:449
  17.1 0.0 copy-done.1
  17.1 2.9 %collective-permute-start.3 = (f32[640,128]{1,0:T(8,128)S(1)}, f32[640,128]{1,0:T(8,128)S(1)}, u32[]{:S(2)}, u32[]{:S(2)}) collective-permute-start(f32[640,128]{1,0:T(8,128)S(1)} %get-tuple-element.21.late_ref), channel_id=1, source_target_pairs={{0,15},{1,0},{2,1},{3,2},{4,3},{5,4},{6,5},{7,6},{8,7},{9,8},{10,9... | collective-permute-start | bytes 983048 | tf_op jit(solution)/shard_map/ppermute | solution.py:460
  20.0 17.1 %all_to_all.11 = f32[128,2,128]{2,1,0:T(2,128)S(1)} all-to-all(f32[128,2,128]{2,1,0:T(2,128)S(1)} %bitcast.8), channel_id=1, replica_groups=mesh['row'=8,'col'=16] {'row','col'}, dimensions={0} | all-to-all | bytes 262144 | tf_op jit(solution)/shard_map/all_to_all | solution.py:461
  37.1 0.0 collective-permute-done.3.late_ref
  37.1 7.0 %blend.1 = (f32[16384,128]{1,0:T(8,128)}, f32[2,8,8]{2,1,0:T(8,128)}) custom-call(s32[4,8,8]{2,1,0:T(8,128)} %copy-done.1, f32[256,128]{1,0:T(8,128)S(1)} %bitcast.7, f32[4096,128]{1,0:T(8,128)S(1)} %get-tuple-element.20.keep_ref, f32[16384,128]{1,0:T(8,128)} %bitcast.4, f32[384,128]{1,0:T(8,128)S(1)} %collective-permute-done.east_ref.left_ref, ...), custom_call_target="tpu_custom_call" | custom-call | flops 30000000 | bytes 10000000 | tf_op jit(solution)/shard_map/blend/pallas_call | solution.py:463
Async XLA Ops:
  0.6 9.3 %copy-start = (f32[8,8,2,128,128]{4,3,2,1,0:T(8,128)S(1)}, f32[8,8,2,128,128]{4,3,2,1,0:T(8,128)}, u32[]{:S(2)}) copy-start(f32[8,8,2,128,128]{4,3,2,1,0:T(8,128)} %p_hbm.1) | copy-start | bytes 25165828
  2.5 14.6 %copy-start.1 = (s32[4,8,8]{2,1,0:T(8,128)}, s32[4,8,8]{2,1,0:T(8,128)S(1)}, u32[]{:S(2)}) copy-start(s32[4,8,8]{2,1,0:T(8,128)S(1)} %get-tuple-element.13.table_ref) | copy-start | bytes 3076
  2.5 13.0 %collective-permute-start.2 = (f32[1040,128]{1,0:T(8,128)S(1)}, f32[1040,128]{1,0:T(8,128)S(1)}, u32[]{:S(2)}, u32[]{:S(2)}) collective-permute-start(f32[1040,128]{1,0:T(8,128)S(1)} %get-tuple-element.18), channel_id=1, source_target_pairs={{0,112},{16,0},{32,16},{48,32},{64,48},{80,64},{96,80},{112,96},{1... | collective-permute-start | bytes 1597448 | tf_op jit(solution)/shard_map/ppermute | solution.py:436
  3.9 11.6 %collective-permute-start.1 = (f32[640,128]{1,0:T(8,128)S(1)}, f32[640,128]{1,0:T(8,128)S(1)}, u32[]{:S(2)}, u32[]{:S(2)}) collective-permute-start(f32[640,128]{1,0:T(8,128)S(1)} %get-tuple-element.17), channel_id=1, source_target_pairs={{0,1},{1,2},{2,3},{3,4},{4,5},{5,6},{6,7},{7,8},{8,9},{9,10},{10,1... | collective-permute-start | bytes 983048 | tf_op jit(solution)/shard_map/ppermute | solution.py:435
  5.2 9.5 %collective-permute-start = (f32[384,128]{1,0:T(8,128)S(1)}, f32[384,128]{1,0:T(8,128)S(1)}, u32[]{:S(2)}, u32[]{:S(2)}) collective-permute-start(f32[384,128]{1,0:T(8,128)S(1)} %get-tuple-element.16), channel_id=1, source_target_pairs={{0,15},{1,0},{2,1},{3,2},{4,3},{5,4},{6,5},{7,6},{8,7},{9,8},{10,9... | collective-permute-start | bytes 589832 | tf_op jit(solution)/shard_map/ppermute | solution.py:434
  17.1 20.0 %collective-permute-start.3 = (f32[640,128]{1,0:T(8,128)S(1)}, f32[640,128]{1,0:T(8,128)S(1)}, u32[]{:S(2)}, u32[]{:S(2)}) collective-permute-start(f32[640,128]{1,0:T(8,128)S(1)} %get-tuple-element.21.late_ref), channel_id=1, source_target_pairs={{0,15},{1,0},{2,1},{3,2},{4,3},{5,4},{6,5},{7,6},{8,7},{9,8},{10,9... | collective-permute-start | bytes 983048 | tf_op jit(solution)/shard_map/ppermute | solution.py:460
